TPU v7x, 32 devices: a whole 2x2x4 slice. The times are simulated.
32 devices in a mesh: span: 4 (over x, core), seq: 8 (over z, y).
Axes of the slice: x: 2, y: 2, z: 4, core: 2. Of those that a mesh axis runs over, the one named last changes fastest.
Arguments:
- inputs: bfloat16 [2, 2048, 2560], P(None, ('span', 'seq')), may hold values from -6 to 6
- norm_one: bfloat16 [2560], P(('span', 'seq')), may hold values from 0.25 to 1.75
- rec_proj: bfloat16 [2560, 5120], P(('span', 'seq')), may hold values from -0.125 to 0.125
- conv_weight: bfloat16 [2560, 4], P(('span', 'seq')), may hold values from -3 to 3
- conv_bias: bfloat16 [2560], P(('span', 'seq')), may hold values from -3 to 3
- gate_weight: bfloat16 [2560, 512], P(('span', 'seq')), may hold values from -0.375 to 0.375
- gate_bias: bfloat16 [2560, 2], P(('span', 'seq')), may hold values from -4 to 4
- decay_param: bfloat16 [2560], P(('span', 'seq')), may hold values from -14 to -3.5
- out_proj: bfloat16 [2560, 2560], P(('span', 'seq')), may hold values from -0.5 to 0.5
- norm_two: bfloat16 [2560], P(('span', 'seq')), may hold values from 0.25 to 1.75
- mlp_wide: bfloat16 [2560, 2, 7680], P('span', None, 'seq'), may hold values from -0.125 to 0.125
- mlp_narrow: bfloat16 [2560, 7680], P('span', 'seq'), may hold values from -0.09375 to 0.09375
- cotangent: bfloat16 [2, 2048, 2560], P(None, ('span', 'seq')), may hold values from -6 to 6
Outputs:
- output: bfloat16 [2, 2048, 2560], P(None, ('span', 'seq'))
- input_grad: float32 [2, 2048, 2560], P(None, ('span', 'seq'))
- norm_one_grad: float32 [2560], P(('span', 'seq'))
- rec_proj_grad: float32 [2560, 5120], P(('span', 'seq'))
- conv_weight_grad: float32 [2560, 4], P(('span', 'seq'))
- conv_bias_grad: float32 [2560], P(('span', 'seq'))
- gate_weight_grad: float32 [2560, 512], P(('span', 'seq'))
- gate_bias_grad: float32 [2560, 2], P(('span', 'seq'))
- decay_param_grad: float32 [2560], P(('span', 'seq'))
- out_proj_grad: float32 [2560, 2560], P(('span', 'seq'))
- norm_two_grad: float32 [2560], P(('span', 'seq'))
- mlp_wide_grad: float32 [2560, 2, 7680], P('span', None, 'seq')
- mlp_narrow_grad: float32 [2560, 7680], P('span', 'seq')
All inputs are finite; a program needn't handle non-finite values.
Results may differ from a plain program's by a relative error of at most 0.008.
The roundings to bfloat16 on the way count: a program that leaves them out, or rounds other values in their place, can miss the bound.
Values may be sent and summed in bfloat16 or wider, within the bound.
A program may use at most 384 MiB of HBM per device.

v0:
```python
import jax
import jax.numpy as jnp
from jax import lax
from jax.sharding import PartitionSpec as P

CONV = 4


EPS = 1e-06


def passed_along(block, axis, distance):
    devices = range(lax.axis_size(axis))
    route = [(i - distance, i) for i in devices if i - distance in devices]
    return lax.ppermute(block, axis, route)


def entering(value, axis, join, neutral, backward):
    count, mine = (lax.axis_size(axis), lax.axis_index(axis))
    pieces = jax.tree.map(lambda part: lax.all_gather(part, axis), value)
    if backward:
        pieces = jax.tree.map(lambda part: part[::-1], pieces)
        mine = count - 1 - mine
    subtotal = jax.tree.map(
        lambda part, zero: jnp.full_like(part, 0) + jnp.asarray(zero, part.dtype), value, neutral
    )

    def step(position, subtotal):
        longer = join(subtotal, jax.tree.map(lambda part: part[position], pieces))
        return jax.tree.map(lambda new, old: jnp.where(position < mine, new, old), longer, subtotal)

    return lax.fori_loop(0, count - 1, step, subtotal)


def affine(left, right):
    return (left[0] * right[0], right[0] * left[1] + right[1])


def normed(v, gain):
    return v * lax.rsqrt(jnp.mean(v * v, axis=-1, keepdims=True) + EPS) * gain


def on_device(
    inputs,
    norm_one,
    rec_proj,
    conv_weight,
    conv_bias,
    gate_weight,
    gate_bias,
    decay_param,
    out_proj,
    norm_two,
    mlp_wide,
    mlp_narrow,
    cotangent,
):
    batch, steps, width = inputs.shape
    head_w = gate_weight.shape[1] // 2
    heads = width // head_w
    edge = CONV - 1
    f32 = jnp.float32
    bf16 = jnp.bfloat16
    gathered = (
        lax.all_gather(norm_one, ("span", "seq"), axis=0, tiled=True),
        lax.all_gather(rec_proj, ("span", "seq"), axis=0, tiled=True),
        lax.all_gather(conv_weight, ("span", "seq"), axis=0, tiled=True),
        lax.all_gather(conv_bias, ("span", "seq"), axis=0, tiled=True),
        lax.all_gather(gate_weight, ("span", "seq"), axis=0, tiled=True),
        lax.all_gather(gate_bias, ("span", "seq"), axis=0, tiled=True),
        lax.all_gather(decay_param, ("span", "seq"), axis=0, tiled=True),
        lax.all_gather(out_proj, ("span", "seq"), axis=0, tiled=True),
        lax.all_gather(norm_two, ("span", "seq"), axis=0, tiled=True),
    )
    (
        gain_one,
        proj_full,
        conv_full,
        conv_shift,
        gate_full,
        gate_shift,
        decay_full,
        out_full,
        gain_two,
    ) = gathered
    gain_one = gain_one.astype(f32)
    gain_two = gain_two.astype(f32)
    conv_taps = conv_full.astype(f32)
    conv_offset = conv_shift.astype(f32)
    gate_offset = gate_shift.astype(f32)
    decay_rate = decay_full.astype(f32)
    wide_local, narrow_local = (
        lax.all_gather(mlp_wide, "span", axis=0, tiled=True),
        lax.all_gather(mlp_narrow, "span", axis=0, tiled=True),
    )
    x = inputs.astype(f32)
    normal_one = normed(x, gain_one).astype(bf16)
    projected = jnp.einsum("mtd,de->mte", normal_one, proj_full, preferred_element_type=f32)
    x_branch = projected[..., :width].astype(bf16)
    y_branch, gelu_back = jax.vjp(jax.nn.gelu, projected[..., width:])
    before = passed_along(x_branch[:, steps - edge :, :], ("span", "seq"), 1)
    extended = jnp.concatenate([before, x_branch], axis=1).astype(f32)

    def convolve(ext, taps, offset):
        total = offset + jnp.zeros((batch, steps, width), f32)
        for k in range(CONV):
            total = total + taps[:, k] * ext[:, edge - k : edge - k + steps]
        return total

    conv_out, conv_back = jax.vjp(convolve, extended, conv_taps, conv_offset)
    conv_blocks = conv_out.astype(bf16).reshape(batch, steps, heads, head_w)
    gate_blocks = gate_full.reshape(heads, head_w, 2 * head_w)
    gate_pre = jnp.einsum("mthc,hcd->mthd", conv_blocks, gate_blocks, preferred_element_type=f32)

    def gating(pre, conv_vals, offset, rate):
        recur = jax.nn.sigmoid(pre[..., :head_w].reshape(batch, steps, width) + offset[:, 0])
        inject = jax.nn.sigmoid(pre[..., head_w:].reshape(batch, steps, width) + offset[:, 1])
        log_decay = -8.0 * recur * jax.nn.softplus(rate)
        driven = jnp.sqrt(-jnp.expm1(2.0 * log_decay)) * inject * conv_vals
        return (jnp.exp(log_decay), driven)

    (decay, driven), gate_back = jax.vjp(gating, gate_pre, conv_out, gate_offset, decay_rate)
    decay_cols, driven_cols = (
        lax.all_to_all(decay, "seq", split_axis=2, concat_axis=1, tiled=True),
        lax.all_to_all(driven, "seq", split_axis=2, concat_axis=1, tiled=True),
    )
    prod_cols, state_cols = lax.associative_scan(affine, (decay_cols, driven_cols), axis=1)
    unit = jnp.ones_like(prod_cols[:, -1])
    nothing = jnp.zeros_like(state_cols[:, -1])
    incoming = entering(
        (prod_cols[:, -1], state_cols[:, -1]), "span", affine, (unit, nothing), False
    )[1]
    states_cols = state_cols + prod_cols * incoming[:, None, :]
    states = lax.all_to_all(states_cols, "seq", split_axis=1, concat_axis=2, tiled=True)
    mixed = (states * y_branch).astype(bf16)
    resid = x + jnp.einsum("mtd,de->mte", mixed, out_full, preferred_element_type=f32)
    normal_two = normed(resid, gain_two).astype(bf16)
    group_rows, group_grads = (
        lax.all_gather(normal_two, "seq", axis=1, tiled=True),
        lax.all_gather(cotangent, "seq", axis=1, tiled=True),
    )
    gate_up = jnp.einsum("mtd,dkf->mtkf", group_rows, wide_local, preferred_element_type=f32)

    def activate(values):
        return jax.nn.gelu(values[..., 0, :]) * values[..., 1, :]

    hidden_vals, act_back = jax.vjp(activate, gate_up)
    hidden = hidden_vals.astype(bf16)
    down_part = jnp.einsum("mtf,df->mtd", hidden, narrow_local, preferred_element_type=f32)
    hidden_grad = jnp.einsum("mtd,df->mtf", group_grads, narrow_local, preferred_element_type=f32)
    gate_up_grad = act_back(hidden_grad)[0].astype(bf16)
    normal_part = jnp.einsum("mtkf,dkf->mtd", gate_up_grad, wide_local, preferred_element_type=f32)
    wide_grad = jnp.einsum("mtd,mtkf->dkf", group_rows, gate_up_grad, preferred_element_type=f32)
    narrow_grad = jnp.einsum("mtd,mtf->df", group_grads, hidden, preferred_element_type=f32)
    down_sum, normal_two_grad = (
        lax.psum_scatter(down_part, "seq", scatter_dimension=1, tiled=True),
        lax.psum_scatter(normal_part, "seq", scatter_dimension=1, tiled=True),
    )
    output = (resid + down_sum).astype(bf16)
    norm_back_two = jax.vjp(normed, resid, gain_two)[1]
    resid_part, gain_two_grad = norm_back_two(normal_two_grad)
    resid_grad = cotangent.astype(f32) + resid_part
    branch_grad = resid_grad.astype(bf16)
    mixed_grad = jnp.einsum("mte,de->mtd", branch_grad, out_full, preferred_element_type=f32)
    states_grad = mixed_grad * y_branch
    y_grad = mixed_grad * states
    states_grad_cols = lax.all_to_all(states_grad, "seq", split_axis=2, concat_axis=1, tiled=True)
    following = jnp.concatenate([decay_cols[:, 1:], jnp.ones_like(decay_cols[:, :1])], axis=1)
    carry_cols, local_adjoint = lax.associative_scan(
        affine, (following, states_grad_cols), axis=1, reverse=True
    )
    leading = decay_cols[:, 0]
    arriving = entering(
        (leading * carry_cols[:, 0], leading * local_adjoint[:, 0]),
        "span",
        affine,
        (unit, nothing),
        True,
    )[1]
    adjoint = local_adjoint + carry_cols * arriving[:, None, :]
    earlier = jnp.concatenate([incoming[:, None, :], states_cols[:, :-1]], axis=1)
    decay_grad_cols = adjoint * earlier
    decay_grad, driven_grad = (
        lax.all_to_all(decay_grad_cols, "seq", split_axis=1, concat_axis=2, tiled=True),
        lax.all_to_all(adjoint, "seq", split_axis=1, concat_axis=2, tiled=True),
    )
    pre_grad, conv_direct, gate_bias_grad, decay_param_grad = gate_back((decay_grad, driven_grad))
    pre_low = pre_grad.astype(bf16)
    conv_grad = conv_direct + jnp.einsum(
        "mthd,hcd->mthc", pre_low, gate_blocks, preferred_element_type=f32
    ).reshape(batch, steps, width)
    gate_grad = jnp.einsum(
        "mthc,mthd->hcd", conv_blocks, pre_low, preferred_element_type=f32
    ).reshape(width, 2 * head_w)
    extended_grad, taps_grad, offset_grad = conv_back(conv_grad)
    spill = passed_along(extended_grad[:, :edge].astype(jnp.bfloat16), ("span", "seq"), -1).astype(
        jnp.float32
    )
    branch_x_grad = extended_grad[:, edge:] + jnp.pad(spill, ((0, 0), (steps - edge, 0), (0, 0)))
    projected_grad = jnp.concatenate([branch_x_grad, gelu_back(y_grad)[0]], axis=-1).astype(bf16)
    normal_one_grad = jnp.einsum(
        "mte,de->mtd", projected_grad, proj_full, preferred_element_type=f32
    )
    norm_back_one = jax.vjp(normed, x, gain_one)[1]
    input_part, gain_one_grad = norm_back_one(normal_one_grad)
    input_grad = resid_grad + input_part
    proj_grad = jnp.einsum("mtd,mte->de", normal_one, projected_grad, preferred_element_type=f32)
    out_grad = jnp.einsum("mtd,mte->de", mixed, branch_grad, preferred_element_type=f32)
    owned = (
        lax.psum_scatter(gain_one_grad, ("span", "seq"), scatter_dimension=0, tiled=True),
        lax.psum_scatter(proj_grad, ("span", "seq"), scatter_dimension=0, tiled=True),
        lax.psum_scatter(taps_grad, ("span", "seq"), scatter_dimension=0, tiled=True),
        lax.psum_scatter(offset_grad, ("span", "seq"), scatter_dimension=0, tiled=True),
        lax.psum_scatter(gate_grad, ("span", "seq"), scatter_dimension=0, tiled=True),
        lax.psum_scatter(gate_bias_grad, ("span", "seq"), scatter_dimension=0, tiled=True),
        lax.psum_scatter(decay_param_grad, ("span", "seq"), scatter_dimension=0, tiled=True),
        lax.psum_scatter(out_grad, ("span", "seq"), scatter_dimension=0, tiled=True),
        lax.psum_scatter(gain_two_grad, ("span", "seq"), scatter_dimension=0, tiled=True),
    )
    wide_owned, narrow_owned = (
        lax.psum_scatter(wide_grad, "span", scatter_dimension=0, tiled=True),
        lax.psum_scatter(narrow_grad, "span", scatter_dimension=0, tiled=True),
    )
    return (
        output,
        input_grad,
        owned[0],
        owned[1],
        owned[2],
        owned[3],
        owned[4],
        owned[5],
        owned[6],
        owned[7],
        owned[8],
        wide_owned,
        narrow_owned,
    )


def solution(mesh):
    placed = (
        P(None, ("span", "seq"), None),
        P(("span", "seq")),
        P(("span", "seq"), None),
        P(("span", "seq"), None),
        P(("span", "seq")),
        P(("span", "seq"), None),
        P(("span", "seq"), None),
        P(("span", "seq")),
        P(("span", "seq"), None),
        P(("span", "seq")),
        P("span", None, "seq"),
        P("span", "seq"),
        P(None, ("span", "seq"), None),
    )
    return jax.shard_map(
        on_device,
        mesh=mesh,
        in_specs=placed,
        out_specs=(
            P(None, ("span", "seq"), None),
            P(None, ("span", "seq"), None),
            P(("span", "seq")),
            P(("span", "seq"), None),
            P(("span", "seq"), None),
            P(("span", "seq")),
            P(("span", "seq"), None),
            P(("span", "seq"), None),
            P(("span", "seq")),
            P(("span", "seq"), None),
            P(("span", "seq")),
            P("span", None, "seq"),
            P("span", "seq"),
        ),
        check_vma=False,
    )
```

profile of v0, /device:TPU:8, one launch (start us, length us, event | category | flops | bytes accessed | tf_op | source)
XLA Modules:
  0.0 3889.2 jit_solution(1850112006066936549)
XLA Ops:
  10.5 42.8 %all-reduce.98 = (bf16[2560]{0:T(1024)(128)(2,1)S(1)}, bf16[2560]{0:T(1024)(128)(2,1)S(1)}, bf16[2560]{0:T(1024)(128)(2,1)S(1)}, bf16[2560]{0:T(1024)(128)(2,1)}) all-reduce(bf16[2560]{0:T(1024)(128)(2,1)S(1)} %dynamic-update-slice.2, bf16[2560]{0:T(1024)(128)(2,1)S(1)} %dynamic-update-slice.1, ...), channel_id=1, replica_groups=mesh['span'=4,'seq'=8] {'span','seq'}, use_global_device_ids=true, to_apply=%add.91 | all-reduce | flops 10240 | bytes 40960
  53.4 63.7 %all-gather.4 = bf16[32,80,4]{1,2,0:T(4,128)(2,1)S(1)} all-gather(bf16[1,80,4]{1,2,0:T(4,128)(2,1)S(1)} %bitcast.272), channel_id=1, replica_groups=mesh['span'=4,'seq'=8] {'span','seq'}, dimensions={0}, use_global_device_ids=true | all-gather | bytes 21120 | tf_op jit(solution)/shard_map/all_gather | solution.py:67
  117.2 63.7 %all-gather.5 = bf16[32,80,2]{1,2,0:T(2,128)(2,1)S(1)} all-gather(bf16[1,80,2]{1,2,0:T(2,128)(2,1)S(1)} %bitcast.273), channel_id=1, replica_groups=mesh['span'=4,'seq'=8] {'span','seq'}, dimensions={0}, use_global_device_ids=true | all-gather | bytes 10560 | tf_op jit(solution)/shard_map/all_gather | solution.py:70
  182.0 13.8 fusion.117
  206.6 24.9 all-gather.16.cloned.1.call-done
  261.4 36.6 all-to-all-done
  327.8 39.4 %all-to-all-done.1 = f32[8,1,40960]{2,1,0:T(1,128)S(1)} async-done(((f32[8,1,40960]{2,1,0:T(1,128)}), f32[8,1,40960]{2,1,0:T(1,128)S(1)}, u32[]{:S(2)}, u32[]{:S(2)}) %all-to-all-start.1) | async-done | bytes 1310752 | tf_op jit(solution)/shard_map/all_to_all | solution.py:124
  552.4 35.3 all-to-all-done.2
  606.1 84.1 %all-gather.20.cloned.1.call-done = bf16[2,512,2560]{2,1,0:T(8,128)(2,1)} async-done(((bf16[2,64,2560]{2,1,0:T(8,128)(2,1)}), bf16[2,512,2560]{2,1,0:T(8,128)(2,1)}) %all-gather.20.cloned.1.call-update) | async-done | bytes 5242896 | tf_op jit(solution)/shard_map/all_gather | solution.py:139
  690.2 15.7 fusion.12
  705.9 23.5 all-gather.24.cloned.1.call-done
  729.4 87.4 %all-gather.26.cloned.1.call-done = bf16[2,512,2560]{2,1,0:T(8,128)(2,1)} async-done(((bf16[2,64,2560]{2,1,0:T(8,128)(2,1)}), bf16[2,512,2560]{2,1,0:T(8,128)(2,1)}) %all-gather.26.cloned.1.call-update) | async-done | bytes 5242896 | tf_op jit(solution)/shard_map/all_gather | solution.py:140
  816.8 13.2 multiply_bitcast_fusion
  833.3 16.5 fusion.14
  850.2 10.5 fusion.21
  860.8 164.8 %reduce-scatter.16.cloned.1.call-done = f32[2,64,2560]{2,1,0:T(8,128)} async-done(((f32[2,512,2560]{2,1,0:T(8,128)}), f32[2,64,2560]{2,1,0:T(8,128)}) %reduce-scatter.16.cloned.1.call-update) | async-done | bytes 1310736 | tf_op jit(solution)/shard_map/reduce_scatter | solution.py:157
  1028.5 177.8 %reduce-scatter.14.cloned.1.call-done = f32[2,64,2560]{2,1,0:T(8,128)} async-done(((f32[2,512,2560]{2,1,0:T(8,128)}), f32[2,64,2560]{2,1,0:T(8,128)}) %reduce-scatter.14.cloned.1.call-update) | async-done | bytes 1310736 | tf_op jit(solution)/shard_map/reduce_scatter | solution.py:156
  1209.6 10.8 fusion.65
  1437.6 12.8 rev.14
  1482.0 32.8 all-to-all-done.4
  1525.6 30.0 all-to-all-done.5
  1594.8 18.1 convolution_bitcast_fusion.2
  1614.4 10.7 convolution_bitcast_fusion.1
  1634.9 20.6 convolution_bitcast_fusion
  1656.2 14.7 fusion.36
  1670.9 43.0 %all-reduce.97 = (f32[2560]{0:T(1024)S(1)}, f32[2560]{0:T(1024)S(1)}, f32[2560]{0:T(1024)S(1)}, f32[2560]{0:T(1024)S(1)}) all-reduce(f32[2560]{0:T(1024)S(1)} %get-tuple-element.245, f32[2560]{0:T(1024)S(1)} %reduce_sum.142, f32[2560]{0:T(1024)S(1)} %fusion.85, ...), channel_id=8, replica_groups=mesh['span'=4,'seq'=8] {'span','seq'}, use_global_device_ids=true, to_apply=%region_11.12.clone | all-reduce | flops 10240 | bytes 81920
  1720.5 125.8 %reduce-scatter.28.cloned.1.call-done = f32[80,4]{1,0:T(8,128)} async-done(((f32[2560,4]{1,0:T(8,128)}), f32[80,4]{1,0:T(8,128)}) %reduce-scatter.28.cloned.1.call-update) | async-done | bytes 1296
  1847.7 81.7 %reduce-scatter.26.cloned.1.call-done = f32[640,960]{0,1:T(8,128)} async-done(((f32[2560,960]{0,1:T(8,128)}), f32[640,960]{0,1:T(8,128)}) %reduce-scatter.26.cloned.1.call-update) | async-done | bytes 2457616 | tf_op jit(solution)/shard_map/reduce_scatter | solution.py:222
  1929.4 147.3 %reduce-scatter.20.cloned.1.call-done = f32[80,512]{1,0:T(8,128)} async-done(((f32[2560,512]{1,0:T(8,128)}), f32[80,512]{1,0:T(8,128)}) %reduce-scatter.20.cloned.1.call-update) | async-done | bytes 163856 | tf_op jit(solution)/shard_map/reduce_scatter | solution.py:214
  2076.7 148.4 %reduce-scatter.24.cloned.1.call-done = f32[640,2,960]{0,2,1:T(8,128)} async-done(((f32[2560,2,960]{0,2,1:T(8,128)}), f32[640,2,960]{0,2,1:T(8,128)}) %reduce-scatter.24.cloned.1.call-update) | async-done | bytes 4915216 | tf_op jit(solution)/shard_map/reduce_scatter | solution.py:221
  2225.2 556.3 %reduce-scatter.22.cloned.1.call-done = f32[80,2560]{1,0:T(8,128)} async-done(((f32[2560,2560]{1,0:T(8,128)}), f32[80,2560]{1,0:T(8,128)}) %reduce-scatter.22.cloned.1.call-update) | async-done | bytes 819216 | tf_op jit(solution)/shard_map/reduce_scatter | solution.py:217
  2781.5 1100.9 %reduce-scatter.18.cloned.1.call-done = f32[80,5120]{1,0:T(8,128)} async-done(((f32[2560,5120]{1,0:T(8,128)}), f32[80,5120]{1,0:T(8,128)}) %reduce-scatter.18.cloned.1.call-update) | async-done | bytes 1638416 | tf_op jit(solution)/shard_map/reduce_scatter | solution.py:211
  (753 shorter events, 605.0 us)
Async XLA Ops:
  7.2 46.1 %copy-start.134 = (bf16[80,4]{0,1:T(4,128)(2,1)S(1)}, bf16[80,4]{0,1:T(4,128)(2,1)}, u32[]{:S(2)}) copy-start(bf16[80,4]{0,1:T(4,128)(2,1)} %param.20) | copy-start | bytes 1924
  7.2 109.9 %copy-start.135 = (bf16[80,2]{0,1:T(2,128)(2,1)S(1)}, bf16[80,2]{0,1:T(2,128)(2,1)}, u32[]{:S(2)}) copy-start(bf16[80,2]{0,1:T(2,128)(2,1)} %param.23) | copy-start | bytes 964
  7.2 173.8 %copy-start.2 = (bf16[2,64,2560]{2,1,0:T(8,128)(2,1)S(1)}, bf16[2,64,2560]{2,1,0:T(8,128)(2,1)}, u32[]{:S(2)}) copy-start(bf16[2,64,2560]{2,1,0:T(8,128)(2,1)} %param.17) | copy-start | bytes 1966084
  7.3 174.7 %all-gather.14.cloned.1.call-start = ((), (), s32[]{:S(2)}) async-start(), calls=%async_computation.15 | async-start | bytes 27033600 | tf_op jit(solution)/shard_map/all_gather | solution.py:66
  8.0 223.6 %all-gather.16.cloned.1.call-start = ((), (), s32[]{:S(2)}) async-start(), calls=%async_computation.16 | async-start | bytes 2703360 | tf_op jit(solution)/shard_map/all_gather | solution.py:69
  8.7 587.4 %all-gather.18.cloned.1.call-start = ((), (), s32[]{:S(2)}) async-start(), calls=%async_computation.17 | async-start | bytes 13516800 | tf_op jit(solution)/shard_map/all_gather | solution.py:72
  53.3 142.4 %copy-start.98 = (bf16[2560]{0:T(1024)(128)(2,1)}, bf16[2560]{0:T(1024)(128)(2,1)S(1)}, u32[]{:S(2)}) copy-start(bf16[2560]{0:T(1024)(128)(2,1)S(1)} %get-tuple-element.277) | copy-start | bytes 15364
  53.4 142.4 %copy-start.61 = (f32[2560]{0:T(1024)}, f32[2560]{0:T(1024)S(1)}, u32[]{:S(2)}) copy-start(f32[2560]{0:T(1024)S(1)} %convert_element_type.63) | copy-start | bytes 30724
  182.0 53.6 %copy-start.67 = (f32[2560]{0:T(1024)}, f32[2560]{0:T(1024)S(1)}, u32[]{:S(2)}) copy-start(f32[2560]{0:T(1024)S(1)} %get-tuple-element.383) | copy-start | bytes 30724
  195.8 8.8 collective-permute-start
  248.0 50.0 %all-to-all-start = ((f32[8,1,40960]{2,1,0:T(1,128)}), f32[8,1,40960]{2,1,0:T(1,128)S(1)}, u32[]{:S(2)}, u32[]{:S(2)}) async-start(f32[8,1,40960]{2,1,0:T(1,128)} %reshape.230), calls=%async_computation | async-start | bytes 2621440 | tf_op jit(solution)/shard_map/all_to_all | solution.py:125
  298.0 69.2 %all-to-all-start.1 = ((f32[8,1,40960]{2,1,0:T(1,128)}), f32[8,1,40960]{2,1,0:T(1,128)S(1)}, u32[]{:S(2)}, u32[]{:S(2)}) async-start(f32[8,1,40960]{2,1,0:T(1,128)} %reshape.228), calls=%async_computation.1 | async-start | bytes 2621440 | tf_op jit(solution)/shard_map/all_to_all | solution.py:124
  307.3 298.7 %all-gather.22.cloned.1.call-start = ((), (), s32[]{:S(2)}) async-start(), calls=%async_computation.19 | async-start | bytes 12288000 | tf_op jit(solution)/shard_map/all_gather | solution.py:93
  544.5 43.3 %all-to-all-start.2 = ((f32[2,512,320]{2,0,1:T(2,128)}), f32[2,512,320]{2,0,1:T(2,128)}, u32[]{:S(2)}, u32[]{:S(2)}) async-start(f32[2,512,320]{2,0,1:T(2,128)} %copy.90), calls=%async_computation.2 | async-start | bytes 3145728 | tf_op jit(solution)/shard_map/all_to_all | solution.py:134
  552.4 137.7 %all-gather.20.cloned.1.call-start = ((), (), s32[]{:S(2)}) async-start(), calls=%async_computation.18 | async-start | bytes 5898240 | tf_op jit(solution)/shard_map/all_gather | solution.py:139
  604.7 124.8 %all-gather.24.cloned.1.call-start = ((), (), s32[]{:S(2)}) async-start(), calls=%async_computation.20 | async-start | bytes 6144000 | tf_op jit(solution)/shard_map/all_gather | solution.py:94
  605.2 211.6 %all-gather.26.cloned.1.call-start = ((), (), s32[]{:S(2)}) async-start(), calls=%async_computation.22 | async-start | bytes 5898240 | tf_op jit(solution)/shard_map/all_gather | solution.py:140
  606.0 419.6 %reduce-scatter.16.cloned.1.call-start = ((), (), s32[]{:S(2)}) async-start(), calls=%async_computation.23 | async-start | bytes 11796480 | tf_op jit(solution)/shard_map/reduce_scatter | solution.py:157
  849.8 356.6 %reduce-scatter.14.cloned.1.call-start = ((), (), s32[]{:S(2)}) async-start(), calls=%async_computation.21 | async-start | bytes 11796480 | tf_op jit(solution)/shard_map/reduce_scatter | solution.py:156
  860.8 345.6 %copy-start.50 = (bf16[2,64,2560]{2,1,0:T(8,128)(2,1)S(1)}, bf16[2,64,2560]{2,1,0:T(8,128)(2,1)}, u32[]{:S(2)}) copy-start(bf16[2,64,2560]{2,1,0:T(8,128)(2,1)} %param.29) | copy-start | bytes 1966084
  1227.9 35.5 all-to-all-start.3
  1473.3 41.5 %all-to-all-start.4 = ((f32[2,512,320]{2,0,1:T(2,128)}), f32[2,512,320]{2,0,1:T(2,128)S(1)}, u32[]{:S(2)}, u32[]{:S(2)}) async-start(f32[2,512,320]{2,0,1:T(2,128)} %copy.96), calls=%async_computation.6 | async-start | bytes 3145728 | tf_op jit(solution)/shard_map/all_to_all | solution.py:185
  1514.8 40.8 %all-to-all-start.5 = ((f32[2,512,320]{2,0,1:T(2,128)}), f32[2,512,320]{2,0,1:T(2,128)S(1)}, u32[]{:S(2)}, u32[]{:S(2)}) async-start(f32[2,512,320]{2,0,1:T(2,128)} %copy.100), calls=%async_computation.7 | async-start | bytes 3145728 | tf_op jit(solution)/shard_map/all_to_all | solution.py:184
  1520.9 198.2 %reduce-scatter.30.cloned.1.call-start = ((), (), s32[]{:S(2)}) async-start(), calls=%async_computation.30 | async-start | bytes 1351680
  1577.5 268.7 %reduce-scatter.28.cloned.1.call-start = ((), (), s32[]{:S(2)}) async-start(), calls=%async_computation.29 | async-start | bytes 1351680
  1579.3 350.1 %reduce-scatter.26.cloned.1.call-start = ((), (), s32[]{:S(2)}) async-start(), calls=%async_computation.28 | async-start | bytes 12288000 | tf_op jit(solution)/shard_map/reduce_scatter | solution.py:222
  1589.6 487.1 %reduce-scatter.20.cloned.1.call-start = ((), (), s32[]{:S(2)}) async-start(), calls=%async_computation.25 | async-start | bytes 5406720 | tf_op jit(solution)/shard_map/reduce_scatter | solution.py:214
  1594.7 630.5 %reduce-scatter.24.cloned.1.call-start = ((), (), s32[]{:S(2)}) async-start(), calls=%async_computation.27 | async-start | bytes 24576000 | tf_op jit(solution)/shard_map/reduce_scatter | solution.py:221
  1612.9 1168.6 %reduce-scatter.22.cloned.1.call-start = ((), (), s32[]{:S(2)}) async-start(), calls=%async_computation.26 | async-start | bytes 27033600 | tf_op jit(solution)/shard_map/reduce_scatter | solution.py:217
  1625.1 2257.3 %reduce-scatter.18.cloned.1.call-start = ((), (), s32[]{:S(2)}) async-start(), calls=%async_computation.24 | async-start | bytes 54067200 | tf_op jit(solution)/shard_map/reduce_scatter | solution.py:211
  1627.7 7.0 collective-permute-start.1
  1656.2 60.1 %copy-start.130 = (f32[2,64]{1,0:T(2,128)S(1)}, f32[2,64]{1,0:T(2,128)}, u32[]{:S(2)}) copy-start(f32[2,64]{1,0:T(2,128)} %copy-done.129) | copy-start | bytes 1540
  (135 other events, 890.5 us)
Sparse Core Ops, SparseCore 0:
  11.0 160.5 all-gather.13
  174.5 57.0 all-gather.15
  234.4 136.3 all-gather.17
  372.3 70.0 all-gather.21
  604.8 85.3 all-gather.19
  691.6 37.7 all-gather.23
  731.6 85.1 all-gather.25
  849.9 175.6 reduce-scatter.15
  1029.2 177.1 reduce-scatter.13
  1577.7 133.8 reduce-scatter.29
  1713.9 132.3 reduce-scatter.27
  1849.3 80.0 reduce-scatter.25
  1932.3 144.4 reduce-scatter.19
  2079.8 145.3 reduce-scatter.23
  2228.0 553.4 reduce-scatter.21
  2784.3 1098.0 reduce-scatter.17
where the time goes:
time: 3910 us; the launch traced here: 3890 us
  waiting for transfers between devices  2910 us (74%)
  local copies, waits for them, and re-layouts  385 us (10%)
  blocking collectives  234 us (6%)
  matrix products  169 us (4%)
  other arithmetic  119 us (3%)
  starting transfers between devices  52.7 us (1%)
    reduce_scatter x1, waiting for transfers between devices, on_device(): lax.psum_scatter(proj_grad, ('span', 'seq'), scatter_dimension=0, tiled=T...  1100 us
    reduce_scatter x1, waiting for transfers between devices, on_device(): lax.psum_scatter(out_grad, ('span', 'seq'), scatter_dimension=0, tiled=True)  556 us
    reduce_scatter x1, waiting for transfers between devices, on_device(): lax.psum_scatter(down_part, 'seq', scatter_dimension=1, tiled=True)  178 us
    reduce_scatter x1, waiting for transfers between devices, on_device(): lax.psum_scatter(normal_part, 'seq', scatter_dimension=1, tiled=True)  165 us
    reduce_scatter x1, waiting for transfers between devices, on_device(): lax.psum_scatter(wide_grad, 'span', scatter_dimension=0, tiled=True)  148 us
    reduce_scatter x1, waiting for transfers between devices, on_device(): lax.psum_scatter(gate_grad, ('span', 'seq'), scatter_dimension=0, tiled=T...  147 us
    unnamed x18, waiting for transfers between devices  130 us
    slice x65, local copies, waits for them, and re-layouts, on_device(): lax.associative_scan(affine, (following, states_grad_cols), axis=1, rever...  126 us
  transfers between devices with their start and end apart: 24, of which 20 were waited for; matrix products, arithmetic and copies ran while one was open for 10% of the time, Pallas kernels for 0%

commit v1 on v0

v1 whole, which is shorter than its diff:
```python
import functools

import jax
import jax.numpy as jnp
from jax import lax
from jax.experimental import pallas as pl
from jax.experimental.pallas import tpu as pltpu
from jax.sharding import PartitionSpec as P

CONV = 4
EPS = 1e-06
AXES = ("span", "seq")
F32 = jnp.float32
BF16 = jnp.bfloat16
SUBS = 8


def swap(value, mask):
    count = lax.axis_size("span") * lax.axis_size("seq")
    return lax.ppermute(value, AXES, [(i, i ^ mask) for i in range(count)])


def dot(a, b, dims, out=F32):
    return lax.dot_general(a, b, ((dims[0], dims[1]), ((), ())), preferred_element_type=F32).astype(out)


def nn(a, b, out=F32):
    return dot(a, b, ((1,), (0,)), out)


def nt(a, b, out=F32):
    return dot(a, b, ((1,), (1,)), out)


def tn(a, b, out=F32):
    return dot(a, b, ((0,), (0,)), out)


def normed(v, gain):
    return v * lax.rsqrt(jnp.mean(v * v, axis=-1, keepdims=True) + EPS) * gain


def norm_back(v, gain, grad):
    scale = lax.rsqrt(jnp.mean(v * v, axis=-1, keepdims=True) + EPS)
    z = v * scale
    e = grad * gain
    return scale * (e - z * jnp.mean(e * z, axis=-1, keepdims=True)), jnp.sum(grad * z, axis=0)


def one_less_exp(u):
    series = 1.0 + u / 7.0
    for n in (6.0, 5.0, 4.0, 3.0, 2.0):
        series = 1.0 + u / n * series
    return jnp.where(u > -0.25, -u * series, 1.0 - jnp.exp(u))


def roll(v, by):
    return pltpu.roll(v, by % SUBS, 0)


def quarter_of(shape, quarters):
    return lax.broadcasted_iota(jnp.int32, shape, 0) % quarters


def spread(v, quarters, at):
    q = quarter_of(v.shape, quarters)
    held = jnp.where(q == at, v, 0.0)
    total = held
    for k in range(1, quarters):
        total = total + roll(held, k if at == 0 else -k)
    return total


def scan_carries(prods, sums, quarters, backward):
    q = quarter_of(prods[0].shape, quarters)
    sign = -1 if backward else 1
    order = (1, 0) if backward else (0, 1)
    place = quarters - 1 - q if backward else q
    whole = None
    enter = [None, None]
    for b in order:
        p, s = prods[b], sums[b]
        d = 1
        while d < quarters:
            pp, ss = roll(p, sign * d), roll(s, sign * d)
            ok = place >= d
            s = jnp.where(ok, p * ss + s, s)
            p = jnp.where(ok, p * pp, p)
            d *= 2
        first = place == 0
        ep = jnp.where(first, 1.0, roll(p, sign))
        es = jnp.where(first, 0.0, roll(s, sign))
        last = 0 if backward else quarters - 1
        tp, ts = spread(p, quarters, last), spread(s, quarters, last)
        if whole is None:
            enter[b] = (ep, es)
            whole = (tp, ts)
        else:
            enter[b] = (ep * whole[0], ep * whole[1] + es)
            whole = (tp * whole[0], tp * whole[1] + ts)
    return enter, whole


def earlier_rows(groups, halo, quarters, steps):
    q = quarter_of(groups[0].shape[1:], quarters)
    edge = CONV - 1
    out = []
    for b in (0, 1):
        ahead = []
        for k in range(edge, 0, -1):
            same = roll(groups[b][steps - k], 1)
            before = halo[k - 1] if b == 0 else roll(groups[0][steps - k], 1 - quarters)
            ahead.append(jnp.where(q == 0, before, same)[None])
        out.append(jnp.concatenate([*ahead, groups[b]], axis=0))
    return out


def forward_kernel(steps, quarters, xb, chan, gate, conv_o, recur_o, inject_o, decay_o, local_o, prod_o, enter_o, carry_o):
    rows = 2 * steps * SUBS
    width = xb.shape[1]
    head = xb[...].astype(F32)
    groups = [head[b * steps * SUBS : (b + 1) * steps * SUBS].reshape(steps, SUBS, width) for b in (0, 1)]
    halo = [head[rows + k * SUBS : rows + (k + 1) * SUBS] for k in range(CONV - 1)]
    edge = CONV - 1
    convs = []
    for ext in earlier_rows(groups, halo, quarters, steps):
        total = jnp.broadcast_to(chan[4:5][None], (steps, SUBS, width))
        for k in range(CONV):
            total = total + chan[k : k + 1][None] * ext[edge - k : edge - k + steps]
        convs.append(total.reshape(steps * SUBS, width))
    conv = jnp.concatenate(convs, axis=0)
    pre = jnp.dot(conv.astype(BF16), gate[...], preferred_element_type=F32)
    recur = jax.nn.sigmoid(pre[:, :width] + chan[5:6])
    inject = jax.nn.sigmoid(pre[:, width:] + chan[6:7])
    log_decay = -8.0 * recur * chan[7:8]
    decay = jnp.exp(log_decay)
    driven = jnp.sqrt(one_less_exp(2.0 * log_decay)) * inject * conv
    conv_o[...] = conv
    recur_o[...] = recur
    inject_o[...] = inject
    decay_o[...] = decay
    prods, sums = [], []
    for b in (0, 1):
        h = p = None
        for t in range(steps):
            at = (b * steps + t) * SUBS
            d, u = decay[at : at + SUBS], driven[at : at + SUBS]
            h = u if h is None else d * h + u
            p = d if p is None else d * p
            local_o[at : at + SUBS] = h
            prod_o[at : at + SUBS] = p
        prods.append(p)
        sums.append(h)
    enter, whole = scan_carries(prods, sums, quarters, False)
    for b in (0, 1):
        enter_o[b * SUBS : (b + 1) * SUBS] = enter[b][0]
        enter_o[(2 + b) * SUBS : (3 + b) * SUBS] = enter[b][1]
    q = quarter_of(whole[0].shape, quarters)
    carry_o[...] = jnp.where(q == 0, whole[0], whole[1])


def adjoint_kernel(steps, quarters, grad, decay, prod, local_o, after_o, enter_o, carry_o):
    prods, sums = [], []
    for b in (0, 1):
        g = r = None
        for t in range(steps - 1, -1, -1):
            at = (b * steps + t) * SUBS
            rows = slice(at, at + SUBS)
            a = grad[rows] if g is None else grad[rows] + g
            r = jnp.ones_like(a) if r is None else r * decay[at + SUBS : at + 2 * SUBS]
            local_o[rows] = a
            after_o[rows] = r
            g = decay[rows] * a
        last = ((b + 1) * steps - 1) * SUBS
        prods.append(prod[last : last + SUBS])
        sums.append(g)
    enter, whole = scan_carries(prods, sums, quarters, True)
    for b in (0, 1):
        enter_o[b * SUBS : (b + 1) * SUBS] = enter[b][0]
        enter_o[(2 + b) * SUBS : (3 + b) * SUBS] = enter[b][1]
    carry_o[...] = whole[1]


def backward_kernel(
    steps, quarters, local, after, states, came, entered, conv_r, recur_r, inject_r, decay_r, xb, chan, gate,
    dx_o, spill_o, gate_o, small_o,
):
    rows = 2 * steps * SUBS
    width = xb.shape[1]
    edge = CONV - 1
    block = steps * SUBS

    def by_step(v):
        return [v[b * block : (b + 1) * block].reshape(steps, SUBS, width) for b in (0, 1)]

    adjoint = jnp.concatenate(
        [
            (l + a * came[b * SUBS : (b + 1) * SUBS][None]).reshape(block, width)
            for b, (l, a) in enumerate(zip(by_step(local[...]), by_step(after[...])))
        ],
        axis=0,
    )
    earlier = jnp.concatenate(
        [
            jnp.concatenate([entered[b * SUBS : (b + 1) * SUBS], states[b * block : (b + 1) * block - SUBS]], axis=0)
            for b in (0, 1)
        ],
        axis=0,
    )
    conv, recur, inject, decay = conv_r[...], recur_r[...], inject_r[...], decay_r[...]
    rate = chan[7:8]
    mult = jnp.sqrt(one_less_exp(-16.0 * recur * rate))
    d_decay = adjoint * earlier
    d_log = d_decay * decay - adjoint * inject * conv * (decay * decay / mult)
    d_inject = adjoint * mult * conv
    d_conv = adjoint * mult * inject
    d_rate = jnp.sum(d_log * (-8.0 * recur), axis=0, keepdims=True)
    d_recur = d_log * (-8.0 * rate) * recur * (1.0 - recur)
    d_inject = d_inject * inject * (1.0 - inject)
    low = jnp.concatenate([d_recur.astype(BF16), d_inject.astype(BF16)], axis=1)
    d_conv = d_conv + lax.dot_general(low, gate[...], (((1,), (1,)), ((), ())), preferred_element_type=F32)
    gate_o[...] = lax.dot_general(conv.astype(BF16), low, (((0,), (0,)), ((), ())), preferred_element_type=F32)
    head = xb[...].astype(F32)
    halo = [head[rows + k * SUBS : rows + (k + 1) * SUBS] for k in range(edge)]
    exts = earlier_rows(by_step(head), halo, quarters, steps)
    groups = by_step(d_conv)
    for k in range(CONV):
        taps = sum(
            jnp.sum(groups[b] * exts[b][edge - k : edge - k + steps], axis=(0, 1), keepdims=True)[0] for b in (0, 1)
        )
        small_o[k : k + 1] = taps
    small_o[4:5] = jnp.sum(d_conv, axis=0, keepdims=True)
    small_o[5:6] = jnp.sum(d_recur, axis=0, keepdims=True)
    small_o[6:7] = jnp.sum(d_inject, axis=0, keepdims=True)
    small_o[7:8] = d_rate
    q = quarter_of((SUBS, width), quarters)
    for b in (0, 1):
        beyond = []
        for j in range(edge):
            same = roll(groups[b][j], -1)
            later = roll(groups[1][j], quarters - 1) if b == 0 else jnp.zeros_like(same)
            beyond.append(jnp.where(q == quarters - 1, later, same)[None])
        ext = jnp.concatenate([groups[b], *beyond], axis=0)
        total = chan[0:1][None] * ext[:steps]
        for k in range(1, CONV):
            total = total + chan[k : k + 1][None] * ext[k : k + steps]
        dx_o[b * block : (b + 1) * block] = total.reshape(block, width)
    for j in range(1, CONV):
        total = jnp.zeros((SUBS, width), F32)
        for k in range(j, CONV):
            total = total + chan[k : k + 1] * groups[0][k - j]
        spill_o[(j - 1) * SUBS : j * SUBS] = total


def by_heads(kernel, heads, head_w, arrays, outs):
    def spec(shape, tall):
        if tall:
            return pl.BlockSpec((head_w, shape[1]), lambda h: (h, 0))
        return pl.BlockSpec((shape[0], head_w), lambda h: (0, h))

    return pl.pallas_call(
        kernel,
        grid=(heads,),
        in_specs=[spec(a.shape, tall) for a, tall in arrays],
        out_specs=[spec(s, tall) for s, tall in outs],
        out_shape=[jax.ShapeDtypeStruct(s, F32) for s, _ in outs],
        compiler_params=pltpu.CompilerParams(vmem_limit_bytes=48 * 1024 * 1024),
    )(*[a for a, _ in arrays])


def on_device(
    inputs, norm_one, rec_proj, conv_weight, conv_bias, gate_weight, gate_bias, decay_param, out_proj, norm_two,
    mlp_wide, mlp_narrow, cotangent,
):
    spans, seqs = lax.axis_size("span"), lax.axis_size("seq")
    count = spans * seqs
    span, seq = lax.axis_index("span"), lax.axis_index("seq")
    me = span * seqs + seq
    side = me % 2
    pair = me // 2
    pairs = count // 2
    batch, tokens, width = inputs.shape
    half = width // 2
    quarters = SUBS // batch
    steps = tokens // quarters
    own = batch * tokens
    rows = 2 * own
    head_w = gate_weight.shape[1] // 2
    heads = half // head_w
    edge = CONV - 1
    share = width // count
    units = mlp_narrow.shape[1]
    inner = [2 * k for k in range(1, seqs // 2)]
    core = seqs
    xs = [2 * seqs * k for k in range(1, spans // 2)]
    top = count // 2
    upper = me // top

    def to_rows(v):
        return v.reshape(batch, quarters, steps, width).transpose(2, 0, 1, 3).reshape(own, width)

    def from_rows(v):
        return v.reshape(steps, batch, quarters, width).transpose(1, 2, 0, 3).reshape(batch, tokens, width)

    def in_order(mine, other, axis):
        return jnp.concatenate([jnp.where(side == 0, mine, other), jnp.where(side == 0, other, mine)], axis=axis)

    def cut(v, index, size, axis):
        return lax.dynamic_slice_in_dim(v, index * size, size, axis)

    small = jnp.concatenate(
        [norm_one[:, None], norm_two[:, None], conv_weight, conv_bias[:, None], gate_bias, decay_param[:, None]], axis=1
    )
    small = lax.all_gather(small, AXES, axis=0, tiled=True).astype(F32).T
    gain_one, gain_two = small[0], small[1]
    rate_pre = cut(small[9:10], side, half, 1)
    chan = cut(jnp.concatenate([small[2:9], jax.nn.softplus(small[9:10])], axis=0), side, half, 1)

    def gathered_rows(block, buffer, place):
        pieces = {0: block}
        for m in inner:
            pieces[m] = swap(block, m)
        for m in xs:
            for n in (0, *inner):
                pieces[m ^ n] = swap(pieces[n], m)
        for n in list(pieces):
            pieces[core ^ n] = swap(pieces[n], core)
        for m, piece in pieces.items():
            buffer = lax.dynamic_update_slice_in_dim(buffer, piece, place(me ^ m), 0)
        return buffer

    def columns_half(block):
        mine, theirs = cut(block, side, half, 1), cut(block, 1 - side, half, 1)
        block = in_order(mine, swap(theirs, 1), 0)
        return gathered_rows(block, jnp.zeros((width, half), BF16), lambda d: d // 2 * 2 * share)

    def rows_half(block):
        full = lax.all_gather(block, AXES, axis=0, tiled=True)
        return cut(full, side, half, 0)

    proj_x = columns_half(rec_proj[:, :width])
    proj_y = columns_half(rec_proj[:, width:])
    gates = rows_half(gate_weight)
    out_half = rows_half(out_proj)

    mine = to_rows(inputs)
    x = mine.astype(F32)
    tail = inputs[:, tokens - edge :]
    halo = lax.ppermute(tail, AXES, [(i, i + 1) for i in range(1, count - 1, 2)]) + lax.ppermute(
        tail, AXES, [(i, i + 2) for i in range(1, count - 2, 2)]
    )
    halo = jnp.zeros((edge, batch, quarters, width), BF16).at[:, :, 0].set(halo[:, ::-1].transpose(1, 0, 2))
    both = in_order(mine, swap(mine, 1), 0)
    lead = jnp.concatenate([both, halo.reshape(edge * SUBS, width), jnp.zeros((8, width), BF16)], axis=0)
    normal_one = normed(lead.astype(F32), gain_one).astype(BF16)
    x_branch = nn(normal_one, proj_x, BF16)
    normal_one = normal_one[:rows]
    y_pre = nn(normal_one, proj_y)
    y_branch, gelu_back = jax.vjp(jax.nn.gelu, y_pre)

    kernel = functools.partial(forward_kernel, steps, quarters)
    full = ((rows, half), False)
    ends = ((4 * SUBS, half), False)
    conv, recur, inject, decay, local, prod, enter, carry = by_heads(
        kernel, heads, head_w, [(x_branch, False), (chan, False), (gates, True)],
        [full] * 6 + [ends, ((SUBS, half), False)],
    )

    def exchanged(carry):
        every = lax.all_gather(carry, AXES, axis=0).reshape(pairs, 2, *carry.shape)
        return lax.dynamic_index_in_dim(every, side, 1, keepdims=False)

    carries = exchanged(carry).reshape(pairs, batch, quarters, half)
    totals = carries[:, :, 0]
    h = jnp.zeros((batch, half), F32)
    for j in range(pairs - 1):
        h = jnp.where(j < pair, totals[j] * h + carries[j, :, 1], h)

    def at_subs(v):
        return jnp.repeat(v, quarters, axis=0)

    def entering(enter, h):
        enter = enter.reshape(2, 2, SUBS, half)
        return enter[0] * at_subs(h)[None] + enter[1]

    def by_steps(v):
        return v.reshape(2, steps, SUBS, half)

    entered = entering(enter, h)
    states = (by_steps(local) + by_steps(prod) * entered[:, None]).reshape(rows, half)
    mixed = (states * y_branch).astype(BF16)

    def over_sides(partial):
        partial = partial.reshape(2, own, width)
        other = lax.dynamic_index_in_dim(partial, 1 - side, 0, keepdims=False).astype(BF16)
        return lax.dynamic_index_in_dim(partial, side, 0, keepdims=False) + swap(other, 1).astype(F32)

    resid = x + over_sides(nn(mixed, out_half))

    def by_span(v):
        size = width // spans
        return jnp.concatenate([cut(v, span ^ j, size, 1) for j in range(spans)], axis=1)

    def span_gather(block):
        pieces = {0: block}
        for m in xs:
            pieces[m] = swap(block, m)
        for n in list(pieces):
            pieces[n ^ core] = swap(pieces[n], core)
        return jnp.concatenate([pieces[m * seqs] for m in range(spans)], axis=1)

    wide = span_gather(mlp_wide.transpose(1, 2, 0).reshape(2 * units, width // spans))
    narrow = span_gather(mlp_narrow.T)

    def token_gather(v):
        blocks = [v] + [swap(v, m) for m in inner]
        others = [swap(b, 1) for b in blocks]
        return jnp.concatenate(blocks, axis=0), jnp.concatenate(others, axis=0)

    c = to_rows(cotangent)
    grads = token_gather(by_span(c))
    c = c.astype(F32)
    normal_two = token_gather(by_span(normed(resid, gain_two).astype(BF16)))

    def activate(values):
        return jax.nn.gelu(values[:, :units]) * values[:, units:]

    hidden, wide_back = [], []
    for part in (0, 1):
        value, back = jax.vjp(activate, nt(normal_two[part], wide))
        hidden.append(value.astype(BF16))
        wide_back.append(back(nt(grads[part], narrow))[0].astype(BF16))

    def token_scatter(far, near):
        near = near.reshape(len(inner) + 1, own, width)
        far = far.reshape(len(inner) + 1, own, width)
        blocks = [near[k] + swap(far[k], 1).astype(F32) for k in range(len(inner) + 1)]
        total = blocks[0]
        for k, m in enumerate(inner):
            total = total + swap(blocks[k + 1].astype(BF16), m).astype(F32)
        return by_span(total)

    normal_two_grad = token_scatter(nn(wide_back[1], wide, BF16), nn(wide_back[0], wide))
    down = token_scatter(nn(hidden[1], narrow, BF16), nn(hidden[0], narrow))
    output = from_rows((resid + down).astype(BF16))

    def span_scatter(left, right):
        size = width // spans
        kept = [j for j in range(spans) if j % 2 == 0]
        given = [j for j in range(spans) if j % 2 == 1]

        def columns(js):
            return jnp.concatenate([right[:, j * size : (j + 1) * size] for j in js], axis=1)

        recv = swap(tn(left, columns(given), BF16), core)
        total = tn(left, columns(kept)) + recv.astype(F32)
        out = total[:, :size]
        for k, m in enumerate(xs):
            out = out + swap(total[:, (k + 1) * size : (k + 2) * size].astype(BF16), m).astype(F32)
        return out

    all_normal = jnp.concatenate(normal_two, axis=0)
    all_grads = jnp.concatenate(grads, axis=0)
    wide_owned = span_scatter(jnp.concatenate(wide_back, axis=0), all_normal)
    wide_owned = wide_owned.reshape(2, units, width // spans).transpose(2, 0, 1)
    narrow_owned = span_scatter(jnp.concatenate(hidden, axis=0), all_grads).T

    resid_part, gain_two_grad = norm_back(resid, gain_two, normal_two_grad)
    resid_grad = c + resid_part
    branch_low = resid_grad.astype(BF16)
    branch_low = in_order(branch_low, swap(branch_low, 1), 0)
    mixed_grad = nt(branch_low, out_half)
    states_grad = mixed_grad * y_branch
    y_grad = gelu_back(mixed_grad * states)[0].astype(BF16)

    kernel = functools.partial(adjoint_kernel, steps, quarters)
    local_adj, after, back_enter, back_carry = by_heads(
        kernel, heads, head_w, [(states_grad, False), (decay, False), (prod, False)],
        [full, full, ends, ((SUBS, half), False)],
    )
    back_carries = exchanged(back_carry).reshape(pairs, batch, quarters, half)[:, :, 0]
    h = jnp.zeros((batch, half), F32)
    for j in range(pairs - 1, 0, -1):
        h = jnp.where(j > pair, totals[j] * h + back_carries[j], h)
    came = entering(back_enter, h)
    kernel = functools.partial(backward_kernel, steps, quarters)
    flat = (2 * SUBS, half)
    dx, spill, gate_grad, small_grad = by_heads(
        kernel, heads, head_w,
        [
            (local_adj, False), (after, False), (states, False), (came.reshape(flat), False),
            (entered.reshape(flat), False), (conv, False), (recur, False), (inject, False), (decay, False),
            (x_branch, False), (chan, False), (gates, True),
        ],
        [full, ((edge * SUBS, half), False), ((half, 2 * head_w), True), ((SUBS, half), False)],
    )
    spill = lax.ppermute(
        spill.reshape(edge, batch, quarters, half)[::-1, :, 0], AXES, [(i, i - 2) for i in range(2, count)]
    )
    spill = jnp.pad(
        spill[:, :, None], ((0, 0), (0, 0), (quarters - 1, 0), (0, 0))
    ).reshape(edge * SUBS, half)
    x_grad = jnp.concatenate([dx[: rows - edge * SUBS], dx[rows - edge * SUBS :] + spill], axis=0).astype(BF16)

    normal_one_grad = over_sides(nt(y_grad, proj_y) + nt(x_grad, proj_x))
    input_part, gain_one_grad = norm_back(x, gain_one, normal_one_grad)
    input_grad = from_rows(resid_grad + input_part)

    def blocks_of(v, masks, wrap):
        size = 2 * share
        return [lax.dynamic_slice_in_dim(v, (me ^ m) // 2 % wrap * size, size, 0) for m in masks]

    def to_columns_owner(v_kept, v_given):
        recv = swap(v_given, core)
        n = len(inner) + 1
        total = (v_kept + recv.astype(F32)).reshape(len(xs) + 1, n, 2 * share, v_kept.shape[1])
        near = total[0]
        for k, m in enumerate(xs):
            near = near + swap(total[k + 1].astype(BF16), m).astype(F32)
        out = near[0]
        for k, m in enumerate(inner):
            out = out + swap(near[k + 1].astype(BF16), m).astype(F32)
        out = out.reshape(2, share, out.shape[1])
        other = lax.dynamic_index_in_dim(out, 1 - side, 0, keepdims=False).astype(BF16)
        return lax.dynamic_index_in_dim(out, side, 0, keepdims=False), swap(other, 1).astype(F32)

    order = [m ^ n for m in (0, *xs) for n in (0, *inner)]
    turned = normal_one.T
    kept = jnp.concatenate(blocks_of(turned, order, pairs), axis=0)
    given = jnp.concatenate(blocks_of(turned, [m ^ core for m in order], pairs), axis=0)
    proj_owned = jnp.concatenate(
        [in_order(*to_columns_owner(nn(kept, g), nn(given, g, BF16)), 1) for g in (x_grad, y_grad)], axis=1
    )

    def to_rows_owner(v_kept, v_given):
        cols = v_kept.shape[1]
        total = (v_kept + swap(v_given, core).astype(F32)).reshape(len(low_order), 2 * share, cols)
        away = cut(total, 1 - upper, cols // 2, 2).astype(BF16)
        near = cut(total, upper, cols // 2, 2) + swap(away, top).astype(F32)
        out = near[0]
        for k, m in enumerate(low_order[1:]):
            out = out + swap(near[k + 1].astype(BF16), m).astype(F32)
        other = swap(out.astype(BF16), top).astype(F32)
        out = in_order(out, other, 1).reshape(2, share, cols)
        gone = lax.dynamic_index_in_dim(out, 1 - side, 0, keepdims=False).astype(BF16)
        here = lax.dynamic_index_in_dim(out, side, 0, keepdims=False)
        return jnp.where(upper == side, here, swap(gone, 1).astype(F32))

    low_order = [m ^ n for m in (0, *[v for v in xs if v < top]) for n in (0, *inner)]
    turned = mixed.T
    kept = jnp.concatenate(blocks_of(turned, low_order, pairs // 2), axis=0)
    given = jnp.concatenate(blocks_of(turned, [m ^ core for m in low_order], pairs // 2), axis=0)
    out_owned = to_rows_owner(nn(kept, branch_low), nn(given, branch_low, BF16))
    by_row = jnp.concatenate([gate_grad, small_grad.T, jnp.zeros((half, head_w - SUBS), F32)], axis=1)
    kept = jnp.concatenate(blocks_of(by_row, low_order, pairs // 2), axis=0)
    given = jnp.concatenate(blocks_of(by_row, [m ^ core for m in low_order], pairs // 2), axis=0).astype(BF16)
    rest = to_rows_owner(kept, given)
    gate_owned, small_owned = rest[:, : 2 * head_w], rest[:, 2 * head_w : 2 * head_w + SUBS]

    gains = jnp.pad(jnp.stack([gain_one_grad, gain_two_grad], axis=1), ((0, 0), (0, 126)))
    kept = jnp.concatenate(blocks_of(gains, order, pairs), axis=0)
    given = jnp.concatenate(blocks_of(gains, [m ^ core for m in order], pairs), axis=0)
    gains = sum(to_columns_owner(kept, given))

    return (
        output,
        input_grad,
        gains[:, 0],
        proj_owned,
        small_owned[:, :CONV],
        small_owned[:, 4],
        gate_owned,
        small_owned[:, 5:7],
        small_owned[:, 7] * jax.nn.sigmoid(decay_param.astype(F32)),
        out_owned,
        gains[:, 1],
        wide_owned,
        narrow_owned,
    )


def solution(mesh):
    both = ("span", "seq")
    tokens = P(None, both, None)
    placed = (
        tokens, P(both), P(both, None), P(both, None), P(both), P(both, None), P(both, None), P(both), P(both, None),
        P(both), P("span", None, "seq"), P("span", "seq"), tokens,
    )
    given = (
        tokens, tokens, P(both), P(both, None), P(both, None), P(both), P(both, None), P(both, None), P(both),
        P(both, None), P(both), P("span", None, "seq"), P("span", "seq"),
    )
    return jax.shard_map(on_device, mesh=mesh, in_specs=placed, out_specs=given, check_vma=False)
```

time: 3910 us -> 1270 us (0.32)
  waiting for transfers between devices: 2910 us -> 709 us
  local copies, waits for them, and re-layouts: 385 us -> 140 us
  blocking collectives: 234 us -> 66.1 us
  other arithmetic: 119 us -> 47.7 us
  starting transfers between devices: 52.7 us -> 112 us
    reduce_scatter x7 -> x0, waiting for transfers between devices: 2380 us -> none  [the longest x1 1100 us: on_device(): lax.psum_scatter(proj_grad, ('span', 'seq'), scatter_dimension=0, tiled=T...]
    ppermute x2 -> x109, waiting for transfers between devices: 5.99 us -> 694 us  [the longest x106 672 us: swap(): return lax.ppermute(value, AXES, [(i, i ^ mask) for i in range(count)])]
    all_gather x7 -> x4, waiting for transfers between devices: 220 us -> 14.6 us  [the longest x2 14.5 us: exchanged(): every = lax.all_gather(carry, AXES, axis=0).reshape(pairs, 2, *carry.shape)]
    slice x131 -> x28, local copies, waits for them, and re-layouts: 212 us -> 17.8 us  [the longest x2 4.87 us: columns(): right[:, j * size:(j + 1) * size]]
    all_to_all x6 -> x0, waiting for transfers between devices: 179 us -> none  [the longest x1 39.4 us: on_device(): lax.all_to_all(decay, 'seq', split_axis=2, concat_axis=1, tiled=True)]
    unnamed x18 -> x4, waiting for transfers between devices: 130 us -> 1.39 us
    ppermute x2 -> x109, starting transfers between devices: 9.64 us -> 111 us  [the longest x106 106 us: swap(): return lax.ppermute(value, AXES, [(i, i ^ mask) for i in range(count)])]
    unnamed x2 -> x0, blocking collectives: 85.9 us -> none
  transfers between devices with their start and end apart: 24 -> 113, of which waited for: 20 -> 48; matrix products, arithmetic and copies ran while one was open for 10% -> 23% of each run, Pallas kernels for 0% -> 1%
where the time goes in v1:
time: 1270 us; the launch traced here: 1260 us
  waiting for transfers between devices  709 us (56%)
  matrix products  147 us (12%)
  local copies, waits for them, and re-layouts  140 us (11%)
  starting transfers between devices  112 us (9%)
  blocking collectives  66.1 us (5%)
  other arithmetic  47.7 us (4%)
  Pallas kernels  18.1 us (1%)
  between operations  17.3 us (1%)
    ppermute x106, waiting for transfers between devices, swap(): return lax.ppermute(value, AXES, [(i, i ^ mask) for i in range(count)])  672 us
    dot_general x24, matrix products, dot(): lax.dot_general(a, b, ((dims[0], dims[1]), ((), ())), preferred_element_t...  147 us
    ppermute x106, starting transfers between devices, swap(): return lax.ppermute(value, AXES, [(i, i ^ mask) for i in range(count)])  106 us
    all_gather x1, blocking collectives, on_device(): small = lax.all_gather(small, AXES, axis=0, tiled=True).astype(F32).T  66.1 us
    unnamed x329, local copies, waits for them, and re-layouts  41.2 us
    dynamic_update_slice x30, local copies, waits for them, and re-layouts, gathered_rows(): buffer = lax.dynamic_update_slice_in_dim(buffer, piece, place(me ^ m), 0)  31.7 us
  transfers between devices with their start and end apart: 113, of which 48 were waited for; matrix products, arithmetic and copies ran while one was open for 23% of the time, Pallas kernels for 1%

profile of v1, /device:TPU:8, one launch (start us, length us, event | category | flops | bytes accessed | tf_op | source)
XLA Modules:
  0.0 1257.4 jit_solution(17405445483007125892)
XLA Ops:
  15.6 66.1 %all-gather.2 = bf16[32,80,10]{1,2,0:T(8,128)(2,1)S(1)} all-gather(bf16[1,80,10]{1,2,0:T(8,128)(2,1)S(1)} %bitcast.621), channel_id=1, replica_groups=mesh['span'=4,'seq'=8] {'span','seq'}, dimensions={0}, use_global_device_ids=true | all-gather | bytes 52800 | tf_op jit(solution)/shard_map/all_gather | solution.py:314
  94.6 21.1 %collective-permute-done.1 = bf16[2,3,2560]{2,1,0:T(4,128)(2,1)S(1)} collective-permute-done((bf16[2,3,2560]{2,1,0:T(4,128)(2,1)S(1)}, bf16[2,3,2560]{2,1,0:T(4,128)(2,1)S(1)}, u32[]{:S(2)}, u32[]{:S(2)}) %collective-permute-start.1) | collective-permute-done | bytes 30752 | tf_op jit(solution)/shard_map/ppermute | solution.py:349
  196.7 28.1 %collective-permute-done.20 = bf16[160,1280]{1,0:T(8,128)(2,1)} collective-permute-done((bf16[160,1280]{1,0:T(8,128)(2,1)}, bf16[160,1280]{1,0:T(8,128)(2,1)}, u32[]{:S(2)}, u32[]{:S(2)}) %collective-permute-start.20) | collective-permute-done | bytes 409632 | tf_op jit(solution)/shard_map/ppermute | solution.py:20
  230.1 16.2 %collective-permute-done.22 = bf16[160,1280]{1,0:T(8,128)(2,1)S(1)} collective-permute-done((bf16[160,1280]{1,0:T(8,128)(2,1)}, bf16[160,1280]{1,0:T(8,128)(2,1)S(1)}, u32[]{:S(2)}, u32[]{:S(2)}) %collective-permute-start.22) | collective-permute-done | bytes 409632 | tf_op jit(solution)/shard_map/ppermute | solution.py:20
  252.3 46.4 %collective-permute-done.57 = bf16[128,2560]{1,0:T(8,128)(2,1)} collective-permute-done((bf16[128,2560]{1,0:T(8,128)(2,1)}, bf16[128,2560]{1,0:T(8,128)(2,1)}, u32[]{:S(2)}, u32[]{:S(2)}) %collective-permute-start.57) | collective-permute-done | bytes 655392 | tf_op jit(solution)/shard_map/ppermute | solution.py:20
  300.7 25.3 %collective-permute-done.58 = bf16[128,2560]{1,0:T(8,128)(2,1)} collective-permute-done((bf16[128,2560]{1,0:T(8,128)(2,1)}, bf16[128,2560]{1,0:T(8,128)(2,1)}, u32[]{:S(2)}, u32[]{:S(2)}) %collective-permute-start.58) | collective-permute-done | bytes 655392 | tf_op jit(solution)/shard_map/ppermute | solution.py:20
  349.8 14.6 %collective-permute-done.26 = bf16[160,1280]{1,0:T(8,128)(2,1)S(1)} collective-permute-done((bf16[160,1280]{1,0:T(8,128)(2,1)}, bf16[160,1280]{1,0:T(8,128)(2,1)S(1)}, u32[]{:S(2)}, u32[]{:S(2)}) %collective-permute-start.26) | collective-permute-done | bytes 409632 | tf_op jit(solution)/shard_map/ppermute | solution.py:20
  372.1 13.6 %collective-permute-done.60 = bf16[128,2560]{1,0:T(8,128)(2,1)S(1)} collective-permute-done((bf16[128,2560]{1,0:T(8,128)(2,1)}, bf16[128,2560]{1,0:T(8,128)(2,1)S(1)}, u32[]{:S(2)}, u32[]{:S(2)}) %collective-permute-start.60) | collective-permute-done | bytes 655392 | tf_op jit(solution)/shard_map/ppermute | solution.py:20
  424.0 12.1 collective-permute-done.35
  446.0 32.4 %collective-permute-done.38 = bf16[128,2560]{1,0:T(8,128)(2,1)S(1)} collective-permute-done((bf16[128,2560]{1,0:T(8,128)(2,1)}, bf16[128,2560]{1,0:T(8,128)(2,1)S(1)}, u32[]{:S(2)}, u32[]{:S(2)}) %collective-permute-start.38) | collective-permute-done | bytes 655392 | tf_op jit(solution)/shard_map/ppermute | solution.py:20
  479.0 13.4 %collective-permute-done.37 = bf16[128,2560]{1,0:T(8,128)(2,1)} collective-permute-done((bf16[128,2560]{1,0:T(8,128)(2,1)}, bf16[128,2560]{1,0:T(8,128)(2,1)}, u32[]{:S(2)}, u32[]{:S(2)}) %collective-permute-start.37) | collective-permute-done | bytes 655392 | tf_op jit(solution)/shard_map/ppermute | solution.py:20
  492.4 12.0 fusion.7
  518.2 11.4 fusion.227
  545.2 13.1 %collective-permute-done.46 = bf16[128,2560]{1,0:T(8,128)(2,1)S(1)} collective-permute-done((bf16[128,2560]{1,0:T(8,128)(2,1)}, bf16[128,2560]{1,0:T(8,128)(2,1)S(1)}, u32[]{:S(2)}, u32[]{:S(2)}) %collective-permute-start.46) | collective-permute-done | bytes 655392 | tf_op jit(solution)/shard_map/ppermute | solution.py:20
  596.0 11.4 convolution_convert_fusion.5
  609.4 11.8 collective-permute-done.54
  621.8 13.5 %collective-permute-done.52 = bf16[128,2560]{1,0:T(8,128)(2,1)} collective-permute-done((bf16[128,2560]{1,0:T(8,128)(2,1)}, bf16[128,2560]{1,0:T(8,128)(2,1)}, u32[]{:S(2)}, u32[]{:S(2)}) %collective-permute-start.52) | collective-permute-done | bytes 655392 | tf_op jit(solution)/shard_map/ppermute | solution.py:20
  635.9 13.5 %collective-permute-done.50 = bf16[128,2560]{1,0:T(8,128)(2,1)} collective-permute-done((bf16[128,2560]{1,0:T(8,128)(2,1)S(1)}, bf16[128,2560]{1,0:T(8,128)(2,1)}, u32[]{:S(2)}, u32[]{:S(2)}) %collective-permute-start.50) | collective-permute-done | bytes 655392 | tf_op jit(solution)/shard_map/ppermute | solution.py:20
  653.1 10.2 collective-permute-done.68
  664.8 12.5 collective-permute-done.66
  677.4 13.6 %collective-permute-done.64 = bf16[128,2560]{1,0:T(8,128)(2,1)S(1)} collective-permute-done((bf16[128,2560]{1,0:T(8,128)(2,1)S(1)}, bf16[128,2560]{1,0:T(8,128)(2,1)S(1)}, u32[]{:S(2)}, u32[]{:S(2)}) %collective-permute-start.64) | collective-permute-done | bytes 655392 | tf_op jit(solution)/shard_map/ppermute | solution.py:20
  695.5 28.2 %collective-permute-done.55 = bf16[128,2560]{1,0:T(8,128)(2,1)S(1)} collective-permute-done((bf16[128,2560]{1,0:T(8,128)(2,1)S(1)}, bf16[128,2560]{1,0:T(8,128)(2,1)S(1)}, u32[]{:S(2)}, u32[]{:S(2)}) %collective-permute-start.55) | collective-permute-done | bytes 655392 | tf_op jit(solution)/shard_map/ppermute | solution.py:20
  723.8 24.9 %collective-permute-done.53 = bf16[128,2560]{1,0:T(8,128)(2,1)S(1)} collective-permute-done((bf16[128,2560]{1,0:T(8,128)(2,1)S(1)}, bf16[128,2560]{1,0:T(8,128)(2,1)S(1)}, u32[]{:S(2)}, u32[]{:S(2)}) %collective-permute-start.53) | collective-permute-done | bytes 655392 | tf_op jit(solution)/shard_map/ppermute | solution.py:20
  754.1 25.2 %collective-permute-done.69 = bf16[128,2560]{1,0:T(8,128)(2,1)S(1)} collective-permute-done((bf16[128,2560]{1,0:T(8,128)(2,1)S(1)}, bf16[128,2560]{1,0:T(8,128)(2,1)S(1)}, u32[]{:S(2)}, u32[]{:S(2)}) %collective-permute-start.69) | collective-permute-done | bytes 655392 | tf_op jit(solution)/shard_map/ppermute | solution.py:20
  796.3 12.1 collective-permute-done.70
  858.9 14.5 %all-gather.14.cloned.1.call-done = f32[256,1280]{1,0:T(8,128)} async-done(((f32[8,1280]{1,0:T(8,128)}), f32[256,1280]{1,0:T(8,128)}) %all-gather.14.cloned.1.call-update) | async-done | bytes 1310736 | tf_op jit(solution)/shard_map/all_gather | solution.py:370
  954.7 37.8 %collective-permute-done.92 = bf16[4,160,384]{2,1,0:T(8,128)(2,1)} collective-permute-done((bf16[4,160,384]{2,1,0:T(8,128)(2,1)}, bf16[4,160,384]{2,1,0:T(8,128)(2,1)}, u32[]{:S(2)}, u32[]{:S(2)}) %collective-permute-start.92) | collective-permute-done | bytes 491552 | tf_op jit(solution)/shard_map/ppermute | solution.py:20
  1013.5 70.7 %collective-permute-done.96 = bf16[160,384]{1,0:T(8,128)(2,1)S(1)} collective-permute-done((bf16[160,384]{1,0:T(8,128)(2,1)S(1)}, bf16[160,384]{1,0:T(8,128)(2,1)S(1)}, u32[]{:S(2)}, u32[]{:S(2)}) %collective-permute-start.96) | collective-permute-done | bytes 122912 | tf_op jit(solution)/shard_map/ppermute | solution.py:20
  1105.8 15.6 %collective-permute-done.87 = bf16[160,1280]{1,0:T(8,128)(2,1)S(1)} collective-permute-done((bf16[160,1280]{1,0:T(8,128)(2,1)S(1)}, bf16[160,1280]{1,0:T(8,128)(2,1)S(1)}, u32[]{:S(2)}, u32[]{:S(2)}) %collective-permute-start.87) | collective-permute-done | bytes 409632 | tf_op jit(solution)/shard_map/ppermute | solution.py:20
  1130.2 17.9 %collective-permute-done.88 = bf16[160,1280]{1,0:T(8,128)(2,1)S(1)} collective-permute-done((bf16[160,1280]{1,0:T(8,128)(2,1)S(1)}, bf16[160,1280]{1,0:T(8,128)(2,1)S(1)}, u32[]{:S(2)}, u32[]{:S(2)}) %collective-permute-start.88) | collective-permute-done | bytes 409632 | tf_op jit(solution)/shard_map/ppermute | solution.py:20
  1178.8 29.5 %collective-permute-done.80 = bf16[4,160,1280]{2,1,0:T(8,128)(2,1)S(1)} collective-permute-done((bf16[4,160,1280]{2,1,0:T(8,128)(2,1)S(1)}, bf16[4,160,1280]{2,1,0:T(8,128)(2,1)S(1)}, u32[]{:S(2)}, u32[]{:S(2)}) %collective-permute-start.80) | collective-permute-done | bytes 1638432 | tf_op jit(solution)/shard_map/ppermute | solution.py:20
  1222.1 16.9 %collective-permute-done.83 = bf16[160,1280]{1,0:T(8,128)(2,1)S(1)} collective-permute-done((bf16[160,1280]{1,0:T(8,128)(2,1)S(1)}, bf16[160,1280]{1,0:T(8,128)(2,1)S(1)}, u32[]{:S(2)}, u32[]{:S(2)}) %collective-permute-start.83) | collective-permute-done | bytes 409632 | tf_op jit(solution)/shard_map/ppermute | solution.py:20
  (750 shorter events, 534.5 us)
Async XLA Ops:
  7.2 156.7 %all-gather.8.cloned.1.call-start = ((), (), s32[]{:S(2)}) async-start(), calls=%async_computation | async-start | bytes 2703360 | tf_op jit(solution)/shard_map/all_gather | solution.py:338
  8.0 389.9 %all-gather.12.cloned.1.call-start = ((), (), s32[]{:S(2)}) async-start(), calls=%async_computation.2 | async-start | bytes 1351680 | tf_op jit(solution)/shard_map/all_gather | solution.py:370
  8.9 83.0 %collective-permute-start.2 = (bf16[2,3,2560]{2,1,0:T(4,128)(2,1)S(1)}, bf16[2,3,2560]{2,1,0:T(4,128)(2,1)S(1)}, u32[]{:S(2)}, u32[]{:S(2)}) collective-permute-start(bf16[2,3,2560]{2,1,0:T(4,128)(2,1)S(1)} %slice.532), channel_id=1, source_target_pairs={{1,3},{3,5},{5,7},{7,9},{9,11},{11,13},{13,15},{15,17},{17,19},{19... | collective-permute-start | bytes 92168 | tf_op jit(solution)/shard_map/ppermute | solution.py:349
  10.9 71.0 %collective-permute-start.19 = (bf16[80,1280]{1,0:T(8,128)(2,1)S(1)}, bf16[80,1280]{1,0:T(8,128)(2,1)S(1)}, u32[]{:S(2)}, u32[]{:S(2)}) collective-permute-start(bf16[80,1280]{1,0:T(8,128)(2,1)S(1)} %constant_dynamic-slice_fusion.37), channel_id=1, source_target_pairs={{0,1},{1,0},{2,3},{3,2},{4,5},{5,4},{6,7},{7,6},{8,9},{9,8},{10,11... | collective-permute-start | bytes 614408 | tf_op jit(solution)/shard_map/ppermute | solution.py:20
  15.3 66.6 %collective-permute-start.3 = (bf16[80,1280]{1,0:T(8,128)(2,1)S(1)}, bf16[80,1280]{1,0:T(8,128)(2,1)S(1)}, u32[]{:S(2)}, u32[]{:S(2)}) collective-permute-start(bf16[80,1280]{1,0:T(8,128)(2,1)S(1)} %constant_dynamic-slice_fusion.40), channel_id=1, source_target_pairs={{0,1},{1,0},{2,3},{3,2},{4,5},{5,4},{6,7},{7,6},{8,9},{9,8},{10,11... | collective-permute-start | bytes 614408 | tf_op jit(solution)/shard_map/ppermute | solution.py:20
  176.0 229.0 %all-gather.10.cloned.1.call-start = ((), (), s32[]{:S(2)}) async-start(), calls=%async_computation.1 | async-start | bytes 13516800 | tf_op jit(solution)/shard_map/all_gather | solution.py:338
  176.7 696.8 %all-gather.14.cloned.1.call-start = ((), (), s32[]{:S(2)}) async-start(), calls=%async_computation.3 | async-start | bytes 1351680 | tf_op jit(solution)/shard_map/all_gather | solution.py:370
  177.0 247.0 %collective-permute-start.40 = (bf16[1920,640]{1,0:T(8,128)(2,1)}, bf16[1920,640]{1,0:T(8,128)(2,1)}, u32[]{:S(2)}, u32[]{:S(2)}) collective-permute-start(bf16[1920,640]{1,0:T(8,128)(2,1)} %bitcast.628), channel_id=1, source_target_pairs={{0,16},{1,17},{2,18},{3,19},{4,20},{5,21},{6,22},{7,23},{8,24},{9,... | collective-permute-start | bytes 7372808 | tf_op jit(solution)/shard_map/ppermute | solution.py:20
  177.5 268.0 %collective-permute-start.39 = (bf16[1920,640]{1,0:T(8,128)(2,1)}, bf16[1920,640]{1,0:T(8,128)(2,1)}, u32[]{:S(2)}, u32[]{:S(2)}) collective-permute-start(bf16[1920,640]{1,0:T(8,128)(2,1)} %bitcast.629), channel_id=1, source_target_pairs={{0,8},{1,9},{2,10},{3,11},{4,12},{5,13},{6,14},{7,15},{8,0},{9,1},... | collective-permute-start | bytes 7372808 | tf_op jit(solution)/shard_map/ppermute | solution.py:20
  185.2 64.7 %collective-permute-start.56 = (bf16[128,2560]{1,0:T(8,128)(2,1)}, bf16[128,2560]{1,0:T(8,128)(2,1)}, u32[]{:S(2)}, u32[]{:S(2)}) collective-permute-start(bf16[128,2560]{1,0:T(8,128)(2,1)} %get-tuple-element.253), channel_id=1, source_target_pairs={{0,2},{1,3},{2,0},{3,1},{4,6},{5,7},{6,4},{7,5},{8,10},{9,11},{10,... | collective-permute-start | bytes 1966088 | tf_op jit(solution)/shard_map/ppermute | solution.py:20
  247.3 83.8 %collective-permute-start.59 = (bf16[128,2560]{1,0:T(8,128)(2,1)}, bf16[128,2560]{1,0:T(8,128)(2,1)S(1)}, u32[]{:S(2)}, u32[]{:S(2)}) collective-permute-start(bf16[128,2560]{1,0:T(8,128)(2,1)} %get-tuple-element.253), channel_id=1, source_target_pairs={{0,1},{1,0},{2,3},{3,2},{4,5},{5,4},{6,7},{7,6},{8,9},{9,8},{10,11... | collective-permute-start | bytes 1966088 | tf_op jit(solution)/shard_map/ppermute | solution.py:20
  249.9 76.1 %collective-permute-start.58 = (bf16[128,2560]{1,0:T(8,128)(2,1)}, bf16[128,2560]{1,0:T(8,128)(2,1)}, u32[]{:S(2)}, u32[]{:S(2)}) collective-permute-start(bf16[128,2560]{1,0:T(8,128)(2,1)} %get-tuple-element.253), channel_id=1, source_target_pairs={{0,6},{1,7},{2,4},{3,5},{4,2},{5,3},{6,0},{7,1},{8,14},{9,15},{10,... | collective-permute-start | bytes 1966088 | tf_op jit(solution)/shard_map/ppermute | solution.py:20
  298.7 66.5 %collective-permute-start.27 = (bf16[160,1280]{1,0:T(8,128)(2,1)}, bf16[160,1280]{1,0:T(8,128)(2,1)}, u32[]{:S(2)}, u32[]{:S(2)}) collective-permute-start(bf16[160,1280]{1,0:T(8,128)(2,1)} %get-tuple-element.326), channel_id=1, source_target_pairs={{0,8},{1,9},{2,10},{3,11},{4,12},{5,13},{6,14},{7,15},{8,0},{9,1},... | collective-permute-start | bytes 1228808 | tf_op jit(solution)/shard_map/ppermute | solution.py:20
  369.3 69.0 %collective-permute-start.43 = (bf16[960,640]{1,0:T(8,128)(2,1)}, bf16[960,640]{1,0:T(8,128)(2,1)}, u32[]{:S(2)}, u32[]{:S(2)}) collective-permute-start(bf16[960,640]{1,0:T(8,128)(2,1)} %bitcast.50), channel_id=1, source_target_pairs={{0,16},{1,17},{2,18},{3,19},{4,20},{5,21},{6,22},{7,23},{8,24},{9,... | collective-permute-start | bytes 3686408 | tf_op jit(solution)/shard_map/ppermute | solution.py:20
  438.3 54.1 %collective-permute-start.37 = (bf16[128,2560]{1,0:T(8,128)(2,1)}, bf16[128,2560]{1,0:T(8,128)(2,1)}, u32[]{:S(2)}, u32[]{:S(2)}) collective-permute-start(bf16[128,2560]{1,0:T(8,128)(2,1)} %get-tuple-element.255), channel_id=1, source_target_pairs={{0,4},{1,5},{2,6},{3,7},{4,0},{5,1},{6,2},{7,3},{8,12},{9,13},{10,... | collective-permute-start | bytes 1966088 | tf_op jit(solution)/shard_map/ppermute | solution.py:20
  445.5 58.9 %collective-permute-start.42 = (bf16[960,640]{1,0:T(8,128)(2,1)}, bf16[960,640]{1,0:T(8,128)(2,1)}, u32[]{:S(2)}, u32[]{:S(2)}) collective-permute-start(bf16[960,640]{1,0:T(8,128)(2,1)} %bitcast.50), channel_id=1, source_target_pairs={{0,8},{1,9},{2,10},{3,11},{4,12},{5,13},{6,14},{7,15},{8,0},{9,1},... | collective-permute-start | bytes 3686408 | tf_op jit(solution)/shard_map/ppermute | solution.py:20
  445.6 58.8 %collective-permute-start.44 = (bf16[960,640]{1,0:T(8,128)(2,1)}, bf16[960,640]{1,0:T(8,128)(2,1)}, u32[]{:S(2)}, u32[]{:S(2)}) collective-permute-start(bf16[960,640]{1,0:T(8,128)(2,1)} %collective-permute-done.43), channel_id=1, source_target_pairs={{0,8},{1,9},{2,10},{3,11},{4,12},{5,13},{6,14},{7,15},{8,0},{9,1},... | collective-permute-start | bytes 3686408 | tf_op jit(solution)/shard_map/ppermute | solution.py:20
  582.7 235.2 %collective-permute-start.107 = (bf16[960,1280]{1,0:T(8,128)(2,1)}, bf16[960,1280]{1,0:T(8,128)(2,1)}, u32[]{:S(2)}, u32[]{:S(2)}) collective-permute-start(bf16[960,1280]{1,0:T(8,128)(2,1)} %convolution_convert_fusion.6), channel_id=1, source_target_pairs={{0,8},{1,9},{2,10},{3,11},{4,12},{5,13},{6,14},{7,15},{8,0},{9,1},... | collective-permute-start | bytes 7372808 | tf_op jit(solution)/shard_map/ppermute | solution.py:20
  589.6 105.3 %collective-permute-start.49 = (bf16[128,2560]{1,0:T(8,128)(2,1)S(1)}, bf16[128,2560]{1,0:T(8,128)(2,1)S(1)}, u32[]{:S(2)}, u32[]{:S(2)}) collective-permute-start(bf16[128,2560]{1,0:T(8,128)(2,1)S(1)} %get-tuple-element.186), channel_id=1, source_target_pairs={{0,1},{1,0},{2,3},{3,2},{4,5},{5,4},{6,7},{7,6},{8,9},{9,8},{10,11... | collective-permute-start | bytes 1966088 | tf_op jit(solution)/shard_map/ppermute | solution.py:20
  592.2 57.2 %collective-permute-start.50 = (bf16[128,2560]{1,0:T(8,128)(2,1)S(1)}, bf16[128,2560]{1,0:T(8,128)(2,1)}, u32[]{:S(2)}, u32[]{:S(2)}) collective-permute-start(bf16[128,2560]{1,0:T(8,128)(2,1)S(1)} %get-tuple-element.189), channel_id=1, source_target_pairs={{0,1},{1,0},{2,3},{3,2},{4,5},{5,4},{6,7},{7,6},{8,9},{9,8},{10,11... | collective-permute-start | bytes 1966088 | tf_op jit(solution)/shard_map/ppermute | solution.py:20
  690.9 57.8 %collective-permute-start.53 = (bf16[128,2560]{1,0:T(8,128)(2,1)S(1)}, bf16[128,2560]{1,0:T(8,128)(2,1)S(1)}, u32[]{:S(2)}, u32[]{:S(2)}) collective-permute-start(bf16[128,2560]{1,0:T(8,128)(2,1)S(1)} %get-tuple-element.169), channel_id=1, source_target_pairs={{0,4},{1,5},{2,6},{3,7},{4,0},{5,1},{6,2},{7,3},{8,12},{9,13},{10,... | collective-permute-start | bytes 1966088 | tf_op jit(solution)/shard_map/ppermute | solution.py:20
  694.9 59.2 %collective-permute-start.63 = (bf16[128,2560]{1,0:T(8,128)(2,1)S(1)}, bf16[128,2560]{1,0:T(8,128)(2,1)S(1)}, u32[]{:S(2)}, u32[]{:S(2)}) collective-permute-start(bf16[128,2560]{1,0:T(8,128)(2,1)S(1)} %get-tuple-element.182), channel_id=1, source_target_pairs={{0,1},{1,0},{2,3},{3,2},{4,5},{5,4},{6,7},{7,6},{8,9},{9,8},{10,11... | collective-permute-start | bytes 1966088 | tf_op jit(solution)/shard_map/ppermute | solution.py:20
  695.5 58.5 %collective-permute-start.65 = (bf16[128,2560]{1,0:T(8,128)(2,1)S(1)}, bf16[128,2560]{1,0:T(8,128)(2,1)S(1)}, u32[]{:S(2)}, u32[]{:S(2)}) collective-permute-start(bf16[128,2560]{1,0:T(8,128)(2,1)S(1)} %get-tuple-element.164), channel_id=1, source_target_pairs={{0,2},{1,3},{2,0},{3,1},{4,6},{5,7},{6,4},{7,5},{8,10},{9,11},{10,... | collective-permute-start | bytes 1966088 | tf_op jit(solution)/shard_map/ppermute | solution.py:20
  723.8 55.5 %collective-permute-start.69 = (bf16[128,2560]{1,0:T(8,128)(2,1)S(1)}, bf16[128,2560]{1,0:T(8,128)(2,1)S(1)}, u32[]{:S(2)}, u32[]{:S(2)}) collective-permute-start(bf16[128,2560]{1,0:T(8,128)(2,1)S(1)} %get-tuple-element.165), channel_id=1, source_target_pairs={{0,6},{1,7},{2,4},{3,5},{4,2},{5,3},{6,0},{7,1},{8,14},{9,15},{10,... | collective-permute-start | bytes 1966088 | tf_op jit(solution)/shard_map/ppermute | solution.py:20
  836.1 76.0 %collective-permute-start.105 = (bf16[1920,1280]{1,0:T(8,128)(2,1)}, bf16[1920,1280]{1,0:T(8,128)(2,1)}, u32[]{:S(2)}, u32[]{:S(2)}) collective-permute-start(bf16[1920,1280]{1,0:T(8,128)(2,1)} %convolution_convert_fusion), channel_id=1, source_target_pairs={{0,8},{1,9},{2,10},{3,11},{4,12},{5,13},{6,14},{7,15},{8,0},{9,1},... | collective-permute-start | bytes 14745608 | tf_op jit(solution)/shard_map/ppermute | solution.py:20
  844.1 93.2 %collective-permute-start.85 = (bf16[1280,1280]{1,0:T(8,128)(2,1)}, bf16[1280,1280]{1,0:T(8,128)(2,1)}, u32[]{:S(2)}, u32[]{:S(2)}) collective-permute-start(bf16[1280,1280]{1,0:T(8,128)(2,1)} %convolution_convert_fusion.1), channel_id=1, source_target_pairs={{0,8},{1,9},{2,10},{3,11},{4,12},{5,13},{6,14},{7,15},{8,0},{9,1},... | collective-permute-start | bytes 9830408 | tf_op jit(solution)/shard_map/ppermute | solution.py:20
  847.7 97.4 %collective-permute-start.98 = (bf16[640,2560]{1,0:T(8,128)(2,1)}, bf16[640,2560]{1,0:T(8,128)(2,1)}, u32[]{:S(2)}, u32[]{:S(2)}) collective-permute-start(bf16[640,2560]{1,0:T(8,128)(2,1)} %convolution_convert_fusion.3), channel_id=1, source_target_pairs={{0,8},{1,9},{2,10},{3,11},{4,12},{5,13},{6,14},{7,15},{8,0},{9,1},... | collective-permute-start | bytes 9830408 | tf_op jit(solution)/shard_map/ppermute | solution.py:20
  912.1 254.4 %collective-permute-start.79 = (bf16[1280,1280]{1,0:T(8,128)(2,1)}, bf16[1280,1280]{1,0:T(8,128)(2,1)}, u32[]{:S(2)}, u32[]{:S(2)}) collective-permute-start(bf16[1280,1280]{1,0:T(8,128)(2,1)} %convolution_convert_fusion.2), channel_id=1, source_target_pairs={{0,8},{1,9},{2,10},{3,11},{4,12},{5,13},{6,14},{7,15},{8,0},{9,1},... | collective-permute-start | bytes 9830408 | tf_op jit(solution)/shard_map/ppermute | solution.py:20
  925.5 246.5 %collective-permute-start.106 = (bf16[1920,640]{1,0:T(8,128)(2,1)}, bf16[1920,640]{1,0:T(8,128)(2,1)}, u32[]{:S(2)}, u32[]{:S(2)}) collective-permute-start(bf16[1920,640]{1,0:T(8,128)(2,1)} %slice.916), channel_id=1, source_target_pairs={{0,16},{1,17},{2,18},{3,19},{4,20},{5,21},{6,22},{7,23},{8,24},{9,... | collective-permute-start | bytes 7372808 | tf_op jit(solution)/shard_map/ppermute | solution.py:20
  1010.2 86.2 %collective-permute-start.86 = (bf16[4,160,1280]{2,1,0:T(8,128)(2,1)}, bf16[4,160,1280]{2,1,0:T(8,128)(2,1)}, u32[]{:S(2)}, u32[]{:S(2)}) collective-permute-start(bf16[4,160,1280]{2,1,0:T(8,128)(2,1)} %bitcast.114), channel_id=1, source_target_pairs={{0,16},{1,17},{2,18},{3,19},{4,20},{5,21},{6,22},{7,23},{8,24},{9,... | collective-permute-start | bytes 4915208 | tf_op jit(solution)/shard_map/ppermute | solution.py:20
  1011.4 88.8 %collective-permute-start.99 = (bf16[4,160,1280]{2,1,0:T(8,128)(2,1)}, bf16[4,160,1280]{2,1,0:T(8,128)(2,1)}, u32[]{:S(2)}, u32[]{:S(2)}) collective-permute-start(bf16[4,160,1280]{2,1,0:T(8,128)(2,1)} %dynamic-slice_convert_fusion), channel_id=1, source_target_pairs={{0,16},{1,17},{2,18},{3,19},{4,20},{5,21},{6,22},{7,23},{8,24},{9,... | collective-permute-start | bytes 4915208 | tf_op jit(solution)/shard_map/ppermute | solution.py:20
  1012.5 71.8 %collective-permute-start.96 = (bf16[160,384]{1,0:T(8,128)(2,1)S(1)}, bf16[160,384]{1,0:T(8,128)(2,1)S(1)}, u32[]{:S(2)}, u32[]{:S(2)}) collective-permute-start(bf16[160,384]{1,0:T(8,128)(2,1)S(1)} %get-tuple-element.136), channel_id=1, source_target_pairs={{0,16},{1,17},{2,18},{3,19},{4,20},{5,21},{6,22},{7,23},{8,24},{9,... | collective-permute-start | bytes 368648 | tf_op jit(solution)/shard_map/ppermute | solution.py:20
  (237 other events, 5269.8 us)
Sparse Core Ops, SparseCore 0:
  11.0 58.1 all-gather.7
  176.1 62.2 all-gather.11
  241.2 156.4 all-gather.9
  818.0 55.4 all-gather.13

commit v2 on v1

--- a/solution.py
+++ b/solution.py
@@ -268,6 +268,373 @@
     )(*[a for a, _ in arrays])
 
 
+MESH = pl.DeviceIdType.MESH
+VMEM_LIMIT = 60 * 1024 * 1024
+
+
+class Links:
+    def __init__(self, sizes, sends, recvs):
+        self.spans, self.seqs = sizes
+        self.span, self.seq = lax.axis_index("span"), lax.axis_index("seq")
+        self.sends, self.recvs = sends, recvs
+        self.used = 0
+        self.open = []
+
+    def flipped(self, index, mask):
+        bit = 1
+        while bit <= mask:
+            if mask & bit:
+                index = index + (1 - 2 * (index // bit % 2)) * bit
+            bit *= 2
+        return index
+
+    def peer(self, mask):
+        low, high = mask % self.seqs, mask // self.seqs
+        return (self.flipped(self.span, high), self.flipped(self.seq, low))
+
+    def other(self, mask):
+        span, seq = self.peer(mask)
+        return span * self.seqs + seq
+
+    def greet(self, masks):
+        barrier = pltpu.get_barrier_semaphore()
+        for mask in masks:
+            pl.semaphore_signal(barrier, inc=1, device_id=self.peer(mask), device_id_type=MESH)
+        pl.semaphore_wait(barrier, len(masks))
+
+    def send(self, source, target, mask, only=None):
+        slot = self.used
+        self.used += 1
+        copy = pltpu.make_async_remote_copy(
+            source, target, self.sends.at[slot], self.recvs.at[slot], device_id=self.peer(mask), device_id_type=MESH
+        )
+        if only is None:
+            copy.start()
+        else:
+            pl.when(only)(copy.start)
+        self.open.append((copy, only))
+        return copy
+
+    def close(self):
+        for copy, only in self.open:
+            if only is None:
+                copy.wait_send()
+            else:
+                pl.when(only)(copy.wait_send)
+
+
+def in_turn(parts, order):
+    for name in order:
+        next(parts[name], None)
+    for part in parts.values():
+        for _ in part:
+            pass
+
+
+def gather_kernel(
+    sizes, share, half, rec_proj, out_proj, gate_weight, small, tokens, wide, narrow,
+    proj_x, proj_y, out_half, gates, every, tokens_o, wide_o, narrow_o, sends, recvs, locals_,
+):
+    links = Links(sizes, sends, recvs)
+    spans, seqs = sizes
+    count = spans * seqs
+    me = links.span * seqs + links.seq
+    side = me % 2
+    upper = me // (count // 2)
+    inner = [2 * k for k in range(1, seqs // 2)]
+    core, top = seqs, count // 2
+    double = 2 * share
+    links.greet([1, *inner, core, top])
+    kept = [0]
+
+    def local(source, target, only=None):
+        copy = pltpu.make_async_copy(source, target, locals_.at[kept[0]])
+        kept[0] += 1
+        if only is None:
+            copy.start()
+        else:
+            pl.when(only)(copy.start)
+        return copy
+
+    def pieces_out(place, piece):
+        over_inner = {m: links.send(piece(place(me)), piece(place(me)), m) for m in inner}
+        over_top = {0: links.send(piece(place(me)), piece(place(me)), top)}
+        over_core = [links.send(piece(place(me)), piece(place(me)), core)]
+        yield
+        for m in inner:
+            over_inner[m].wait_recv()
+            there = piece(place(links.other(m)))
+            over_top[m] = links.send(there, there, top)
+            over_core.append(links.send(there, there, core))
+        yield
+        for m in (0, *inner):
+            over_top[m].wait_recv()
+            there = piece(place(links.other(top + m)))
+            over_core.append(links.send(there, there, core))
+        yield
+        for copy in over_core:
+            copy.wait_recv()
+
+    def columns_part(source, first, target):
+        def piece(start):
+            return target.at[pl.ds(pl.multiple_of(start, 16), double)]
+
+        def columns(which):
+            return source.at[:, pl.ds(pl.multiple_of(first + which * half, 128), half)]
+
+        row = target.at[pl.ds(pl.multiple_of(me * share, 16), share)]
+        mine = local(columns(side), row)
+        theirs = links.send(columns(1 - side), row, 1)
+        yield
+        mine.wait()
+        theirs.wait_recv()
+        yield from pieces_out(lambda d: d // 2 * double, piece)
+
+    def whole_part(source, target):
+        height = source.shape[0]
+
+        def piece(start):
+            return target.at[pl.ds(pl.multiple_of(start, 16), 2 * height)]
+
+        row = target.at[pl.ds(pl.multiple_of(me * height, 16), height)]
+        mine = local(source, row)
+        theirs = links.send(source, row, 1)
+        yield
+        mine.wait()
+        theirs.wait_recv()
+        yield from pieces_out(lambda d: d // 2 * 2 * height, piece)
+
+    def rows_part(source, target):
+        width = source.shape[1]
+        pairs_half = count // 4
+
+        def place(d):
+            return d // 2 % pairs_half * double
+
+        def rows(start, size):
+            return target.at[pl.ds(pl.multiple_of(start, 16), size)]
+
+        def piece(start, which):
+            return target.at[pl.ds(pl.multiple_of(start, 16), double), pl.ds(pl.multiple_of(which * (width // 2), 128), width // 2)]
+
+        holds = side == upper
+        row = rows(place(me) + side * share, share)
+        mine = local(source, row, holds)
+        gift = links.send(source, row, 1, side != upper)
+        yield
+
+        @pl.when(holds)
+        def _():
+            mine.wait()
+            gift.wait_recv()
+
+        across = links.send(rows(place(me), double), rows(place(me), double), top, holds)
+        pl.when(side != upper)(across.wait_recv)
+        over_inner = {m: links.send(piece(place(me), upper), piece(place(me), upper), m) for m in inner}
+        over_core = [links.send(rows(place(me), double), rows(place(me), double), core)]
+        over_top = {}
+        yield
+        for m in inner:
+            over_inner[m].wait_recv()
+            there = piece(place(links.other(m)), upper)
+            over_top[m] = links.send(there, there, top)
+            over_core.append(links.send(there, there, core))
+        yield
+        for m in inner:
+            over_top[m].wait_recv()
+            there = piece(place(links.other(m)), 1 - upper)
+            over_core.append(links.send(there, there, core))
+        yield
+        for copy in over_core:
+            copy.wait_recv()
+
+    parts = {
+        "x": columns_part(rec_proj, 0, proj_x),
+        "s": whole_part(small, every),
+        "g": rows_part(gate_weight, gates),
+        "y": columns_part(rec_proj, 2 * half, proj_y),
+        "o": rows_part(out_proj, out_half),
+    }
+    in_turn(parts, "xsgxsgyoxyxogsygsygoyo")
+    links.close()
+
+
+def gather_weights(sizes, rec_proj, out_proj, gate_weight, small, tokens, wide, narrow):
+    share = rec_proj.shape[0]
+    half = rec_proj.shape[1] // 4
+    count = sizes[0] * sizes[1]
+    held = [
+        (count * share, half), (count * share, half), (count // 2 * share, out_proj.shape[1]),
+        (count // 2 * share, gate_weight.shape[1]), (count * small.shape[0], small.shape[1]),
+        tokens.shape, wide.shape, narrow.shape,
+    ]
+    anywhere = pl.BlockSpec(memory_space=pl.ANY)
+    copies = 5 * 16
+    return pl.pallas_call(
+        functools.partial(gather_kernel, sizes, share, half),
+        in_specs=[anywhere] * 7,
+        out_specs=[anywhere] * 8,
+        out_shape=[jax.ShapeDtypeStruct(s, BF16) for s in held],
+        scratch_shapes=[
+            pltpu.SemaphoreType.DMA((copies,)), pltpu.SemaphoreType.DMA((copies,)), pltpu.SemaphoreType.DMA((8,))
+        ],
+        input_output_aliases={4: 5, 5: 6, 6: 7},
+        compiler_params=pltpu.CompilerParams(collective_id=0, has_side_effects=True, vmem_limit_bytes=VMEM_LIMIT),
+    )(rec_proj, out_proj, gate_weight, small, tokens, wide, narrow)
+
+
+def scatter_kernel(
+    sizes, share, kept_d, given_d, kept_m, given_m, grad_x, grad_y, branch, kept_g, given_g, kept_n, given_n,
+    proj_o, out_o, gate_o, gain_o, sends, recvs, *bufs,
+):
+    links = Links(sizes, sends, recvs)
+    spans, seqs = sizes
+    count = spans * seqs
+    me = links.span * seqs + links.seq
+    side = me % 2
+    upper = me // (count // 2)
+    inner = [2 * k for k in range(1, seqs // 2)]
+    core, top = seqs, count // 2
+    double = 2 * share
+    n = len(inner) + 1
+    links.greet([1, *inner, core, top])
+
+    def part(kept, given, cols, scratch, finish):
+        to_core, from_core, to_top, from_top, to_inner, from_inner, to_side, from_side = scratch
+        crossing = []
+        for i in range(2):
+            for j in range(n):
+                to_core[i * n + j] = given((1 - i) * n + j).astype(BF16)
+            crossing.append(links.send(to_core.at[pl.ds(i * n, n)], from_core.at[pl.ds(i * n, n)], core))
+        yield
+        crossing[0].wait_recv()
+        over_top = {}
+        for j in (*range(1, n), 0):
+            to_top[j] = (kept(n + j) + from_core[j].astype(F32)).astype(BF16)
+            over_top[j] = links.send(to_top.at[j], from_top.at[j], top)
+        crossing[1].wait_recv()
+        yield
+        over_inner = []
+        for j in range(1, n):
+            over_top[j].wait_recv()
+            to_inner[j - 1] = (kept(j) + from_core[n + j].astype(F32) + from_top[j].astype(F32)).astype(BF16)
+            over_inner.append(links.send(to_inner.at[j - 1], from_inner.at[j - 1], inner[j - 1]))
+        over_top[0].wait_recv()
+        yield
+        total = kept(0) + from_core[n].astype(F32) + from_top[0].astype(F32)
+        for j in range(1, n):
+            over_inner[j - 1].wait_recv()
+            total = total + from_inner[j - 1].astype(F32)
+        yield from finish(total, to_side, from_side)
+
+    def sided(total):
+        low, high = total[:share], total[share:]
+        first = side == 0
+        return jnp.where(first, low, high), jnp.where(first, high, low)
+
+    def by_columns(put):
+        def finish(total, to_side, from_side):
+            mine, theirs = sided(total)
+            to_side[...] = theirs.astype(BF16)
+            copy = links.send(to_side, from_side, 1)
+            yield
+            copy.wait_recv()
+            put(mine, from_side[...].astype(F32))
+
+        return finish
+
+    def into(first, cols):
+        def put(mine, recv):
+            proj_o[:, first : first + cols] = jnp.where(side == 0, mine, recv)
+            proj_o[:, first + cols : first + 2 * cols] = jnp.where(side == 0, recv, mine)
+
+        return put
+
+    def put_gain(mine, recv):
+        gain_o[...] = mine + recv
+
+    def by_rows(target, to_last, from_last):
+        cols = target.shape[1] // 2
+
+        def finish(total, to_side, from_side):
+            to_side[...] = total.astype(BF16)
+            copy = links.send(to_side, from_side, top)
+            yield
+            copy.wait_recv()
+            other = from_side[...].astype(F32)
+            first = side == 0
+            (low, low_far), (high, high_far) = sided(jnp.where(first, total, other)), sided(jnp.where(first, other, total))
+            to_last[:, :cols] = low_far.astype(BF16)
+            to_last[:, cols:] = high_far.astype(BF16)
+            copy = links.send(to_last, from_last, 1)
+            yield
+            copy.wait_recv()
+            holds = side == upper
+            target[:, :cols] = jnp.where(holds, low, from_last[:, :cols].astype(F32))
+            target[:, cols:] = jnp.where(holds, high, from_last[:, cols:].astype(F32))
+
+        return finish
+
+    def product(lhs, rhs, wrap, columns=None):
+        def block(j):
+            rows = lhs[j % wrap * double : (j % wrap + 1) * double]
+            if columns is None:
+                return jnp.dot(rows, rhs[...], preferred_element_type=F32)
+            which = upper if j < n else 1 - upper
+            right = rhs[:, pl.ds(pl.multiple_of(which * columns, 128), columns)]
+            return jnp.dot(rows, right, preferred_element_type=F32)
+
+        return block
+
+    def stored(blocks, columns=None):
+        def block(j):
+            if columns is None:
+                return blocks[j * double : (j + 1) * double].astype(F32)
+            which = upper if j < n else 1 - upper
+            return blocks[j % n * double : (j % n + 1) * double, pl.ds(pl.multiple_of(which * columns, 128), columns)].astype(F32)
+
+        return block
+
+    half = grad_x.shape[1]
+    wide = branch.shape[1] // 2
+    thin = kept_g.shape[1] // 2
+    parts = {
+        "y": part(product(kept_d, grad_y, 2 * n), product(given_d, grad_y, 2 * n), half, bufs[0:8], by_columns(into(2 * half, half))),
+        "o": part(product(kept_m, branch, n, wide), product(given_m, branch, n, wide), wide, bufs[8:16], by_rows(out_o, *bufs[16:18])),
+        "x": part(product(kept_d, grad_x, 2 * n), product(given_d, grad_x, 2 * n), half, bufs[18:26], by_columns(into(0, half))),
+        "g": part(stored(kept_g, thin), stored(given_g, thin), thin, bufs[26:34], by_rows(gate_o, *bufs[34:36])),
+        "n": part(stored(kept_n), stored(given_n), kept_n.shape[1], bufs[36:44], by_columns(put_gain)),
+    }
+    in_turn(parts, "yxoyxoyxgnoyxgnoygnoxoygnoxgngg")
+    links.close()
+
+
+def scatter_grads(sizes, kept_d, given_d, kept_m, given_m, grad_x, grad_y, branch, kept_g, given_g, kept_n, given_n):
+    n = sizes[1] // 2
+    share = kept_d.shape[0] // (4 * n)
+    half, wide, thin, gain = grad_x.shape[1], branch.shape[1], kept_g.shape[1], kept_n.shape[1]
+
+    def scratch(cols, last):
+        double = 2 * share
+        side = share if last is None else double
+        shapes = [(2 * n, double, cols)] * 2 + [(n, double, cols)] * 2 + [(n - 1, double, cols)] * 2 + [(side, cols)] * 2
+        if last is not None:
+            shapes += [(share, last)] * 2
+        return [pltpu.VMEM(s, BF16) for s in shapes]
+
+    bufs = [*scratch(half, None), *scratch(wide // 2, wide), *scratch(half, None), *scratch(thin // 2, thin), *scratch(gain, None)]
+    copies = 5 * (2 + n + (n - 1) + 2)
+    inside = pl.BlockSpec(memory_space=pltpu.VMEM)
+    return pl.pallas_call(
+        functools.partial(scatter_kernel, sizes, share),
+        in_specs=[inside] * 11,
+        out_specs=[inside] * 4,
+        out_shape=[jax.ShapeDtypeStruct((share, cols), F32) for cols in (4 * half, wide, thin, gain)],
+        scratch_shapes=[pltpu.SemaphoreType.DMA((copies,)), pltpu.SemaphoreType.DMA((copies,)), *bufs],
+        compiler_params=pltpu.CompilerParams(collective_id=1, has_side_effects=True, vmem_limit_bytes=VMEM_LIMIT),
+    )(kept_d, given_d, kept_m, given_m, grad_x, grad_y, branch, kept_g, given_g, kept_n, given_n)
+
+
 def on_device(
     inputs, norm_one, rec_proj, conv_weight, conv_bias, gate_weight, gate_bias, decay_param, out_proj, norm_two,
     mlp_wide, mlp_narrow, cotangent,
@@ -308,13 +675,7 @@
     def cut(v, index, size, axis):
         return lax.dynamic_slice_in_dim(v, index * size, size, axis)
 
-    small = jnp.concatenate(
-        [norm_one[:, None], norm_two[:, None], conv_weight, conv_bias[:, None], gate_bias, decay_param[:, None]], axis=1
-    )
-    small = lax.all_gather(small, AXES, axis=0, tiled=True).astype(F32).T
-    gain_one, gain_two = small[0], small[1]
-    rate_pre = cut(small[9:10], side, half, 1)
-    chan = cut(jnp.concatenate([small[2:9], jax.nn.softplus(small[9:10])], axis=0), side, half, 1)
+    direct = share % 16 == 0 and spans == 4
 
     def gathered_rows(block, buffer, place):
         pieces = {0: block}
@@ -338,10 +699,29 @@
         full = lax.all_gather(block, AXES, axis=0, tiled=True)
         return cut(full, side, half, 0)
 
-    proj_x = columns_half(rec_proj[:, :width])
-    proj_y = columns_half(rec_proj[:, width:])
-    gates = rows_half(gate_weight)
-    out_half = rows_half(out_proj)
+    def by_span(v):
+        size = width // spans
+        return jnp.concatenate([cut(v, span ^ j, size, 1) for j in range(spans)], axis=1)
+
+    small = jnp.stack([norm_one, norm_two, *conv_weight.T, conv_bias, *gate_bias.T, decay_param])
+    wide_own = mlp_wide.transpose(1, 2, 0).reshape(2 * units, width // spans)
+    narrow_own = mlp_narrow.T
+    grads_own = by_span(to_rows(cotangent))
+    if direct:
+        packed = jnp.pad(small, ((0, 6), (0, -share % 128)))
+        proj_x, proj_y, out_half, gates, small, grads_own, wide_own, narrow_own = gather_weights(
+            (spans, seqs), rec_proj, out_proj, gate_weight, packed, grads_own, wide_own, narrow_own
+        )
+        small = small.reshape(count, 16, -1)[:, :10, :share].transpose(1, 0, 2).reshape(10, width)
+    else:
+        proj_x = columns_half(rec_proj[:, :width])
+        proj_y = columns_half(rec_proj[:, width:])
+        gates = rows_half(gate_weight)
+        out_half = rows_half(out_proj)
+        small = lax.all_gather(small, AXES, axis=1, tiled=True)
+    small = small.astype(F32)
+    gain_one, gain_two = small[0], small[1]
+    chan = cut(jnp.concatenate([small[2:9], jax.nn.softplus(small[9:10])], axis=0), side, half, 1)
 
     mine = to_rows(inputs)
     x = mine.astype(F32)
@@ -397,10 +777,6 @@
 
     resid = x + over_sides(nn(mixed, out_half))
 
-    def by_span(v):
-        size = width // spans
-        return jnp.concatenate([cut(v, span ^ j, size, 1) for j in range(spans)], axis=1)
-
     def span_gather(block):
         pieces = {0: block}
         for m in xs:
@@ -409,17 +785,16 @@
             pieces[n ^ core] = swap(pieces[n], core)
         return jnp.concatenate([pieces[m * seqs] for m in range(spans)], axis=1)
 
-    wide = span_gather(mlp_wide.transpose(1, 2, 0).reshape(2 * units, width // spans))
-    narrow = span_gather(mlp_narrow.T)
+    wide = span_gather(wide_own)
+    narrow = span_gather(narrow_own)
 
     def token_gather(v):
         blocks = [v] + [swap(v, m) for m in inner]
         others = [swap(b, 1) for b in blocks]
         return jnp.concatenate(blocks, axis=0), jnp.concatenate(others, axis=0)
 
-    c = to_rows(cotangent)
-    grads = token_gather(by_span(c))
-    c = c.astype(F32)
+    grads = token_gather(grads_own)
+    c = to_rows(cotangent).astype(F32)
     normal_two = token_gather(by_span(normed(resid, gain_two).astype(BF16)))
 
     def activate(values):
@@ -524,14 +899,6 @@
         other = lax.dynamic_index_in_dim(out, 1 - side, 0, keepdims=False).astype(BF16)
         return lax.dynamic_index_in_dim(out, side, 0, keepdims=False), swap(other, 1).astype(F32)
 
-    order = [m ^ n for m in (0, *xs) for n in (0, *inner)]
-    turned = normal_one.T
-    kept = jnp.concatenate(blocks_of(turned, order, pairs), axis=0)
-    given = jnp.concatenate(blocks_of(turned, [m ^ core for m in order], pairs), axis=0)
-    proj_owned = jnp.concatenate(
-        [in_order(*to_columns_owner(nn(kept, g), nn(given, g, BF16)), 1) for g in (x_grad, y_grad)], axis=1
-    )
-
     def to_rows_owner(v_kept, v_given):
         cols = v_kept.shape[1]
         total = (v_kept + swap(v_given, core).astype(F32)).reshape(len(low_order), 2 * share, cols)
@@ -546,21 +913,30 @@
         here = lax.dynamic_index_in_dim(out, side, 0, keepdims=False)
         return jnp.where(upper == side, here, swap(gone, 1).astype(F32))
 
+    order = [m ^ n for m in (0, *xs) for n in (0, *inner)]
     low_order = [m ^ n for m in (0, *[v for v in xs if v < top]) for n in (0, *inner)]
-    turned = mixed.T
-    kept = jnp.concatenate(blocks_of(turned, low_order, pairs // 2), axis=0)
-    given = jnp.concatenate(blocks_of(turned, [m ^ core for m in low_order], pairs // 2), axis=0)
-    out_owned = to_rows_owner(nn(kept, branch_low), nn(given, branch_low, BF16))
+
+    def ordered(v, masks, wrap):
+        return [jnp.concatenate(blocks_of(v, [m ^ c for m in masks], wrap), axis=0) for c in (0, core)]
+
+    kept_d, given_d = ordered(normal_one.T, order, pairs)
+    kept_m, given_m = ordered(mixed.T, low_order, pairs // 2)
     by_row = jnp.concatenate([gate_grad, small_grad.T, jnp.zeros((half, head_w - SUBS), F32)], axis=1)
-    kept = jnp.concatenate(blocks_of(by_row, low_order, pairs // 2), axis=0)
-    given = jnp.concatenate(blocks_of(by_row, [m ^ core for m in low_order], pairs // 2), axis=0).astype(BF16)
-    rest = to_rows_owner(kept, given)
+    kept_g, given_g = ordered(by_row, low_order, pairs // 2)
+    gains = jnp.pad(jnp.stack([gain_one_grad, gain_two_grad], axis=1), ((0, 0), (0, 126)))
+    kept_n, given_n = ordered(gains, order, pairs)
+    if direct:
+        proj_owned, out_owned, rest, gains = scatter_grads(
+            (spans, seqs), kept_d, given_d, kept_m, given_m, x_grad, y_grad, branch_low, kept_g, given_g, kept_n, given_n
+        )
+    else:
+        proj_owned = jnp.concatenate(
+            [in_order(*to_columns_owner(nn(kept_d, g), nn(given_d, g, BF16)), 1) for g in (x_grad, y_grad)], axis=1
+        )
+        out_owned = to_rows_owner(nn(kept_m, branch_low), nn(given_m, branch_low, BF16))
+        rest = to_rows_owner(kept_g, given_g.astype(BF16))
+        gains = sum(to_columns_owner(kept_n, given_n.astype(BF16)))
     gate_owned, small_owned = rest[:, : 2 * head_w], rest[:, 2 * head_w : 2 * head_w + SUBS]
-
-    gains = jnp.pad(jnp.stack([gain_one_grad, gain_two_grad], axis=1), ((0, 0), (0, 126)))
-    kept = jnp.concatenate(blocks_of(gains, order, pairs), axis=0)
-    given = jnp.concatenate(blocks_of(gains, [m ^ core for m in order], pairs), axis=0)
-    gains = sum(to_columns_owner(kept, given))
 
     return (
         output,

time: 1270 us -> 1070 us (0.84)
  waiting for transfers between devices: 709 us -> 299 us
  Pallas kernels: 18.1 us -> 373 us
  blocking collectives: 66.1 us -> 0 us
  starting transfers between devices: 112 us -> 82.5 us
  local copies, waits for them, and re-layouts: 140 us -> 117 us
  matrix products: 147 us -> 127 us
    ppermute x106 -> x42, waiting for transfers between devices: 672 us -> 273 us  [swap(): return lax.ppermute(value, AXES, [(i, i ^ mask) for i in range(count)])]
    pallas_call x0 -> x2, Pallas kernels: none -> 355 us  [the longest x1 207 us: scatter_grads(): pl.pallas_call(functools.partial(scatter_kernel, sizes, share), in_specs=...]
    all_gather x1 -> x0, blocking collectives: 66.1 us -> none  [on_device(): small = lax.all_gather(small, AXES, axis=0, tiled=True).astype(F32).T]
    dynamic_update_slice x30 -> x0, local copies, waits for them, and re-layouts: 31.7 us -> none  [gathered_rows(): buffer = lax.dynamic_update_slice_in_dim(buffer, piece, place(me ^ m), 0)]
    ppermute x106 -> x42, starting transfers between devices: 106 us -> 76.4 us  [swap(): return lax.ppermute(value, AXES, [(i, i ^ mask) for i in range(count)])]
    unnamed x329 -> x277, local copies, waits for them, and re-layouts: 41.2 us -> 62.5 us
    dot_general x24 -> x18, matrix products: 147 us -> 127 us  [dot(): lax.dot_general(a, b, ((dims[0], dims[1]), ((), ())), preferred_element_t...]
  transfers between devices with their start and end apart: 113 -> 47, of which waited for: 48 -> 21; matrix products, arithmetic and copies ran while one was open for 23% -> 21% of each run, Pallas kernels for 1% -> 21%
where the time goes in v2:
time: 1070 us; the launch traced here: 1050 us
  Pallas kernels  373 us (35%)
  waiting for transfers between devices  299 us (28%)
  matrix products  127 us (12%)
  local copies, waits for them, and re-layouts  117 us (11%)
  starting transfers between devices  82.5 us (8%)
  other arithmetic  37.6 us (4%)
  between operations  16.6 us (2%)
    ppermute x42, waiting for transfers between devices, swap(): return lax.ppermute(value, AXES, [(i, i ^ mask) for i in range(count)])  273 us
    pallas_call x1, Pallas kernels, scatter_grads(): pl.pallas_call(functools.partial(scatter_kernel, sizes, share), in_specs=...  207 us
    pallas_call x1, Pallas kernels, gather_weights(): pl.pallas_call(functools.partial(gather_kernel, sizes, share, half), in_s...  148 us
    dot_general x18, matrix products, dot(): lax.dot_general(a, b, ((dims[0], dims[1]), ((), ())), preferred_element_t...  127 us
    ppermute x42, starting transfers between devices, swap(): return lax.ppermute(value, AXES, [(i, i ^ mask) for i in range(count)])  76.4 us
    unnamed x277, local copies, waits for them, and re-layouts  62.5 us
  transfers between devices with their start and end apart: 47, of which 21 were waited for; matrix products, arithmetic and copies ran while one was open for 21% of the time, Pallas kernels for 21%

profile of v2, /device:TPU:8, one launch (start us, length us, event | category | flops | bytes accessed | tf_op | source)
XLA Modules:
  0.0 1052.6 jit_solution(16454917049817028501)
XLA Ops:
  14.6 148.4 %shard_map.228 = (bf16[2560,1280]{1,0:T(8,128)(2,1)}, bf16[2560,1280]{1,0:T(8,128)(2,1)}, bf16[1280,2560]{1,0:T(8,128)(2,1)}, bf16[1280,512]{1,0:T(8,128)(2,1)},...) custom-call(bf16[80,5120]{1,0:T(8,128)(2,1)} %rec_proj.1, ...), custom_call_target="tpu_custom_call", output_to_operand_aliasing={{5}: (4, {}), {6}: (5, {}), {7}: (6, {})} | custom-call | tf_op jit(solution)/shard_map/pallas_call | solution.py:473
  182.0 15.0 %collective-permute-done.1 = bf16[2,3,2560]{2,1,0:T(4,128)(2,1)S(1)} collective-permute-done((bf16[2,3,2560]{2,1,0:T(4,128)(2,1)S(1)}, bf16[2,3,2560]{2,1,0:T(4,128)(2,1)S(1)}, u32[]{:S(2)}, u32[]{:S(2)}) %collective-permute-start.1) | collective-permute-done | bytes 30752 | tf_op jit(solution)/shard_map/ppermute | solution.py:729
  200.8 15.6 %collective-permute-start.8 = (bf16[1920,640]{1,0:T(8,128)(2,1)}, bf16[1920,640]{1,0:T(8,128)(2,1)}, u32[]{:S(2)}, u32[]{:S(2)}) collective-permute-start(bf16[1920,640]{1,0:T(8,128)(2,1)} %get-tuple-element.62), channel_id=1, source_target_pairs={{0,16},{1,17},{2,18},{3,19},{4,20},{5,21},{6,22},{7,23},{8,24},{9,... | collective-permute-start | bytes 7372808 | tf_op jit(solution)/shard_map/ppermute | solution.py:20
  266.4 18.2 %collective-permute-done.11 = bf16[960,640]{1,0:T(8,128)(2,1)} collective-permute-done((bf16[960,640]{1,0:T(8,128)(2,1)S(1)}, bf16[960,640]{1,0:T(8,128)(2,1)}, u32[]{:S(2)}, u32[]{:S(2)}) %collective-permute-start.11) | collective-permute-done | bytes 1228832 | tf_op jit(solution)/shard_map/ppermute | solution.py:20
  332.6 7.6 collective-permute-start.4
  340.2 12.0 %collective-permute-start.5 = (bf16[128,2560]{1,0:T(8,128)(2,1)}, bf16[128,2560]{1,0:T(8,128)(2,1)}, u32[]{:S(2)}, u32[]{:S(2)}) collective-permute-start(bf16[128,2560]{1,0:T(8,128)(2,1)} %get-tuple-element.206), channel_id=1, source_target_pairs={{0,4},{1,5},{2,6},{3,7},{4,0},{5,1},{6,2},{7,3},{8,12},{9,13},{10,... | collective-permute-start | bytes 1966088 | tf_op jit(solution)/shard_map/ppermute | solution.py:20
  357.2 11.1 %collective-permute-done.4 = bf16[128,2560]{1,0:T(8,128)(2,1)} collective-permute-done((bf16[128,2560]{1,0:T(8,128)(2,1)}, bf16[128,2560]{1,0:T(8,128)(2,1)}, u32[]{:S(2)}, u32[]{:S(2)}) %collective-permute-start.4) | collective-permute-done | bytes 655392 | tf_op jit(solution)/shard_map/ppermute | solution.py:20
  369.3 26.0 %collective-permute-done.5 = bf16[128,2560]{1,0:T(8,128)(2,1)} collective-permute-done((bf16[128,2560]{1,0:T(8,128)(2,1)}, bf16[128,2560]{1,0:T(8,128)(2,1)}, u32[]{:S(2)}, u32[]{:S(2)}) %collective-permute-start.5) | collective-permute-done | bytes 655392 | tf_op jit(solution)/shard_map/ppermute | solution.py:20
  396.2 11.9 %collective-permute-done.6 = bf16[128,2560]{1,0:T(8,128)(2,1)} collective-permute-done((bf16[128,2560]{1,0:T(8,128)(2,1)}, bf16[128,2560]{1,0:T(8,128)(2,1)}, u32[]{:S(2)}, u32[]{:S(2)}) %collective-permute-start.6) | collective-permute-done | bytes 655392 | tf_op jit(solution)/shard_map/ppermute | solution.py:20
  419.2 14.9 %fusion.3 = f32[512,1920]{1,0:T(8,128)} fusion(bf16[1920,2560]{1,0:T(8,128)(2,1)} %constant_dynamic-update-slice_fusion, bf16[128,2560]{1,0:T(8,128)(2,1)} %collective-permute-done.6, bf16[128,2560]{1,0:T(8,128)(2,1)} %collective-permute-done.5, bf16[128,2560]{1,0:T(8,128)(2,1)} %collective-permute-done.4, bf16[128,640]{1,0:T(8,128)(2,1)S(1)} %copy-done.61, ...), kind=kOutput, calls=%fused_computation.23 | convolution fusion | flops 5051514880 | bytes 16384000 | tf_op jit(solution)/shard_map/dot_general | solution.py:24
  434.1 8.0 fusion.95
  442.8 9.0 fusion.184
  454.7 10.5 fusion.17
  465.2 9.2 fusion.96
  489.5 9.9 convolution_convert_fusion.2
  503.8 12.5 %collective-permute-done.20 = bf16[128,2560]{1,0:T(8,128)(2,1)S(1)} collective-permute-done((bf16[128,2560]{1,0:T(8,128)(2,1)S(1)}, bf16[128,2560]{1,0:T(8,128)(2,1)S(1)}, u32[]{:S(2)}, u32[]{:S(2)}) %collective-permute-start.20) | collective-permute-done | bytes 655392 | tf_op jit(solution)/shard_map/ppermute | solution.py:20
  517.9 12.5 %collective-permute-done.22 = bf16[128,2560]{1,0:T(8,128)(2,1)S(1)} collective-permute-done((bf16[128,2560]{1,0:T(8,128)(2,1)S(1)}, bf16[128,2560]{1,0:T(8,128)(2,1)S(1)}, u32[]{:S(2)}, u32[]{:S(2)}) %collective-permute-start.22) | collective-permute-done | bytes 655392 | tf_op jit(solution)/shard_map/ppermute | solution.py:20
  532.5 25.9 %collective-permute-done.32 = bf16[128,2560]{1,0:T(8,128)(2,1)S(1)} collective-permute-done((bf16[128,2560]{1,0:T(8,128)(2,1)S(1)}, bf16[128,2560]{1,0:T(8,128)(2,1)S(1)}, u32[]{:S(2)}, u32[]{:S(2)}) %collective-permute-start.32) | collective-permute-done | bytes 655392 | tf_op jit(solution)/shard_map/ppermute | solution.py:20
  558.5 14.0 %collective-permute-done.34 = bf16[128,2560]{1,0:T(8,128)(2,1)S(1)} collective-permute-done((bf16[128,2560]{1,0:T(8,128)(2,1)S(1)}, bf16[128,2560]{1,0:T(8,128)(2,1)S(1)}, u32[]{:S(2)}, u32[]{:S(2)}) %collective-permute-start.34) | collective-permute-done | bytes 655392 | tf_op jit(solution)/shard_map/ppermute | solution.py:20
  572.5 13.7 %collective-permute-done.36 = bf16[128,2560]{1,0:T(8,128)(2,1)S(1)} collective-permute-done((bf16[128,2560]{1,0:T(8,128)(2,1)S(1)}, bf16[128,2560]{1,0:T(8,128)(2,1)S(1)}, u32[]{:S(2)}, u32[]{:S(2)}) %collective-permute-start.36) | collective-permute-done | bytes 655392 | tf_op jit(solution)/shard_map/ppermute | solution.py:20
  590.8 25.0 %collective-permute-done.21 = bf16[128,2560]{1,0:T(8,128)(2,1)S(1)} collective-permute-done((bf16[128,2560]{1,0:T(8,128)(2,1)S(1)}, bf16[128,2560]{1,0:T(8,128)(2,1)S(1)}, u32[]{:S(2)}, u32[]{:S(2)}) %collective-permute-start.21) | collective-permute-done | bytes 655392 | tf_op jit(solution)/shard_map/ppermute | solution.py:20
  619.2 41.1 %collective-permute-done.23 = bf16[128,2560]{1,0:T(8,128)(2,1)S(1)} collective-permute-done((bf16[128,2560]{1,0:T(8,128)(2,1)S(1)}, bf16[128,2560]{1,0:T(8,128)(2,1)S(1)}, u32[]{:S(2)}, u32[]{:S(2)}) %collective-permute-start.23) | collective-permute-done | bytes 655392 | tf_op jit(solution)/shard_map/ppermute | solution.py:20
  661.0 11.0 %collective-permute-done.35 = bf16[128,2560]{1,0:T(8,128)(2,1)S(1)} collective-permute-done((bf16[128,2560]{1,0:T(8,128)(2,1)S(1)}, bf16[128,2560]{1,0:T(8,128)(2,1)S(1)}, u32[]{:S(2)}, u32[]{:S(2)}) %collective-permute-start.35) | collective-permute-done | bytes 655392 | tf_op jit(solution)/shard_map/ppermute | solution.py:20
  672.0 15.6 %collective-permute-done.37 = bf16[128,2560]{1,0:T(8,128)(2,1)S(1)} collective-permute-done((bf16[128,2560]{1,0:T(8,128)(2,1)S(1)}, bf16[128,2560]{1,0:T(8,128)(2,1)S(1)}, u32[]{:S(2)}, u32[]{:S(2)}) %collective-permute-start.37) | collective-permute-done | bytes 655392 | tf_op jit(solution)/shard_map/ppermute | solution.py:20
  695.0 11.8 %collective-permute-done.38 = bf16[128,2560]{1,0:T(8,128)(2,1)S(1)} collective-permute-done((bf16[128,2560]{1,0:T(8,128)(2,1)S(1)}, bf16[128,2560]{1,0:T(8,128)(2,1)S(1)}, u32[]{:S(2)}, u32[]{:S(2)}) %collective-permute-start.38) | collective-permute-done | bytes 655392 | tf_op jit(solution)/shard_map/ppermute | solution.py:20
  726.7 7.0 convolution_convert_fusion
  739.5 6.8 fusion.185
  746.3 7.8 collective-permute-done.44
  757.2 11.4 %all-gather.7.cloned.1.call-done = f32[256,1280]{1,0:T(8,128)} async-done(((f32[8,1280]{1,0:T(8,128)}), f32[256,1280]{1,0:T(8,128)}) %all-gather.7.cloned.1.call-update) | async-done | bytes 1310736 | tf_op jit(solution)/shard_map/all_gather | solution.py:750
  772.6 7.8 shard_map.231
  798.7 7.8 convert_add_fusion
  816.2 206.7 %shard_map.232 = (f32[80,5120]{1,0:T(8,128)}, f32[80,2560]{1,0:T(8,128)}, f32[80,768]{1,0:T(8,128)}, f32[80,128]{1,0:T(8,128)}) custom-call(bf16[1280,256]{1,0:T(8,128)(2,1)} %copy.177.kept_d, bf16[1280,256]{1,0:T(8,128)(2,1)} %copy.178.given_d, bf16[640,256]{1,0:T(8,128)(2,1)} %copy.179.kept_m, bf16[640,256]{1,0:T(8,128)(2,1)} %copy.180.given_m, ...), custom_call_target="tpu_custom_call" | custom-call | tf_op jit(solution)/shard_map/pallas_call | solution.py:628
  (491 shorter events, 270.0 us)
Async XLA Ops:
  7.2 295.1 %all-gather.5.cloned.1.call-start = ((), (), s32[]{:S(2)}) async-start(), calls=%async_computation | async-start | bytes 1351680 | tf_op jit(solution)/shard_map/all_gather | solution.py:750
  163.1 79.7 %collective-permute-start.24 = (bf16[128,2560]{1,0:T(8,128)(2,1)}, bf16[128,2560]{1,0:T(8,128)(2,1)}, u32[]{:S(2)}, u32[]{:S(2)}) collective-permute-start(bf16[128,2560]{1,0:T(8,128)(2,1)} %get-tuple-element.64), channel_id=1, source_target_pairs={{0,2},{1,3},{2,0},{3,1},{4,6},{5,7},{6,4},{7,5},{8,10},{9,11},{10,... | collective-permute-start | bytes 1966088 | tf_op jit(solution)/shard_map/ppermute | solution.py:20
  163.1 81.7 %collective-permute-start.25 = (bf16[128,2560]{1,0:T(8,128)(2,1)}, bf16[128,2560]{1,0:T(8,128)(2,1)}, u32[]{:S(2)}, u32[]{:S(2)}) collective-permute-start(bf16[128,2560]{1,0:T(8,128)(2,1)} %get-tuple-element.64), channel_id=1, source_target_pairs={{0,4},{1,5},{2,6},{3,7},{4,0},{5,1},{6,2},{7,3},{8,12},{9,13},{10,... | collective-permute-start | bytes 1966088 | tf_op jit(solution)/shard_map/ppermute | solution.py:20
  197.1 49.8 %collective-permute-start.26 = (bf16[128,2560]{1,0:T(8,128)(2,1)}, bf16[128,2560]{1,0:T(8,128)(2,1)}, u32[]{:S(2)}, u32[]{:S(2)}) collective-permute-start(bf16[128,2560]{1,0:T(8,128)(2,1)} %get-tuple-element.64), channel_id=1, source_target_pairs={{0,6},{1,7},{2,4},{3,5},{4,2},{5,3},{6,0},{7,1},{8,14},{9,15},{10,... | collective-permute-start | bytes 1966088 | tf_op jit(solution)/shard_map/ppermute | solution.py:20
  200.0 50.9 %collective-permute-start.27 = (bf16[128,2560]{1,0:T(8,128)(2,1)}, bf16[128,2560]{1,0:T(8,128)(2,1)}, u32[]{:S(2)}, u32[]{:S(2)}) collective-permute-start(bf16[128,2560]{1,0:T(8,128)(2,1)} %get-tuple-element.64), channel_id=1, source_target_pairs={{0,1},{1,0},{2,3},{3,2},{4,5},{5,4},{6,7},{7,6},{8,9},{9,8},{10,11... | collective-permute-start | bytes 1966088 | tf_op jit(solution)/shard_map/ppermute | solution.py:20
  200.8 101.4 %collective-permute-start.8 = (bf16[1920,640]{1,0:T(8,128)(2,1)}, bf16[1920,640]{1,0:T(8,128)(2,1)}, u32[]{:S(2)}, u32[]{:S(2)}) collective-permute-start(bf16[1920,640]{1,0:T(8,128)(2,1)} %get-tuple-element.62), channel_id=1, source_target_pairs={{0,16},{1,17},{2,18},{3,19},{4,20},{5,21},{6,22},{7,23},{8,24},{9,... | collective-permute-start | bytes 7372808 | tf_op jit(solution)/shard_map/ppermute | solution.py:20
  235.1 533.4 %all-gather.7.cloned.1.call-start = ((), (), s32[]{:S(2)}) async-start(), calls=%async_computation.1 | async-start | bytes 1351680 | tf_op jit(solution)/shard_map/all_gather | solution.py:750
  244.8 39.8 %collective-permute-start.11 = (bf16[960,640]{1,0:T(8,128)(2,1)S(1)}, bf16[960,640]{1,0:T(8,128)(2,1)}, u32[]{:S(2)}, u32[]{:S(2)}) collective-permute-start(bf16[960,640]{1,0:T(8,128)(2,1)S(1)} %copy-done.17), channel_id=1, source_target_pairs={{0,16},{1,17},{2,18},{3,19},{4,20},{5,21},{6,22},{7,23},{8,24},{9,... | collective-permute-start | bytes 3686408 | tf_op jit(solution)/shard_map/ppermute | solution.py:20
  246.9 41.9 %collective-permute-start.28 = (bf16[128,2560]{1,0:T(8,128)(2,1)}, bf16[128,2560]{1,0:T(8,128)(2,1)}, u32[]{:S(2)}, u32[]{:S(2)}) collective-permute-start(bf16[128,2560]{1,0:T(8,128)(2,1)} %collective-permute-done.24), channel_id=1, source_target_pairs={{0,1},{1,0},{2,3},{3,2},{4,5},{5,4},{6,7},{7,6},{8,9},{9,8},{10,11... | collective-permute-start | bytes 1966088 | tf_op jit(solution)/shard_map/ppermute | solution.py:20
  250.9 39.9 %collective-permute-start.29 = (bf16[128,2560]{1,0:T(8,128)(2,1)}, bf16[128,2560]{1,0:T(8,128)(2,1)}, u32[]{:S(2)}, u32[]{:S(2)}) collective-permute-start(bf16[128,2560]{1,0:T(8,128)(2,1)} %collective-permute-done.25), channel_id=1, source_target_pairs={{0,1},{1,0},{2,3},{3,2},{4,5},{5,4},{6,7},{7,6},{8,9},{9,8},{10,11... | collective-permute-start | bytes 1966088 | tf_op jit(solution)/shard_map/ppermute | solution.py:20
  263.7 54.2 %collective-permute-start.7 = (bf16[1920,640]{1,0:T(8,128)(2,1)}, bf16[1920,640]{1,0:T(8,128)(2,1)}, u32[]{:S(2)}, u32[]{:S(2)}) collective-permute-start(bf16[1920,640]{1,0:T(8,128)(2,1)} %get-tuple-element.62), channel_id=1, source_target_pairs={{0,8},{1,9},{2,10},{3,11},{4,12},{5,13},{6,14},{7,15},{8,0},{9,1},... | collective-permute-start | bytes 7372808 | tf_op jit(solution)/shard_map/ppermute | solution.py:20
  302.2 113.2 %collective-permute-start.9 = (bf16[1920,640]{1,0:T(8,128)(2,1)}, bf16[1920,640]{1,0:T(8,128)(2,1)}, u32[]{:S(2)}, u32[]{:S(2)}) collective-permute-start(bf16[1920,640]{1,0:T(8,128)(2,1)} %collective-permute-done.8), channel_id=1, source_target_pairs={{0,8},{1,9},{2,10},{3,11},{4,12},{5,13},{6,14},{7,15},{8,0},{9,1},... | collective-permute-start | bytes 7372808 | tf_op jit(solution)/shard_map/ppermute | solution.py:20
  332.6 35.7 %collective-permute-start.4 = (bf16[128,2560]{1,0:T(8,128)(2,1)}, bf16[128,2560]{1,0:T(8,128)(2,1)}, u32[]{:S(2)}, u32[]{:S(2)}) collective-permute-start(bf16[128,2560]{1,0:T(8,128)(2,1)} %get-tuple-element.206), channel_id=1, source_target_pairs={{0,2},{1,3},{2,0},{3,1},{4,6},{5,7},{6,4},{7,5},{8,10},{9,11},{10,... | collective-permute-start | bytes 1966088 | tf_op jit(solution)/shard_map/ppermute | solution.py:20
  340.2 55.2 %collective-permute-start.5 = (bf16[128,2560]{1,0:T(8,128)(2,1)}, bf16[128,2560]{1,0:T(8,128)(2,1)}, u32[]{:S(2)}, u32[]{:S(2)}) collective-permute-start(bf16[128,2560]{1,0:T(8,128)(2,1)} %get-tuple-element.206), channel_id=1, source_target_pairs={{0,4},{1,5},{2,6},{3,7},{4,0},{5,1},{6,2},{7,3},{8,12},{9,13},{10,... | collective-permute-start | bytes 1966088 | tf_op jit(solution)/shard_map/ppermute | solution.py:20
  352.2 55.9 %collective-permute-start.6 = (bf16[128,2560]{1,0:T(8,128)(2,1)}, bf16[128,2560]{1,0:T(8,128)(2,1)}, u32[]{:S(2)}, u32[]{:S(2)}) collective-permute-start(bf16[128,2560]{1,0:T(8,128)(2,1)} %get-tuple-element.206), channel_id=1, source_target_pairs={{0,6},{1,7},{2,4},{3,5},{4,2},{5,3},{6,0},{7,1},{8,14},{9,15},{10,... | collective-permute-start | bytes 1966088 | tf_op jit(solution)/shard_map/ppermute | solution.py:20
  356.6 57.9 %collective-permute-start.13 = (bf16[128,2560]{1,0:T(8,128)(2,1)}, bf16[128,2560]{1,0:T(8,128)(2,1)S(1)}, u32[]{:S(2)}, u32[]{:S(2)}) collective-permute-start(bf16[128,2560]{1,0:T(8,128)(2,1)} %get-tuple-element.206), channel_id=1, source_target_pairs={{0,1},{1,0},{2,3},{3,2},{4,5},{5,4},{6,7},{7,6},{8,9},{9,8},{10,11... | collective-permute-start | bytes 1966088 | tf_op jit(solution)/shard_map/ppermute | solution.py:20
  368.3 86.4 %collective-permute-start.14 = (bf16[128,2560]{1,0:T(8,128)(2,1)}, bf16[128,2560]{1,0:T(8,128)(2,1)S(1)}, u32[]{:S(2)}, u32[]{:S(2)}) collective-permute-start(bf16[128,2560]{1,0:T(8,128)(2,1)} %collective-permute-done.4), channel_id=1, source_target_pairs={{0,1},{1,0},{2,3},{3,2},{4,5},{5,4},{6,7},{7,6},{8,9},{9,8},{10,11... | collective-permute-start | bytes 1966088 | tf_op jit(solution)/shard_map/ppermute | solution.py:20
  395.4 59.3 %collective-permute-start.15 = (bf16[128,2560]{1,0:T(8,128)(2,1)}, bf16[128,2560]{1,0:T(8,128)(2,1)S(1)}, u32[]{:S(2)}, u32[]{:S(2)}) collective-permute-start(bf16[128,2560]{1,0:T(8,128)(2,1)} %collective-permute-done.5), channel_id=1, source_target_pairs={{0,1},{1,0},{2,3},{3,2},{4,5},{5,4},{6,7},{7,6},{8,9},{9,8},{10,11... | collective-permute-start | bytes 1966088 | tf_op jit(solution)/shard_map/ppermute | solution.py:20
  408.1 46.7 %collective-permute-start.16 = (bf16[128,2560]{1,0:T(8,128)(2,1)}, bf16[128,2560]{1,0:T(8,128)(2,1)S(1)}, u32[]{:S(2)}, u32[]{:S(2)}) collective-permute-start(bf16[128,2560]{1,0:T(8,128)(2,1)} %collective-permute-done.6), channel_id=1, source_target_pairs={{0,1},{1,0},{2,3},{3,2},{4,5},{5,4},{6,7},{7,6},{8,9},{9,8},{10,11... | collective-permute-start | bytes 1966088 | tf_op jit(solution)/shard_map/ppermute | solution.py:20
  484.5 231.0 %collective-permute-start.43 = (bf16[960,1280]{1,0:T(8,128)(2,1)}, bf16[960,1280]{1,0:T(8,128)(2,1)}, u32[]{:S(2)}, u32[]{:S(2)}) collective-permute-start(bf16[960,1280]{1,0:T(8,128)(2,1)} %convolution_convert_fusion.3), channel_id=1, source_target_pairs={{0,8},{1,9},{2,10},{3,11},{4,12},{5,13},{6,14},{7,15},{8,0},{9,1},... | collective-permute-start | bytes 7372808 | tf_op jit(solution)/shard_map/ppermute | solution.py:20
  486.8 43.6 %collective-permute-start.22 = (bf16[128,2560]{1,0:T(8,128)(2,1)S(1)}, bf16[128,2560]{1,0:T(8,128)(2,1)S(1)}, u32[]{:S(2)}, u32[]{:S(2)}) collective-permute-start(bf16[128,2560]{1,0:T(8,128)(2,1)S(1)} %get-tuple-element.169), channel_id=1, source_target_pairs={{0,1},{1,0},{2,3},{3,2},{4,5},{5,4},{6,7},{7,6},{8,9},{9,8},{10,11... | collective-permute-start | bytes 1966088 | tf_op jit(solution)/shard_map/ppermute | solution.py:20
  488.3 101.0 %collective-permute-start.17 = (bf16[128,2560]{1,0:T(8,128)(2,1)S(1)}, bf16[128,2560]{1,0:T(8,128)(2,1)S(1)}, u32[]{:S(2)}, u32[]{:S(2)}) collective-permute-start(bf16[128,2560]{1,0:T(8,128)(2,1)S(1)} %get-tuple-element.168), channel_id=1, source_target_pairs={{0,1},{1,0},{2,3},{3,2},{4,5},{5,4},{6,7},{7,6},{8,9},{9,8},{10,11... | collective-permute-start | bytes 1966088 | tf_op jit(solution)/shard_map/ppermute | solution.py:20
  502.3 56.2 %collective-permute-start.32 = (bf16[128,2560]{1,0:T(8,128)(2,1)S(1)}, bf16[128,2560]{1,0:T(8,128)(2,1)S(1)}, u32[]{:S(2)}, u32[]{:S(2)}) collective-permute-start(bf16[128,2560]{1,0:T(8,128)(2,1)S(1)} %get-tuple-element.167), channel_id=1, source_target_pairs={{0,1},{1,0},{2,3},{3,2},{4,5},{5,4},{6,7},{7,6},{8,9},{9,8},{10,11... | collective-permute-start | bytes 1966088 | tf_op jit(solution)/shard_map/ppermute | solution.py:20
  516.3 56.2 %collective-permute-start.34 = (bf16[128,2560]{1,0:T(8,128)(2,1)S(1)}, bf16[128,2560]{1,0:T(8,128)(2,1)S(1)}, u32[]{:S(2)}, u32[]{:S(2)}) collective-permute-start(bf16[128,2560]{1,0:T(8,128)(2,1)S(1)} %get-tuple-element.166), channel_id=1, source_target_pairs={{0,1},{1,0},{2,3},{3,2},{4,5},{5,4},{6,7},{7,6},{8,9},{9,8},{10,11... | collective-permute-start | bytes 1966088 | tf_op jit(solution)/shard_map/ppermute | solution.py:20
  530.4 55.8 %collective-permute-start.36 = (bf16[128,2560]{1,0:T(8,128)(2,1)S(1)}, bf16[128,2560]{1,0:T(8,128)(2,1)S(1)}, u32[]{:S(2)}, u32[]{:S(2)}) collective-permute-start(bf16[128,2560]{1,0:T(8,128)(2,1)S(1)} %get-tuple-element.165), channel_id=1, source_target_pairs={{0,1},{1,0},{2,3},{3,2},{4,5},{5,4},{6,7},{7,6},{8,9},{9,8},{10,11... | collective-permute-start | bytes 1966088 | tf_op jit(solution)/shard_map/ppermute | solution.py:20
  572.5 43.3 %collective-permute-start.21 = (bf16[128,2560]{1,0:T(8,128)(2,1)S(1)}, bf16[128,2560]{1,0:T(8,128)(2,1)S(1)}, u32[]{:S(2)}, u32[]{:S(2)}) collective-permute-start(bf16[128,2560]{1,0:T(8,128)(2,1)S(1)} %get-tuple-element.151), channel_id=1, source_target_pairs={{0,4},{1,5},{2,6},{3,7},{4,0},{5,1},{6,2},{7,3},{8,12},{9,13},{10,... | collective-permute-start | bytes 1966088 | tf_op jit(solution)/shard_map/ppermute | solution.py:20
  586.2 74.2 %collective-permute-start.23 = (bf16[128,2560]{1,0:T(8,128)(2,1)S(1)}, bf16[128,2560]{1,0:T(8,128)(2,1)S(1)}, u32[]{:S(2)}, u32[]{:S(2)}) collective-permute-start(bf16[128,2560]{1,0:T(8,128)(2,1)S(1)} %get-tuple-element.150), channel_id=1, source_target_pairs={{0,6},{1,7},{2,4},{3,5},{4,2},{5,3},{6,0},{7,1},{8,14},{9,15},{10,... | collective-permute-start | bytes 1966088 | tf_op jit(solution)/shard_map/ppermute | solution.py:20
  589.3 71.7 %collective-permute-start.31 = (bf16[128,2560]{1,0:T(8,128)(2,1)S(1)}, bf16[128,2560]{1,0:T(8,128)(2,1)S(1)}, u32[]{:S(2)}, u32[]{:S(2)}) collective-permute-start(bf16[128,2560]{1,0:T(8,128)(2,1)S(1)} %get-tuple-element.164), channel_id=1, source_target_pairs={{0,1},{1,0},{2,3},{3,2},{4,5},{5,4},{6,7},{7,6},{8,9},{9,8},{10,11... | collective-permute-start | bytes 1966088 | tf_op jit(solution)/shard_map/ppermute | solution.py:20
  590.8 70.2 %collective-permute-start.33 = (bf16[128,2560]{1,0:T(8,128)(2,1)S(1)}, bf16[128,2560]{1,0:T(8,128)(2,1)S(1)}, u32[]{:S(2)}, u32[]{:S(2)}) collective-permute-start(bf16[128,2560]{1,0:T(8,128)(2,1)S(1)} %get-tuple-element.146), channel_id=1, source_target_pairs={{0,2},{1,3},{2,0},{3,1},{4,6},{5,7},{6,4},{7,5},{8,10},{9,11},{10,... | collective-permute-start | bytes 1966088 | tf_op jit(solution)/shard_map/ppermute | solution.py:20
  615.8 56.2 %collective-permute-start.35 = (bf16[128,2560]{1,0:T(8,128)(2,1)S(1)}, bf16[128,2560]{1,0:T(8,128)(2,1)S(1)}, u32[]{:S(2)}, u32[]{:S(2)}) collective-permute-start(bf16[128,2560]{1,0:T(8,128)(2,1)S(1)} %get-tuple-element.148), channel_id=1, source_target_pairs={{0,4},{1,5},{2,6},{3,7},{4,0},{5,1},{6,2},{7,3},{8,12},{9,13},{10,... | collective-permute-start | bytes 1966088 | tf_op jit(solution)/shard_map/ppermute | solution.py:20
  733.7 65.0 %collective-permute-start.41 = (bf16[1920,1280]{1,0:T(8,128)(2,1)}, bf16[1920,1280]{1,0:T(8,128)(2,1)}, u32[]{:S(2)}, u32[]{:S(2)}) collective-permute-start(bf16[1920,1280]{1,0:T(8,128)(2,1)} %convolution_convert_fusion), channel_id=1, source_target_pairs={{0,8},{1,9},{2,10},{3,11},{4,12},{5,13},{6,14},{7,15},{8,0},{9,1},... | collective-permute-start | bytes 14745608 | tf_op jit(solution)/shard_map/ppermute | solution.py:20
  808.3 228.4 %collective-permute-start.42 = (bf16[1920,640]{1,0:T(8,128)(2,1)}, bf16[1920,640]{1,0:T(8,128)(2,1)}, u32[]{:S(2)}, u32[]{:S(2)}) collective-permute-start(bf16[1920,640]{1,0:T(8,128)(2,1)} %slice.708), channel_id=1, source_target_pairs={{0,16},{1,17},{2,18},{3,19},{4,20},{5,21},{6,22},{7,23},{8,24},{9,... | collective-permute-start | bytes 7372808 | tf_op jit(solution)/shard_map/ppermute | solution.py:20
  (134 other events, 2296.8 us)
Sparse Core Ops, SparseCore 0:
  235.2 54.7 all-gather.4
  715.6 52.9 all-gather.6

commit v3 on v2

--- a/solution.py
+++ b/solution.py
@@ -159,7 +159,7 @@
     carry_o[...] = jnp.where(q == 0, whole[0], whole[1])
 
 
-def adjoint_kernel(steps, quarters, grad, decay, prod, local_o, after_o, enter_o, carry_o):
+def adjoint_kernel(steps, quarters, grad, decay, flow, local_o, after_o, enter_o, carry_o):
     prods, sums = [], []
     for b in (0, 1):
         g = r = None
@@ -171,14 +171,14 @@
             local_o[rows] = a
             after_o[rows] = r
             g = decay[rows] * a
-        last = ((b + 1) * steps - 1) * SUBS
-        prods.append(prod[last : last + SUBS])
+        prods.append(flow[(2 + b) * SUBS : (3 + b) * SUBS])
         sums.append(g)
     enter, whole = scan_carries(prods, sums, quarters, True)
     for b in (0, 1):
         enter_o[b * SUBS : (b + 1) * SUBS] = enter[b][0]
         enter_o[(2 + b) * SUBS : (3 + b) * SUBS] = enter[b][1]
-    carry_o[...] = whole[1]
+    q = quarter_of(whole[0].shape, quarters)
+    carry_o[...] = jnp.where(q == 0, whole[0], whole[1])
 
 
 def backward_kernel(
@@ -302,17 +302,21 @@
             pl.semaphore_signal(barrier, inc=1, device_id=self.peer(mask), device_id_type=MESH)
         pl.semaphore_wait(barrier, len(masks))
 
-    def send(self, source, target, mask, only=None):
+    def plan(self, source, target, mask, only=None):
         slot = self.used
         self.used += 1
         copy = pltpu.make_async_remote_copy(
             source, target, self.sends.at[slot], self.recvs.at[slot], device_id=self.peer(mask), device_id_type=MESH
         )
+        self.open.append((copy, only))
+        return copy
+
+    def send(self, source, target, mask, only=None):
+        copy = self.plan(source, target, mask, only)
         if only is None:
             copy.start()
         else:
             pl.when(only)(copy.start)
-        self.open.append((copy, only))
         return copy
 
     def close(self):
@@ -635,6 +639,466 @@
     )(kept_d, given_d, kept_m, given_m, grad_x, grad_y, branch, kept_g, given_g, kept_n, given_n)
 
 
+def gelu_parts(v):
+    root = 0.7978845608028654
+    t = jnp.tanh(root * (v + 0.044715 * (v * v * v)))
+    slope = 0.5 * (1.0 + t) + 0.5 * v * (1.0 - t * t) * root * (1.0 + 3.0 * 0.044715 * (v * v))
+    return 0.5 * v * (1.0 + t), slope
+
+
+def feed_kernel(sizes, masks, own, *refs):
+    chunks = len(masks)
+    spans = sizes[0]
+    own_rows, refs = refs[0], refs[1:]
+    cots, refs = refs[: 2 * chunks], refs[2 * chunks :]
+    wides, refs = refs[:spans], refs[spans:]
+    narrows, refs = refs[:spans], refs[spans:]
+    grad_o, near_o, far_o, rows_o, cots_o, act_o, hidden_o, refs = *refs[:7], refs[7:]
+    (rows, cot, wide, narrow, act, hidden, near, down_near, down_far, to_side, from_side, to_inner, from_inner,
+     sends, recvs, loads, stores) = refs
+    units = narrow.shape[0]
+    width = narrow.shape[1]
+    size = width // spans
+    pair = 2 * own
+    links = Links(sizes, sends, recvs)
+
+    def load(source, target, slot):
+        copy = pltpu.make_async_copy(source, target, loads.at[slot])
+        copy.start()
+        return copy
+
+    first = load(own_rows, rows.at[pl.ds(0, own)], 0)
+    late = [load(cots[b], cot.at[pl.ds(b * own, own)], 1 + b) for b in range(2 * chunks)]
+    for j in range(spans):
+        columns = pl.ds(j * size, size)
+        late.append(load(wides[j], wide.at[:, columns], 1 + 2 * chunks + j))
+        late.append(load(narrows[j], narrow.at[:, columns], 1 + 2 * chunks + spans + j))
+    links.greet([1, *masks[1:]])
+    first.wait()
+
+    def block(b):
+        return rows.at[pl.ds(b * own, own)]
+
+    each = range(chunks)
+    over_side = [links.plan(block(2 * i), block(2 * i + 1), 1) for i in each]
+    over_inner = [None] + [links.plan(block(0), block(2 * i), masks[i]) for i in each[1:]]
+    back_side = [links.plan(to_side.at[i], from_side.at[i], 1) for i in each]
+    back_inner = [links.plan(to_inner.at[i - 1], from_inner.at[i - 1], masks[i]) for i in each[1:]]
+    over_side[0].start()
+    over_inner[1].start()
+    for copy in late:
+        copy.wait()
+
+    def onward(i):
+        over_inner[i].wait_recv()
+        over_side[i].start()
+        if i + 1 < chunks:
+            over_inner[i + 1].start()
+
+    def give_on(i):
+        back_side[i].wait_recv()
+        to_inner[i - 1] = (near[i].astype(F32) + from_side[i].astype(F32)).astype(BF16)
+        back_inner[i - 1].start()
+
+    def ahead(i):
+        over_side[i].wait_recv()
+        if i == 0:
+            onward(1)
+        else:
+            back_side[i - 1].start()
+
+    def behind(i):
+        if 0 < i < chunks - 1:
+            onward(i + 1)
+        if i == chunks - 1:
+            back_side[i].start()
+        if i > 1:
+            give_on(i - 1)
+
+    def compute(i):
+        here = pl.ds(pl.multiple_of(i * pair, 16), pair)
+        mine = rows[here]
+        given = cot[here]
+        start = 0
+        while start < units:
+            n = min(384, units - start)
+            gate = lax.dot_general(mine, wide[start : start + n], (((1,), (1,)), ((), ())), preferred_element_type=F32)
+            up = lax.dot_general(
+                mine, wide[units + start : units + start + n], (((1,), (1,)), ((), ())), preferred_element_type=F32
+            )
+            back = lax.dot_general(given, narrow[start : start + n], (((1,), (1,)), ((), ())), preferred_element_type=F32)
+            value, slope = gelu_parts(gate)
+            hidden[here, start : start + n] = (value * up).astype(BF16)
+            act[here, start : start + n] = (back * up * slope).astype(BF16)
+            act[here, units + start : units + start + n] = (back * value).astype(BF16)
+            start += n
+        step = 512
+
+        @pl.loop(0, width // step)
+        def _(k):
+            columns = pl.ds(pl.multiple_of(k * step, 128), step)
+            total = jnp.dot(act[here], wide[:, columns], preferred_element_type=F32)
+            near[i, :, columns] = total[:own].astype(BF16)
+            to_side[i, :, columns] = total[own:].astype(BF16)
+            total = jnp.dot(hidden[here], narrow[:, columns], preferred_element_type=F32)
+            down_near[i, :, columns] = total[:own].astype(BF16)
+            down_far[i, :, columns] = total[own:].astype(BF16)
+
+    @pl.loop(0, chunks)
+    def _(i):
+        for k in range(chunks):
+            pl.when(i == k)(functools.partial(ahead, k))
+        compute(i)
+        for k in range(chunks):
+            pl.when(i == k)(functools.partial(behind, k))
+
+    pairs = [(rows, rows_o), (cot, cots_o), (act, act_o), (hidden, hidden_o), (down_near, near_o), (down_far, far_o)]
+    out = []
+    for k, (source, target) in enumerate(pairs):
+        out.append(pltpu.make_async_copy(source, target, stores.at[k]))
+        out[-1].start()
+    give_on(chunks - 1)
+    back_side[0].wait_recv()
+    total = near[0].astype(F32) + from_side[0].astype(F32)
+    for k in range(chunks - 1):
+        back_inner[k].wait_recv()
+        total = total + from_inner[k].astype(F32)
+    grad_o[...] = total
+    for copy in out:
+        copy.wait()
+    links.close()
+
+
+def feed_forward(sizes, masks, own_rows, cots, wides, narrows):
+    own, width = own_rows.shape
+    units = narrows[0].shape[0]
+    chunks = len(masks)
+    total = 2 * chunks * own
+    anywhere = pl.BlockSpec(memory_space=pl.ANY)
+    copies = 4 * chunks
+    blocks = (chunks, own, width)
+    shapes = [blocks, blocks, (total, width), (total, width), (total, 2 * units), (total, units)]
+    held = [
+        (total, width), (total, width), (2 * units, width), (units, width), (total, 2 * units), (total, units), blocks, blocks,
+        blocks, blocks, blocks, (chunks - 1, own, width), (chunks - 1, own, width),
+    ]
+    return pl.pallas_call(
+        functools.partial(feed_kernel, sizes, masks, own),
+        in_specs=[anywhere] * (1 + 2 * chunks + 2 * len(wides)),
+        out_specs=[pl.BlockSpec(memory_space=pltpu.VMEM)] + [anywhere] * 6,
+        out_shape=[jax.ShapeDtypeStruct((own, width), F32)] + [jax.ShapeDtypeStruct(s, BF16) for s in shapes],
+        scratch_shapes=[pltpu.VMEM(s, BF16) for s in held]
+        + [pltpu.SemaphoreType.DMA((k,)) for k in (copies, copies, 1 + 2 * chunks + 2 * len(wides), 6)],
+        compiler_params=pltpu.CompilerParams(collective_id=2, has_side_effects=True, vmem_limit_bytes=VMEM_LIMIT),
+    )(own_rows, *cots, *wides, *narrows)
+
+
+def expanded(v, quarters):
+    return spread(v, quarters, 0), spread(roll(v, -1), quarters, 0)
+
+
+def chunk_inflow(links, line, blocks, quarters, backward, between):
+    n, spans = line.shape[0], blocks.shape[0]
+    place = links.seq // 2
+    copies = [links.send(line.at[0], line.at[k], 2 * k) for k in range(1, n)]
+    for copy in copies:
+        copy.wait_recv()
+    between()
+    one, nought = jnp.ones(line.shape[1:], F32), jnp.zeros(line.shape[1:], F32)
+    prod, total = one, nought
+    all_prod, all_total = one, nought
+
+    def ordered(count):
+        return range(count - 1, -1, -1) if backward else range(count)
+
+    def ahead(j, at):
+        return at < j if backward else at > j
+
+    for j in ordered(n):
+        p, s = expanded(line[links.flipped(place, j)], quarters)
+        inside = ahead(j, place)
+        total = jnp.where(inside, p * total + s, total)
+        prod = jnp.where(inside, p * prod, prod)
+        all_total = p * all_total + s
+        all_prod = p * all_prod
+    q = quarter_of(line.shape[1:], quarters)
+    blocks[0] = jnp.where(q == 0, all_prod, all_total)
+    copies = [links.send(blocks.at[0], blocks.at[m], m * links.seqs) for m in range(1, spans)]
+    for copy in copies:
+        copy.wait_recv()
+    h = nought
+    for j in ordered(spans):
+        p, s = expanded(blocks[links.flipped(links.span, j)], quarters)
+        h = jnp.where(ahead(j, links.span), p * h + s, h)
+    return prod * h + total
+
+
+def by_head(heads, head_w, body):
+    @pl.loop(0, heads)
+    def _(h):
+        start = pl.multiple_of(h * head_w, 128)
+        columns = pl.ds(start, head_w)
+        body(lambda ref: ref.at[:, columns], lambda ref: ref.at[pl.ds(start, head_w)])
+
+
+def recur_kernel(
+    sizes, steps, quarters, heads, inner, xb, chan, gate, y_pre, out_w, x_own, gain, cot, wide, narrow, *refs
+):
+    spans, seqs = sizes
+    core, tops = seqs, [2 * seqs * k for k in range(1, spans // 2)]
+    n = len(inner) + 1
+    outs, refs = refs[: 8 + 2 * (spans - 1) + 2 * n], refs[8 + 2 * (spans - 1) + 2 * n :]
+    conv, recur, inject, decay, states, flow_o, mixed, resid = outs[:8]
+    wides, narrows = outs[8 : 7 + spans], outs[7 + spans : 6 + 2 * spans]
+    cots, normal = outs[6 + 2 * spans : -1], outs[-1]
+    prod, enter, line, blocks, inflow, to_side, from_side, low, sends, recvs = refs
+    links = Links(sizes, sends, recvs)
+    side = links.seq % 2
+    own, width = x_own.shape
+    rows = 2 * own
+    masks = [1, *inner, *[m * seqs for m in range(1, spans)]]
+    links.greet(masks)
+    early = pl.ds(0, wide.shape[0] // 4)
+    later = pl.ds(wide.shape[0] // 4, wide.shape[0] - wide.shape[0] // 4)
+    across_wide = [links.send(wide.at[early], wides[m // seqs - 1].at[early], m) for m in tops]
+    beside = [links.send(wide, wides[0], core), links.send(narrow, narrows[0], core)]
+    over_inner = {m: links.plan(cot, cots[2 * k], m) for k, m in enumerate(inner)}
+    over_side = [links.send(cot, cots[2 * len(inner)], 1)]
+    head_w = gate.shape[1] // 2
+
+    def gates(cols, tall):
+        forward_kernel(
+            steps, quarters, cols(xb), cols(chan), tall(gate), cols(conv), cols(recur), cols(inject), cols(decay),
+            cols(states), cols(prod), cols(enter), cols(line.at[0]),
+        )
+
+    by_head(heads, head_w, gates)
+    inflow[...] = chunk_inflow(
+        links, line, blocks, quarters, False, lambda: [over_inner[m].start() for m in inner]
+    )
+    across_wide += [links.send(wide.at[later], wides[m // seqs - 1].at[later], m) for m in tops]
+    across_narrow = {m: links.send(narrow, narrows[m // seqs - 1], m) for m in tops}
+    block = steps * SUBS
+
+    def mix(cols, tall):
+        ins, flow, hold, gain_y = cols(inflow), cols(flow_o), cols(states), cols(y_pre)
+        for b in (0, 1):
+            entered = cols(enter)[b * SUBS : (b + 1) * SUBS] * ins[...] + cols(enter)[(2 + b) * SUBS : (3 + b) * SUBS]
+            flow[b * SUBS : (b + 1) * SUBS] = entered
+            flow[(2 + b) * SUBS : (3 + b) * SUBS] = cols(prod)[(b + 1) * block - SUBS : (b + 1) * block]
+            here = slice(b * block, (b + 1) * block)
+            total = hold[here].reshape(steps, SUBS, head_w) + cols(prod)[here].reshape(steps, SUBS, head_w) * entered[None]
+            total = total.reshape(block, head_w)
+            hold[here] = total
+            cols(mixed)[here] = (total * gelu_parts(gain_y[here])[0]).astype(BF16)
+
+    by_head(heads, head_w, mix)
+    step = 512
+
+    @pl.loop(0, width // step)
+    def _(k):
+        columns = pl.ds(pl.multiple_of(k * step, 128), step)
+        total = jnp.dot(mixed[...], out_w[:, columns], preferred_element_type=F32)
+        first = side == 0
+        resid[:, columns] = x_own[:, columns].astype(F32) + jnp.where(first, total[:own], total[own:])
+        to_side[:, columns] = jnp.where(first, total[own:], total[:own]).astype(BF16)
+
+    partial = links.send(to_side, from_side, 1)
+    partial.wait_recv()
+    few = 16
+    size = width // spans
+
+    @pl.loop(0, own // few)
+    def _(k):
+        here = pl.ds(pl.multiple_of(k * few, few), few)
+        total = resid[here] + from_side[here].astype(F32)
+        resid[here] = total
+        low[here] = normed(total, gain[...]).astype(BF16)
+
+    for j in range(spans):
+        start = pl.multiple_of(links.flipped(links.span, j) * size, 128)
+        normal[:, j * size : (j + 1) * size] = low[:, pl.ds(start, size)]
+
+    for k, m in enumerate(inner):
+        over_inner[m].wait_recv()
+        over_side.append(links.send(cots[2 * k], cots[2 * k + 1], 1))
+    for copy in across_wide:
+        copy.wait_recv()
+    for m in tops:
+        beside.append(links.send(wides[m // seqs - 1], wides[m // seqs], core))
+    for m in tops:
+        across_narrow[m].wait_recv()
+        beside.append(links.send(narrows[m // seqs - 1], narrows[m // seqs], core))
+    for copy in (*beside, *over_side):
+        copy.wait_recv()
+    links.close()
+
+
+def recurrent(sizes, steps, quarters, heads, inner, xb, chan, gate, y_pre, out_w, x_own, gain, cot, wide, narrow):
+    spans, seqs = sizes
+    half = xb.shape[1]
+    own, width = x_own.shape
+    rows = 2 * own
+    n = len(inner) + 1
+    inside, anywhere = pl.BlockSpec(memory_space=pltpu.VMEM), pl.BlockSpec(memory_space=pl.ANY)
+    full = jax.ShapeDtypeStruct((rows, half), F32)
+
+    def low(shape):
+        return jax.ShapeDtypeStruct(shape, BF16)
+
+    shapes = [
+        *[full] * 5, jax.ShapeDtypeStruct((4 * SUBS, half), F32), low((rows, half)), jax.ShapeDtypeStruct((own, width), F32),
+        *[low(wide.shape)] * (spans - 1), *[low(narrow.shape)] * (spans - 1), *[low(cot.shape)] * (2 * n - 1), low((own, width)),
+    ]
+    copies = 3 * (spans // 2) * 2 + 2 * n + 2 + (n - 1) + spans
+    end = (SUBS, half)
+    outs = pl.pallas_call(
+        functools.partial(recur_kernel, sizes, steps, quarters, heads, inner),
+        in_specs=[inside] * 7 + [anywhere] * 3,
+        out_specs=[inside] * 8 + [anywhere] * (len(shapes) - 9) + [inside],
+        out_shape=shapes,
+        scratch_shapes=[
+            pltpu.VMEM((rows, half), F32), pltpu.VMEM((4 * SUBS, half), F32), pltpu.VMEM((n, *end), F32),
+            pltpu.VMEM((spans, *end), F32), pltpu.VMEM(end, F32), *[pltpu.VMEM((own, width), BF16)] * 3,
+            pltpu.SemaphoreType.DMA((copies,)), pltpu.SemaphoreType.DMA((copies,)),
+        ],
+        compiler_params=pltpu.CompilerParams(collective_id=3, has_side_effects=True, vmem_limit_bytes=VMEM_LIMIT),
+    )(xb, chan, gate, y_pre, out_w, x_own, gain, cot, wide, narrow)
+    wides, narrows = outs[8 : 7 + spans], outs[7 + spans : 6 + 2 * spans]
+    received = outs[6 + 2 * spans : -1]
+    near, far = [cot] + [received[2 * k] for k in range(n - 1)], [received[2 * (n - 1)]] + [received[2 * k + 1] for k in range(n - 1)]
+    cots = [b for pair in zip(near, far) for b in pair]
+    return outs[:8], [wide, *wides], [narrow, *narrows], cots, outs[-1]
+
+
+def return_kernel(
+    sizes, steps, quarters, heads, inner, branch, out_w, y_pre, states, decay, flow, conv, recur, inject, xb, chan, gate,
+    near, far, wide, narrow, branch_o, y_grad, dx, spill, gate_o, small, down, wides, narrows,
+    grad, local, after, enter, carry, line, blocks, inflow, dmix, from_side, to_inner, from_inner, sends, recvs,
+):
+    spans, seqs = sizes
+    tops = [2 * seqs * k for k in range(1, spans // 2)]
+    n = len(inner) + 1
+    links = Links(sizes, sends, recvs)
+    side = links.seq % 2
+    own, width = branch.shape
+    links.greet([1, *inner, *[m * seqs for m in range(1, spans)]])
+    place = pl.ds(pl.multiple_of(side * own, 16), own)
+    whole = links.send(branch, branch_o.at[place], 1)
+    tall = wide.shape[1] // 2
+    across = [links.send(wide.at[k, pl.ds(0, tall)], wides.at[k, pl.ds(0, tall)], m) for k, m in enumerate(tops)]
+    branch_o[place] = branch[...]
+    whole.wait_recv()
+    sums = [*range(1, n), 0]
+    over_side = {}
+
+    def side_sum(i):
+        over_side[sums[i]] = links.send(far.at[sums[i]], from_side.at[sums[i]], 1)
+
+    over_inner = []
+
+    def inner_sum(i):
+        k = sums[i]
+        over_side[k].wait_recv()
+        if k:
+            to_inner[k - 1] = (near[k].astype(F32) + from_side[k].astype(F32)).astype(BF16)
+            over_inner.append(links.send(to_inner.at[k - 1], from_inner.at[k - 1], inner[k - 1]))
+
+    side_sum(0)
+    head_w = gate.shape[1] // 2
+
+    def first(cols, tall):
+        mixed_grad = lax.dot_general(branch_o[...], tall(out_w)[...], (((1,), (1,)), ((), ())), preferred_element_type=F32)
+        value, slope = gelu_parts(cols(y_pre)[...])
+        cols(grad)[...] = mixed_grad * value
+        cols(y_grad)[...] = (mixed_grad * cols(states)[...] * slope).astype(BF16)
+        adjoint_kernel(
+            steps, quarters, cols(grad), cols(decay), cols(flow), cols(local), cols(after), cols(enter), cols(line.at[0])
+        )
+
+    by_head(heads, head_w, first)
+
+    def between():
+        inner_sum(0)
+        side_sum(1)
+
+    inflow[...] = chunk_inflow(links, line, blocks, quarters, True, between)
+    for k, m in enumerate(tops):
+        across.append(links.send(wide.at[k, pl.ds(tall, tall)], wides.at[k, pl.ds(tall, tall)], m))
+        across.append(links.send(narrow.at[k], narrows.at[k], m))
+    inner_sum(1)
+    side_sum(2)
+
+    def second(cols, tall):
+        came = jnp.concatenate(
+            [
+                cols(enter)[b * SUBS : (b + 1) * SUBS] * cols(inflow)[...] + cols(enter)[(2 + b) * SUBS : (3 + b) * SUBS]
+                for b in (0, 1)
+            ],
+            axis=0,
+        )
+        backward_kernel(
+            steps, quarters, cols(local), cols(after), cols(states), came, cols(flow), cols(conv), cols(recur),
+            cols(inject), cols(decay), cols(xb), cols(chan), tall(gate), cols(dx), cols(spill), tall(gate_o), cols(small),
+        )
+
+    by_head(heads, head_w, second)
+    for i in range(2, n):
+        inner_sum(i)
+        if i + 1 < n:
+            side_sum(i + 1)
+    few = 16
+    for copy in over_inner:
+        copy.wait_recv()
+
+    @pl.loop(0, own // few)
+    def _(k):
+        here = pl.ds(pl.multiple_of(k * few, few), few)
+        total = near[0, here].astype(F32) + from_side[0, here].astype(F32)
+        for j in range(n - 1):
+            total = total + from_inner[j, here].astype(F32)
+        down[here] = total
+
+    for copy in across:
+        copy.wait_recv()
+    links.close()
+
+
+def returned(sizes, steps, quarters, heads, inner, branch, out_w, y_pre, states, decay, flow, conv, recur, inject, xb, chan, gate,
+             near, far, wide, narrow):
+    spans, _ = sizes
+    own, width = branch.shape
+    rows, half = y_pre.shape
+    n = len(inner) + 1
+    inside, anywhere = pl.BlockSpec(memory_space=pltpu.VMEM), pl.BlockSpec(memory_space=pl.ANY)
+
+    def high(*shape):
+        return jax.ShapeDtypeStruct(shape, F32)
+
+    def low(*shape):
+        return jax.ShapeDtypeStruct(shape, BF16)
+
+    shapes = [
+        low(rows, width), low(rows, half), high(rows, half), high((CONV - 1) * SUBS, half), high(*gate.shape), high(SUBS, half),
+        high(own, width), low(*wide.shape), low(*narrow.shape),
+    ]
+    end = (SUBS, half)
+    copies = 3 * (spans // 2) + 2 * n + 2 * n + spans + 1
+    return pl.pallas_call(
+        functools.partial(return_kernel, sizes, steps, quarters, heads, inner),
+        in_specs=[inside] * 14 + [anywhere] * 2,
+        out_specs=[inside] * 7 + [anywhere] * 2,
+        out_shape=shapes,
+        scratch_shapes=[
+            *[pltpu.VMEM((rows, half), F32)] * 3, pltpu.VMEM((4 * SUBS, half), F32), pltpu.VMEM(end, F32),
+            pltpu.VMEM((n, *end), F32), pltpu.VMEM((spans, *end), F32), pltpu.VMEM(end, F32), pltpu.VMEM(end, F32),
+            pltpu.VMEM((n, own, width), BF16), pltpu.VMEM((n - 1, own, width), BF16), pltpu.VMEM((n - 1, own, width), BF16),
+            pltpu.SemaphoreType.DMA((copies,)), pltpu.SemaphoreType.DMA((copies,)),
+        ],
+        compiler_params=pltpu.CompilerParams(collective_id=4, has_side_effects=True, vmem_limit_bytes=VMEM_LIMIT),
+    )(branch, out_w, y_pre, states, decay, flow, conv, recur, inject, xb, chan, gate, near, far, wide, narrow)
+
+
 def on_device(
     inputs, norm_one, rec_proj, conv_weight, conv_bias, gate_weight, gate_bias, decay_param, out_proj, norm_two,
     mlp_wide, mlp_narrow, cotangent,
@@ -736,46 +1200,22 @@
     x_branch = nn(normal_one, proj_x, BF16)
     normal_one = normal_one[:rows]
     y_pre = nn(normal_one, proj_y)
-    y_branch, gelu_back = jax.vjp(jax.nn.gelu, y_pre)
-
-    kernel = functools.partial(forward_kernel, steps, quarters)
-    full = ((rows, half), False)
-    ends = ((4 * SUBS, half), False)
-    conv, recur, inject, decay, local, prod, enter, carry = by_heads(
-        kernel, heads, head_w, [(x_branch, False), (chan, False), (gates, True)],
-        [full] * 6 + [ends, ((SUBS, half), False)],
-    )
-
-    def exchanged(carry):
-        every = lax.all_gather(carry, AXES, axis=0).reshape(pairs, 2, *carry.shape)
-        return lax.dynamic_index_in_dim(every, side, 1, keepdims=False)
-
-    carries = exchanged(carry).reshape(pairs, batch, quarters, half)
-    totals = carries[:, :, 0]
-    h = jnp.zeros((batch, half), F32)
-    for j in range(pairs - 1):
-        h = jnp.where(j < pair, totals[j] * h + carries[j, :, 1], h)
-
-    def at_subs(v):
-        return jnp.repeat(v, quarters, axis=0)
-
-    def entering(enter, h):
-        enter = enter.reshape(2, 2, SUBS, half)
-        return enter[0] * at_subs(h)[None] + enter[1]
-
-    def by_steps(v):
-        return v.reshape(2, steps, SUBS, half)
-
-    entered = entering(enter, h)
-    states = (by_steps(local) + by_steps(prod) * entered[:, None]).reshape(rows, half)
-    mixed = (states * y_branch).astype(BF16)
-
     def over_sides(partial):
         partial = partial.reshape(2, own, width)
         other = lax.dynamic_index_in_dim(partial, 1 - side, 0, keepdims=False).astype(BF16)
         return lax.dynamic_index_in_dim(partial, side, 0, keepdims=False) + swap(other, 1).astype(F32)
 
-    resid = x + over_sides(nn(mixed, out_half))
+    def exchanged(carry):
+        every = lax.all_gather(carry, AXES, axis=0).reshape(pairs, 2, batch, quarters, half)
+        every = lax.dynamic_index_in_dim(every, side, 1, keepdims=False)
+        return every[:, :, 0], every[:, :, 1]
+
+    def entering(enter, h):
+        enter = enter.reshape(2, 2, SUBS, half)
+        return enter[0] * jnp.repeat(h, quarters, axis=0)[None] + enter[1]
+
+    def by_steps(v):
+        return v.reshape(2, steps, SUBS, half)
 
     def span_gather(block):
         pieces = {0: block}
@@ -783,92 +1223,120 @@
             pieces[m] = swap(block, m)
         for n in list(pieces):
             pieces[n ^ core] = swap(pieces[n], core)
-        return jnp.concatenate([pieces[m * seqs] for m in range(spans)], axis=1)
-
-    wide = span_gather(wide_own)
-    narrow = span_gather(narrow_own)
+        return [pieces[m * seqs] for m in range(spans)]
 
     def token_gather(v):
         blocks = [v] + [swap(v, m) for m in inner]
-        others = [swap(b, 1) for b in blocks]
-        return jnp.concatenate(blocks, axis=0), jnp.concatenate(others, axis=0)
-
-    grads = token_gather(grads_own)
+        return [b for block in blocks for b in (block, swap(block, 1))]
+
     c = to_rows(cotangent).astype(F32)
-    normal_two = token_gather(by_span(normed(resid, gain_two).astype(BF16)))
-
-    def activate(values):
-        return jax.nn.gelu(values[:, :units]) * values[:, units:]
-
-    hidden, wide_back = [], []
-    for part in (0, 1):
-        value, back = jax.vjp(activate, nt(normal_two[part], wide))
-        hidden.append(value.astype(BF16))
-        wide_back.append(back(nt(grads[part], narrow))[0].astype(BF16))
-
-    def token_scatter(far, near):
-        near = near.reshape(len(inner) + 1, own, width)
-        far = far.reshape(len(inner) + 1, own, width)
-        blocks = [near[k] + swap(far[k], 1).astype(F32) for k in range(len(inner) + 1)]
-        total = blocks[0]
-        for k, m in enumerate(inner):
-            total = total + swap(blocks[k + 1].astype(BF16), m).astype(F32)
+    if direct:
+        (conv, recur, inject, decay, states, flow, mixed, resid), wides, narrows, cots, normal_two = recurrent(
+            (spans, seqs), steps, quarters, heads, inner, x_branch, chan, gates, y_pre, out_half, mine, gain_two[None],
+            grads_own, wide_own, narrow_own,
+        )
+    else:
+        y_branch, gelu_back = jax.vjp(jax.nn.gelu, y_pre)
+        kernel = functools.partial(forward_kernel, steps, quarters)
+        full = ((rows, half), False)
+        ends = ((4 * SUBS, half), False)
+        conv, recur, inject, decay, local, prod, enter, carry = by_heads(
+            kernel, heads, head_w, [(x_branch, False), (chan, False), (gates, True)],
+            [full] * 6 + [ends, ((SUBS, half), False)],
+        )
+        prods, sums = exchanged(carry)
+        h = jnp.zeros((batch, half), F32)
+        for j in range(pairs - 1):
+            h = jnp.where(j < pair, prods[j] * h + sums[j], h)
+        entered = entering(enter, h)
+        states = (by_steps(local) + by_steps(prod) * entered[:, None]).reshape(rows, half)
+        flow = jnp.concatenate([entered, by_steps(prod)[:, -1]], axis=0).reshape(4 * SUBS, half)
+        mixed = (states * y_branch).astype(BF16)
+        resid = x + over_sides(nn(mixed, out_half))
+        normal_two = by_span(normed(resid, gain_two).astype(BF16))
+        wides, narrows = span_gather(wide_own), span_gather(narrow_own)
+        cots = token_gather(grads_own)
+
+    def token_scatter(near, far):
+        total = None
+        for k, m in enumerate((0, *inner)):
+            block = near[k].astype(F32) + swap(far[k], 1).astype(F32)
+            total = block if m == 0 else total + swap(block.astype(BF16), m).astype(F32)
         return by_span(total)
 
-    normal_two_grad = token_scatter(nn(wide_back[1], wide, BF16), nn(wide_back[0], wide))
-    down = token_scatter(nn(hidden[1], narrow, BF16), nn(hidden[0], narrow))
-    output = from_rows((resid + down).astype(BF16))
-
-    def span_scatter(left, right):
-        size = width // spans
-        kept = [j for j in range(spans) if j % 2 == 0]
-        given = [j for j in range(spans) if j % 2 == 1]
-
-        def columns(js):
-            return jnp.concatenate([right[:, j * size : (j + 1) * size] for j in js], axis=1)
-
-        recv = swap(tn(left, columns(given), BF16), core)
-        total = tn(left, columns(kept)) + recv.astype(F32)
-        out = total[:, :size]
-        for k, m in enumerate(xs):
-            out = out + swap(total[:, (k + 1) * size : (k + 2) * size].astype(BF16), m).astype(F32)
-        return out
-
-    all_normal = jnp.concatenate(normal_two, axis=0)
-    all_grads = jnp.concatenate(grads, axis=0)
-    wide_owned = span_scatter(jnp.concatenate(wide_back, axis=0), all_normal)
-    wide_owned = wide_owned.reshape(2, units, width // spans).transpose(2, 0, 1)
-    narrow_owned = span_scatter(jnp.concatenate(hidden, axis=0), all_grads).T
-
+    if direct:
+        normal_two_grad, near, far, all_normal, all_grads, all_act, all_hidden = feed_forward(
+            (spans, seqs), [0, *inner], normal_two, cots, wides, narrows
+        )
+        normal_two_grad = by_span(normal_two_grad)
+    else:
+        wide, narrow = jnp.concatenate(wides, axis=1), jnp.concatenate(narrows, axis=1)
+        all_normal = jnp.concatenate(token_gather(normal_two), axis=0)
+        all_grads = jnp.concatenate(cots, axis=0)
+
+        def activate(values):
+            return jax.nn.gelu(values[:, :units]) * values[:, units:]
+
+        value, back = jax.vjp(activate, nt(all_normal, wide))
+        all_hidden = value.astype(BF16)
+        all_act = back(nt(all_grads, narrow))[0].astype(BF16)
+
+        def sided(v):
+            v = v.reshape(len(inner) + 1, 2, own, width)
+            return v[:, 0], v[:, 1]
+
+        normal_two_grad = token_scatter(*sided(nn(all_act, wide, BF16)))
+        near, far = sided(nn(all_hidden, narrow, BF16))
+    size = width // spans
+
+    def core_sum(left, right):
+        def columns(odd):
+            return jnp.concatenate([right[:, j * size : (j + 1) * size] for j in range(odd, spans, 2)], axis=1)
+
+        recv = swap(tn(left, columns(1), BF16), core)
+        total = tn(left, columns(0)) + recv.astype(F32)
+        away = [total[:, k * size : (k + 1) * size].astype(BF16) for k in range(1, spans // 2)]
+        return total[:, :size], jnp.stack(away)
+
+    wide_kept, wide_away = core_sum(all_act, all_normal)
+    narrow_kept, narrow_away = core_sum(all_hidden, all_grads)
     resid_part, gain_two_grad = norm_back(resid, gain_two, normal_two_grad)
     resid_grad = c + resid_part
     branch_low = resid_grad.astype(BF16)
-    branch_low = in_order(branch_low, swap(branch_low, 1), 0)
-    mixed_grad = nt(branch_low, out_half)
-    states_grad = mixed_grad * y_branch
-    y_grad = gelu_back(mixed_grad * states)[0].astype(BF16)
-
-    kernel = functools.partial(adjoint_kernel, steps, quarters)
-    local_adj, after, back_enter, back_carry = by_heads(
-        kernel, heads, head_w, [(states_grad, False), (decay, False), (prod, False)],
-        [full, full, ends, ((SUBS, half), False)],
-    )
-    back_carries = exchanged(back_carry).reshape(pairs, batch, quarters, half)[:, :, 0]
-    h = jnp.zeros((batch, half), F32)
-    for j in range(pairs - 1, 0, -1):
-        h = jnp.where(j > pair, totals[j] * h + back_carries[j], h)
-    came = entering(back_enter, h)
-    kernel = functools.partial(backward_kernel, steps, quarters)
-    flat = (2 * SUBS, half)
-    dx, spill, gate_grad, small_grad = by_heads(
-        kernel, heads, head_w,
-        [
-            (local_adj, False), (after, False), (states, False), (came.reshape(flat), False),
-            (entered.reshape(flat), False), (conv, False), (recur, False), (inject, False), (decay, False),
-            (x_branch, False), (chan, False), (gates, True),
-        ],
-        [full, ((edge * SUBS, half), False), ((half, 2 * head_w), True), ((SUBS, half), False)],
-    )
+    if direct:
+        branch_low, y_grad, dx, spill, gate_grad, small_grad, down, wide_came, narrow_came = returned(
+            (spans, seqs), steps, quarters, heads, inner, branch_low, out_half, y_pre, states, decay, flow, conv, recur, inject,
+            x_branch, chan, gates, near, far, wide_away, narrow_away,
+        )
+        down = by_span(down)
+    else:
+        down = token_scatter(near, far)
+        wide_came = jnp.stack([swap(wide_away[k], m) for k, m in enumerate(xs)])
+        narrow_came = jnp.stack([swap(narrow_away[k], m) for k, m in enumerate(xs)])
+        branch_low = in_order(branch_low, swap(branch_low, 1), 0)
+        mixed_grad = nt(branch_low, out_half)
+        y_grad = gelu_back(mixed_grad * states)[0].astype(BF16)
+        kernel = functools.partial(adjoint_kernel, steps, quarters)
+        local_adj, after, enter, carry = by_heads(
+            kernel, heads, head_w, [(mixed_grad * y_branch, False), (decay, False), (flow, False)],
+            [full, full, ends, ((SUBS, half), False)],
+        )
+        prods, sums = exchanged(carry)
+        h = jnp.zeros((batch, half), F32)
+        for j in range(pairs - 1, 0, -1):
+            h = jnp.where(j > pair, prods[j] * h + sums[j], h)
+        came = entering(enter, h).reshape(2 * SUBS, half)
+        kernel = functools.partial(backward_kernel, steps, quarters)
+        dx, spill, gate_grad, small_grad = by_heads(
+            kernel, heads, head_w,
+            [(v, False) for v in (local_adj, after, states, came, flow, conv, recur, inject, decay, x_branch, chan)]
+            + [(gates, True)],
+            [full, ((edge * SUBS, half), False), ((half, 2 * head_w), True), ((SUBS, half), False)],
+        )
+    output = from_rows((resid + down).astype(BF16))
+    wide_owned = wide_kept + jnp.sum(wide_came.astype(F32), axis=0)
+    wide_owned = wide_owned.reshape(2, units, size).transpose(2, 0, 1)
+    narrow_owned = (narrow_kept + jnp.sum(narrow_came.astype(F32), axis=0)).T
     spill = lax.ppermute(
         spill.reshape(edge, batch, quarters, half)[::-1, :, 0], AXES, [(i, i - 2) for i in range(2, count)]
     )

time: 1070 us -> 876 us (0.82)
  Pallas kernels: 373 us -> 713 us
  waiting for transfers between devices: 299 us -> 5.18 us
  matrix products: 127 us -> 45.8 us
  starting transfers between devices: 82.5 us -> 9.27 us
  local copies, waits for them, and re-layouts: 117 us -> 61.1 us
  between operations: 16.6 us -> 2.91 us
    pallas_call x3, Pallas kernels: 18.1 us -> 380 us  [the longest x1 165 us: feed_forward(): pl.pallas_call(functools.partial(feed_kernel, sizes, masks, own), in_spec...]
    ppermute x42 -> x4, waiting for transfers between devices: 273 us -> 5.17 us  [swap(): return lax.ppermute(value, AXES, [(i, i ^ mask) for i in range(count)])]
    dot_general x18 -> x8, matrix products: 127 us -> 45.8 us  [dot(): lax.dot_general(a, b, ((dims[0], dims[1]), ((), ())), preferred_element_t...]
    ppermute x42 -> x4, starting transfers between devices: 76.4 us -> 5.39 us  [swap(): return lax.ppermute(value, AXES, [(i, i ^ mask) for i in range(count)])]
    unnamed x277 -> x141, local copies, waits for them, and re-layouts: 62.5 us -> 26.7 us
    pallas_call x1, Pallas kernels: 207 us -> 175 us  [scatter_grads(): pl.pallas_call(functools.partial(scatter_kernel, sizes, share), in_specs=...]
    ppermute x1, waiting for transfers between devices: 15 us -> 0.01 us  [on_device(): lax.ppermute(tail, AXES, [(i, i + 1) for i in range(1, count - 1, 2)])]
    all_gather x2 -> x0, waiting for transfers between devices: 11.4 us -> none  [exchanged(): every = lax.all_gather(carry, AXES, axis=0).reshape(pairs, 2, *carry.shape)]
  transfers between devices with their start and end apart: 47 -> 7, of which waited for: 21 -> 1; matrix products, arithmetic and copies ran while one was open for 21% -> 5% of each run, Pallas kernels for 21% -> 18%
where the time goes in v3:
time: 876 us; the launch traced here: 866 us
  Pallas kernels  713 us (81%)
  local copies, waits for them, and re-layouts  61.1 us (7%)
  matrix products  45.8 us (5%)
  other arithmetic  28.8 us (3%)
  starting transfers between devices  9.27 us (1%)
    pallas_call x1, Pallas kernels, scatter_grads(): pl.pallas_call(functools.partial(scatter_kernel, sizes, share), in_specs=...  175 us
    pallas_call x1, Pallas kernels, feed_forward(): pl.pallas_call(functools.partial(feed_kernel, sizes, masks, own), in_spec...  165 us
    pallas_call x1, Pallas kernels, gather_weights(): pl.pallas_call(functools.partial(gather_kernel, sizes, share, half), in_s...  157 us
    pallas_call x1, Pallas kernels, returned(): pl.pallas_call(functools.partial(return_kernel, sizes, steps, quarters, h...  117 us
    pallas_call x1, Pallas kernels, recurrent(): pl.pallas_call(functools.partial(recur_kernel, sizes, steps, quarters, he...  98.3 us
    dot_general x8, matrix products, dot(): lax.dot_general(a, b, ((dims[0], dims[1]), ((), ())), preferred_element_t...  45.8 us
    unnamed x141, local copies, waits for them, and re-layouts  26.7 us
  transfers between devices with their start and end apart: 7, of which 1 were waited for; matrix products, arithmetic and copies ran while one was open for 5% of the time, Pallas kernels for 18%

profile of v3, /device:TPU:8, one launch (start us, length us, event | category | flops | bytes accessed | tf_op | source)
XLA Modules:
  0.0 865.8 jit_solution(15474163899146452854)
XLA Ops:
  0.7 2.6 copy.171
  7.8 4.4 collective-permute-start
  14.7 157.1 %shard_map.228 = (bf16[2560,1280]{1,0:T(8,128)(2,1)}, bf16[2560,1280]{1,0:T(8,128)(2,1)}, bf16[1280,2560]{1,0:T(8,128)(2,1)}, bf16[1280,512]{1,0:T(8,128)(2,1)},...) custom-call(bf16[80,5120]{1,0:T(8,128)(2,1)} %rec_proj.1, ...), custom_call_target="tpu_custom_call", output_to_operand_aliasing={{5}: (4, {}), {6}: (5, {}), {7}: (6, {})} | custom-call | tf_op jit(solution)/shard_map/pallas_call | solution.py:477
  180.6 6.0 convolution_convert_fusion.2.xb
  186.6 3.0 fusion.47.y_pre
  189.6 98.3 %shard_map.229 = (f32[256,1280]{1,0:T(8,128)}, f32[256,1280]{1,0:T(8,128)}, f32[256,1280]{1,0:T(8,128)}, f32[256,1280]{1,0:T(8,128)}, f32[256,1280]{1,0:T(8,128)...) custom-call(bf16[288,1280]{1,0:T(8,128)(2,1)} %convolution_convert_f, ...), custom_call_target="tpu_custom_call" | custom-call | tf_op jit(solution)/shard_map/pallas_call | solution.py:955
  287.9 164.8 %shard_map.230 = (f32[128,2560]{1,0:T(8,128)}, bf16[4,128,2560]{2,1,0:T(8,128)(2,1)}, bf16[4,128,2560]{2,1,0:T(8,128)(2,1)}, bf16[1024,2560]{1,0:T(8,128)(2,1)},...) custom-call(bf16[128,2560]{1,0:T(8,128)(2,1)} %get-tuple-element.84.refs_0_, ...), custom_call_target="tpu_custom_call" | custom-call | tf_op jit(solution)/shard_map/pallas_call | solution.py:785
  452.7 4.7 fusion.51
  457.4 7.4 convolution_convert_fusion
  464.9 1.9 fusion.50
  466.9 4.3 convolution_convert_fusion.1
  484.3 1.7 fusion.49
  487.4 4.6 convert_add_fusion.1
  492.0 2.2 copy-done.3
  496.0 8.2 convert_add_fusion
  504.1 3.8 copy-done.8
  508.0 1.7 fusion.21.wide
  509.7 117.2 %shard_map.231 = (bf16[256,2560]{1,0:T(8,128)(2,1)}, bf16[256,1280]{1,0:T(8,128)(2,1)}, f32[256,1280]{1,0:T(8,128)}, f32[24,1280]{1,0:T(8,128)}, f32[1280,512]{1...) custom-call(bf16[128,2560]{1,0:T(8,128)(2,1)} %get-tuple-element.185, ...), custom_call_target="tpu_custom_call" | custom-call | tf_op jit(solution)/shard_map/pallas_call | solution.py:1087
  626.9 6.7 fusion.53
  633.6 4.5 slice_add_fusion
  639.1 1.9 collective-permute-start.5
  641.3 2.2 maximum_maximum_fusion
  644.4 2.0 constant_dynamic-slice_fusion.3
  646.9 5.7 convolution_add_fusion
  654.5 2.2 pad_maximum_fusion
  656.6 1.8 reshape.174
  660.0 3.5 fusion.22
  664.3 5.2 collective-permute-done.6
  673.6 175.3 %shard_map.232 = (f32[80,5120]{1,0:T(8,128)}, f32[80,2560]{1,0:T(8,128)}, f32[80,768]{1,0:T(8,128)}, f32[80,128]{1,0:T(8,128)}) custom-call(bf16[1280,256]{1,0:T(8,128)(2,1)} %get-tuple-element.208.kept_d, bf16[1280,256]{1,0:T(8,128)(2,1)} %get-tuple-element.207.given_d, bf16[640,256]{1,0:T(8,128)(2,1)} %get-tuple-element.248.kept_m, ...), custom_call_target="tpu_custom_call" | custom-call | tf_op jit(solution)/shard_map/pallas_call | solution.py:632
  853.7 3.0 multiply_add_fusion
  856.7 1.7 reshape.179
  858.4 1.8 copy.112
  (226 shorter events, 51.8 us)
Async XLA Ops:
  4.8 171.5 %collective-permute-start.2 = (bf16[2,3,2560]{2,1,0:T(4,128)(2,1)S(1)}, bf16[2,3,2560]{2,1,0:T(4,128)(2,1)S(1)}, u32[]{:S(2)}, u32[]{:S(2)}) collective-permute-start(bf16[2,3,2560]{2,1,0:T(4,128)(2,1)S(1)} %slice.131), channel_id=1, source_target_pairs={{1,3},{3,5},{5,7},{7,9},{9,11},{11,13},{13,15},{15,17},{17,19},{19... | collective-permute-start | bytes 92168 | tf_op jit(solution)/shard_map/ppermute | solution.py:1193
  5.5 170.8 %collective-permute-start.1 = (bf16[2,3,2560]{2,1,0:T(4,128)(2,1)S(1)}, bf16[2,3,2560]{2,1,0:T(4,128)(2,1)S(1)}, u32[]{:S(2)}, u32[]{:S(2)}) collective-permute-start(bf16[2,3,2560]{2,1,0:T(4,128)(2,1)S(1)} %slice.131), channel_id=1, source_target_pairs={{1,2},{3,4},{5,6},{7,8},{9,10},{11,12},{13,14},{15,16},{17,18},{19... | collective-permute-start | bytes 92168 | tf_op jit(solution)/shard_map/ppermute | solution.py:1193
  7.3 4.9 copy-start.40
  7.5 5.3 copy-start.1
  7.8 169.6 %collective-permute-start = (bf16[128,2560]{0,1:T(8,128)(2,1)S(1)}, bf16[128,2560]{0,1:T(8,128)(2,1)}, u32[]{:S(2)}, u32[]{:S(2)}) collective-permute-start(bf16[128,2560]{0,1:T(8,128)(2,1)S(1)} %copy.104), channel_id=1, source_target_pairs={{0,1},{1,0},{2,3},{3,2},{4,5},{5,4},{6,7},{7,6},{8,9},{9,8},{10,11... | collective-permute-start | bytes 1966088 | tf_op jit(solution)/shard_map/ppermute | solution.py:20
  179.4 7.2 slice-start
  180.6 6.0 slice-start.1
  452.7 4.7 copy-start.51
  457.4 7.5 slice-start.2
  457.4 7.5 slice-start.3
  464.8 30.6 %collective-permute-start.3 = (bf16[1920,1280]{1,0:T(8,128)(2,1)}, bf16[1920,1280]{1,0:T(8,128)(2,1)}, u32[]{:S(2)}, u32[]{:S(2)}) collective-permute-start(bf16[1920,1280]{1,0:T(8,128)(2,1)} %convolution_convert_fusion), channel_id=1, source_target_pairs={{0,8},{1,9},{2,10},{3,11},{4,12},{5,13},{6,14},{7,15},{8,0},{9,1},... | collective-permute-start | bytes 14745608 | tf_op jit(solution)/shard_map/ppermute | solution.py:20
  466.9 4.8 copy-start
  471.2 14.8 %collective-permute-start.4 = (bf16[960,1280]{1,0:T(8,128)(2,1)}, bf16[960,1280]{1,0:T(8,128)(2,1)}, u32[]{:S(2)}, u32[]{:S(2)}) collective-permute-start(bf16[960,1280]{1,0:T(8,128)(2,1)} %convolution_convert_fusion.1), channel_id=1, source_target_pairs={{0,8},{1,9},{2,10},{3,11},{4,12},{5,13},{6,14},{7,15},{8,0},{9,1},... | collective-permute-start | bytes 7372808 | tf_op jit(solution)/shard_map/ppermute | solution.py:20
  487.4 8.0 copy-start.33
  487.4 8.0 copy-start.52
  504.1 3.8 copy-start.8
  626.9 6.7 copy-start.9
  633.6 4.5 copy-start.35
  639.1 7.5 collective-permute-start.5
  646.6 5.9 copy-start.10
  646.8 7.1 copy-start.25
  646.8 7.1 copy-start.26
  646.8 7.1 copy-start.27
  646.8 7.1 copy-start.28
  646.8 7.1 copy-start.29
  646.8 7.1 copy-start.30
  652.5 17.0 %copy-start.4 = (f32[256,2560]{1,0:T(8,128)}, f32[256,2560]{1,0:T(8,128)S(1)}, u32[]{:S(2)}) copy-start(f32[256,2560]{1,0:T(8,128)S(1)} %convolution_add_fusion) | copy-start | bytes 7864324
  653.5 16.0 %collective-permute-start.6 = (bf16[128,2560]{1,0:T(8,128)(2,1)}, bf16[128,2560]{1,0:T(8,128)(2,1)}, u32[]{:S(2)}, u32[]{:S(2)}) collective-permute-start(bf16[128,2560]{1,0:T(8,128)(2,1)} %fusion.25), channel_id=1, source_target_pairs={{0,1},{1,0},{2,3},{3,2},{4,5},{5,4},{6,7},{7,6},{8,9},{9,8},{10,11... | collective-permute-start | bytes 1966088 | tf_op jit(solution)/shard_map/ppermute | solution.py:20
  660.0 3.5 copy-start.11
  663.4 6.0 copy-start.2
  673.6 180.1 %copy-start.5 = (f32[256,2560]{1,0:T(8,128)S(1)}, f32[256,2560]{1,0:T(8,128)}, u32[]{:S(2)}) copy-start(f32[256,2560]{1,0:T(8,128)} %copy-done.4) | copy-start | bytes 7864324
  858.4 4.3 copy-start.31
  (32 other events, 49.5 us)

commit v4 on v3

--- a/solution.py
+++ b/solution.py
@@ -296,11 +296,11 @@
         span, seq = self.peer(mask)
         return span * self.seqs + seq
 
-    def greet(self, masks):
+    def greet(self, masks, others=()):
         barrier = pltpu.get_barrier_semaphore()
-        for mask in masks:
-            pl.semaphore_signal(barrier, inc=1, device_id=self.peer(mask), device_id_type=MESH)
-        pl.semaphore_wait(barrier, len(masks))
+        for device in (*[self.peer(mask) for mask in masks], *others):
+            pl.semaphore_signal(barrier, inc=1, device_id=device, device_id_type=MESH)
+        pl.semaphore_wait(barrier, len(masks) + len(others))
 
     def plan(self, source, target, mask, only=None):
         slot = self.used
@@ -318,6 +318,10 @@
         else:
             pl.when(only)(copy.start)
         return copy
+
+    def sent(self, copy):
+        copy.wait_send()
+        self.open = [(c, only) for c, only in self.open if c is not copy]
 
     def close(self):
         for copy, only in self.open:
@@ -488,8 +492,8 @@
 
 
 def scatter_kernel(
-    sizes, share, kept_d, given_d, kept_m, given_m, grad_x, grad_y, branch, kept_g, given_g, kept_n, given_n,
-    proj_o, out_o, gate_o, gain_o, sends, recvs, *bufs,
+    sizes, share, turned, mixed, grad_x, grad_y, branch, gates, small, gain, x_own, gain_one, keep, part_own, part_other,
+    proj_o, out_o, gate_o, input_o, sum_o, sends, recvs, from_part, vector, *bufs,
 ):
     links = Links(sizes, sends, recvs)
     spans, seqs = sizes
@@ -502,30 +506,36 @@
     double = 2 * share
     n = len(inner) + 1
     links.greet([1, *inner, core, top])
-
-    def part(kept, given, cols, scratch, finish):
+    whole = links.send(part_other, from_part, 1)
+
+    def part(block, scratch, finish, shared=None):
         to_core, from_core, to_top, from_top, to_inner, from_inner, to_side, from_side = scratch
-        crossing = []
+        if shared is not None:
+            for copy in shared:
+                links.sent(copy)
+        crossing = [] if shared is None else shared
+        crossing.clear()
         for i in range(2):
             for j in range(n):
-                to_core[i * n + j] = given((1 - i) * n + j).astype(BF16)
+                to_core[i * n + j] = block(1, (1 - i) * n + j).astype(BF16)
             crossing.append(links.send(to_core.at[pl.ds(i * n, n)], from_core.at[pl.ds(i * n, n)], core))
+        mine = list(crossing)
         yield
-        crossing[0].wait_recv()
+        mine[0].wait_recv()
         over_top = {}
         for j in (*range(1, n), 0):
-            to_top[j] = (kept(n + j) + from_core[j].astype(F32)).astype(BF16)
+            to_top[j] = (block(0, n + j) + from_core[j].astype(F32)).astype(BF16)
             over_top[j] = links.send(to_top.at[j], from_top.at[j], top)
-        crossing[1].wait_recv()
+        mine[1].wait_recv()
         yield
         over_inner = []
         for j in range(1, n):
             over_top[j].wait_recv()
-            to_inner[j - 1] = (kept(j) + from_core[n + j].astype(F32) + from_top[j].astype(F32)).astype(BF16)
+            to_inner[j - 1] = (block(0, j) + from_core[n + j].astype(F32) + from_top[j].astype(F32)).astype(BF16)
             over_inner.append(links.send(to_inner.at[j - 1], from_inner.at[j - 1], inner[j - 1]))
         over_top[0].wait_recv()
         yield
-        total = kept(0) + from_core[n].astype(F32) + from_top[0].astype(F32)
+        total = block(0, 0) + from_core[n].astype(F32) + from_top[0].astype(F32)
         for j in range(1, n):
             over_inner[j - 1].wait_recv()
             total = total + from_inner[j - 1].astype(F32)
@@ -536,26 +546,18 @@
         first = side == 0
         return jnp.where(first, low, high), jnp.where(first, high, low)
 
-    def by_columns(put):
+    def by_columns(first, cols):
         def finish(total, to_side, from_side):
             mine, theirs = sided(total)
             to_side[...] = theirs.astype(BF16)
             copy = links.send(to_side, from_side, 1)
             yield
             copy.wait_recv()
-            put(mine, from_side[...].astype(F32))
-
-        return finish
-
-    def into(first, cols):
-        def put(mine, recv):
+            recv = from_side[...].astype(F32)
             proj_o[:, first : first + cols] = jnp.where(side == 0, mine, recv)
             proj_o[:, first + cols : first + 2 * cols] = jnp.where(side == 0, recv, mine)
 
-        return put
-
-    def put_gain(mine, recv):
-        gain_o[...] = mine + recv
+        return finish
 
     def by_rows(target, to_last, from_last):
         cols = target.shape[1] // 2
@@ -579,64 +581,104 @@
 
         return finish
 
-    def product(lhs, rhs, wrap, columns=None):
-        def block(j):
-            rows = lhs[j % wrap * double : (j % wrap + 1) * double]
-            if columns is None:
-                return jnp.dot(rows, rhs[...], preferred_element_type=F32)
-            which = upper if j < n else 1 - upper
-            right = rhs[:, pl.ds(pl.multiple_of(which * columns, 128), columns)]
-            return jnp.dot(rows, right, preferred_element_type=F32)
-
-        return block
-
-    def stored(blocks, columns=None):
-        def block(j):
-            if columns is None:
-                return blocks[j * double : (j + 1) * double].astype(F32)
-            which = upper if j < n else 1 - upper
-            return blocks[j % n * double : (j % n + 1) * double, pl.ds(pl.multiple_of(which * columns, 128), columns)].astype(F32)
-
-        return block
+    def rows_of(c, j, whole):
+        pairs = count // 2 if whole else count // 4
+        owner = links.other(c * core + (j // n * top if whole else 0) + (0, *inner)[j % n])
+        return pl.ds(pl.multiple_of(owner // 2 % pairs * double, 16), double)
+
+    def columns_of(j, columns):
+        return pl.ds(pl.multiple_of((upper if j < n else 1 - upper) * columns, 128), columns)
+
+    def product(lhs, rhs):
+        return lambda c, j: jnp.dot(lhs[rows_of(c, j, True)], rhs[...], preferred_element_type=F32)
+
+    def product_half(lhs, rhs, columns):
+        return lambda c, j: jnp.dot(lhs[rows_of(c, j, False)], rhs[:, columns_of(j, columns)], preferred_element_type=F32)
+
+    def stored(blocks, columns):
+        return lambda c, j: blocks[rows_of(c, j, False), columns_of(j, columns)]
+
+    def sums():
+        whole.wait_recv()
+        few = 16
+        own, width = x_own.shape
+        vector[0] = jnp.zeros(vector.shape[1:], F32)
+        vector[0, 1:2, :width] = gain[...]
+        vector[0, :, width:] = small[...]
+
+        @pl.loop(0, own // few)
+        def _(k):
+            here = pl.ds(pl.multiple_of(k * few, few), few)
+            v = x_own[here].astype(F32)
+            scale = lax.rsqrt(jnp.mean(v * v, axis=-1, keepdims=True) + EPS)
+            z = v * scale
+            d = part_own[here] + from_part[here].astype(F32)
+            e = d * gain_one[...]
+            input_o[here] = keep[here] + scale * (e - z * jnp.mean(e * z, axis=-1, keepdims=True))
+            vector[0, 0:1, :width] += jnp.sum(d * z, axis=0, keepdims=True)
+
+        slot = 1
+        for masks in ([core], [top], inner):
+            copies = [links.send(vector.at[0], vector.at[slot + k], m) for k, m in enumerate(masks)]
+            yield
+            for copy in copies:
+                copy.wait_recv()
+                links.sent(copy)
+            total = vector[0]
+            for k in range(len(masks)):
+                total = total + vector[slot + k]
+            vector[0] = total
+            slot += len(masks)
+        copy = links.send(vector.at[0], vector.at[slot], 1)
+        yield
+        copy.wait_recv()
+        sum_o[:, :width] = vector[0, :, :width] + vector[slot, :, :width]
+        sum_o[:, width:] = jnp.where(side == upper, vector[0, :, width:], vector[slot, :, width:])
 
     half = grad_x.shape[1]
     wide = branch.shape[1] // 2
-    thin = kept_g.shape[1] // 2
+    thin = gates.shape[1] // 2
+    shared = []
+    first = bufs[0]
     parts = {
-        "y": part(product(kept_d, grad_y, 2 * n), product(given_d, grad_y, 2 * n), half, bufs[0:8], by_columns(into(2 * half, half))),
-        "o": part(product(kept_m, branch, n, wide), product(given_m, branch, n, wide), wide, bufs[8:16], by_rows(out_o, *bufs[16:18])),
-        "x": part(product(kept_d, grad_x, 2 * n), product(given_d, grad_x, 2 * n), half, bufs[18:26], by_columns(into(0, half))),
-        "g": part(stored(kept_g, thin), stored(given_g, thin), thin, bufs[26:34], by_rows(gate_o, *bufs[34:36])),
-        "n": part(stored(kept_n), stored(given_n), kept_n.shape[1], bufs[36:44], by_columns(put_gain)),
+        "y": part(product(turned, grad_y), [first, *bufs[1:8]], by_columns(2 * half, half), shared),
+        "o": part(product_half(mixed, branch, wide), [first, *bufs[8:15]], by_rows(out_o, *bufs[15:17]), shared),
+        "x": part(product(turned, grad_x), [first, *bufs[17:24]], by_columns(0, half), shared),
+        "g": part(stored(gates, thin), bufs[24:32], by_rows(gate_o, *bufs[32:34])),
+        "n": sums(),
     }
-    in_turn(parts, "yxoyxoyxgnoyxgnoygnoxoygnoxgngg")
+    in_turn(parts, "yoyxoyxgnoyxgnoygnoxoygnoxgnngg")
     links.close()
 
 
-def scatter_grads(sizes, kept_d, given_d, kept_m, given_m, grad_x, grad_y, branch, kept_g, given_g, kept_n, given_n):
+def scatter_grads(sizes, share, turned, mixed, grad_x, grad_y, branch, gates, small, gain, x_own, gain_one, keep, part_own, part_other):
     n = sizes[1] // 2
-    share = kept_d.shape[0] // (4 * n)
-    half, wide, thin, gain = grad_x.shape[1], branch.shape[1], kept_g.shape[1], kept_n.shape[1]
-
-    def scratch(cols, last):
-        double = 2 * share
+    half, wide, thin = grad_x.shape[1], branch.shape[1], gates.shape[1]
+    own, width = x_own.shape
+    double = 2 * share
+
+    def scratch(cols, last, core=True):
         side = share if last is None else double
-        shapes = [(2 * n, double, cols)] * 2 + [(n, double, cols)] * 2 + [(n - 1, double, cols)] * 2 + [(side, cols)] * 2
+        shapes = [(2 * n, double, cols)] * (2 if core else 1) + [(n, double, cols)] * 2 + [(n - 1, double, cols)] * 2 + [(side, cols)] * 2
         if last is not None:
             shapes += [(share, last)] * 2
         return [pltpu.VMEM(s, BF16) for s in shapes]
 
-    bufs = [*scratch(half, None), *scratch(wide // 2, wide), *scratch(half, None), *scratch(thin // 2, thin), *scratch(gain, None)]
-    copies = 5 * (2 + n + (n - 1) + 2)
+    bufs = [*scratch(half, None), *scratch(wide // 2, wide, False), *scratch(half, None, False), *scratch(thin // 2, thin)]
+    copies = 4 * (2 + n + (n - 1) + 2) + n + 4
     inside = pl.BlockSpec(memory_space=pltpu.VMEM)
+    shapes = [(share, 4 * half), (share, wide), (share, thin), (own, width), (SUBS, width + half)]
     return pl.pallas_call(
         functools.partial(scatter_kernel, sizes, share),
-        in_specs=[inside] * 11,
-        out_specs=[inside] * 4,
-        out_shape=[jax.ShapeDtypeStruct((share, cols), F32) for cols in (4 * half, wide, thin, gain)],
-        scratch_shapes=[pltpu.SemaphoreType.DMA((copies,)), pltpu.SemaphoreType.DMA((copies,)), *bufs],
+        in_specs=[inside] * 13,
+        out_specs=[inside] * 5,
+        out_shape=[jax.ShapeDtypeStruct(s, F32) for s in shapes],
+        scratch_shapes=[
+            pltpu.SemaphoreType.DMA((copies,)), pltpu.SemaphoreType.DMA((copies,)), pltpu.VMEM((own, width), BF16),
+            pltpu.VMEM((n + 3, SUBS, width + half), F32), *bufs,
+        ],
         compiler_params=pltpu.CompilerParams(collective_id=1, has_side_effects=True, vmem_limit_bytes=VMEM_LIMIT),
-    )(kept_d, given_d, kept_m, given_m, grad_x, grad_y, branch, kept_g, given_g, kept_n, given_n)
+    )(turned, mixed, grad_x, grad_y, branch, gates, small, gain, x_own, gain_one, keep, part_own, part_other)
 
 
 def gelu_parts(v):
@@ -653,7 +695,8 @@
     cots, refs = refs[: 2 * chunks], refs[2 * chunks :]
     wides, refs = refs[:spans], refs[spans:]
     narrows, refs = refs[:spans], refs[spans:]
-    grad_o, near_o, far_o, rows_o, cots_o, act_o, hidden_o, refs = *refs[:7], refs[7:]
+    grad_o, near_o, far_o, act_o, hidden_o, refs = *refs[:5], refs[5:]
+    parts_o, refs = refs[: 2 + spans], refs[2 + spans :]
     (rows, cot, wide, narrow, act, hidden, near, down_near, down_far, to_side, from_side, to_inner, from_inner,
      sends, recvs, loads, stores) = refs
     units = narrow.shape[0]
@@ -752,18 +795,27 @@
         for k in range(chunks):
             pl.when(i == k)(functools.partial(behind, k))
 
-    pairs = [(rows, rows_o), (cot, cots_o), (act, act_o), (hidden, hidden_o), (down_near, near_o), (down_far, far_o)]
+    pairs = [(act, act_o), (hidden, hidden_o), (down_near, near_o), (down_far, far_o)]
+    for k, source in enumerate((rows, cot)):
+        for j in range(spans):
+            target = parts_o[k * (1 + spans // 2) + (j // 2 if j % 2 == 0 else spans // 2)]
+            if j % 2:
+                target = target.at[:, pl.ds(j // 2 * size, size)]
+            pairs.append((source.at[:, pl.ds(j * size, size)], target))
     out = []
     for k, (source, target) in enumerate(pairs):
         out.append(pltpu.make_async_copy(source, target, stores.at[k]))
         out[-1].start()
     give_on(chunks - 1)
     back_side[0].wait_recv()
-    total = near[0].astype(F32) + from_side[0].astype(F32)
     for k in range(chunks - 1):
         back_inner[k].wait_recv()
-        total = total + from_inner[k].astype(F32)
-    grad_o[...] = total
+    for j in range(spans):
+        columns = slice(j * size, (j + 1) * size)
+        total = near[0, :, columns].astype(F32) + from_side[0, :, columns].astype(F32)
+        for k in range(chunks - 1):
+            total = total + from_inner[k, :, columns].astype(F32)
+        grad_o[:, pl.ds(pl.multiple_of(links.flipped(links.span, j) * size, 128), size)] = total
     for copy in out:
         copy.wait()
     links.close()
@@ -777,7 +829,9 @@
     anywhere = pl.BlockSpec(memory_space=pl.ANY)
     copies = 4 * chunks
     blocks = (chunks, own, width)
-    shapes = [blocks, blocks, (total, width), (total, width), (total, 2 * units), (total, units)]
+    spans = sizes[0]
+    features = [(total, width // spans)] * (spans // 2) + [(total, width // 2)]
+    shapes = [blocks, blocks, (total, 2 * units), (total, units), *features, *features]
     held = [
         (total, width), (total, width), (2 * units, width), (units, width), (total, 2 * units), (total, units), blocks, blocks,
         blocks, blocks, blocks, (chunks - 1, own, width), (chunks - 1, own, width),
@@ -785,10 +839,10 @@
     return pl.pallas_call(
         functools.partial(feed_kernel, sizes, masks, own),
         in_specs=[anywhere] * (1 + 2 * chunks + 2 * len(wides)),
-        out_specs=[pl.BlockSpec(memory_space=pltpu.VMEM)] + [anywhere] * 6,
+        out_specs=[pl.BlockSpec(memory_space=pltpu.VMEM)] + [anywhere] * len(shapes),
         out_shape=[jax.ShapeDtypeStruct((own, width), F32)] + [jax.ShapeDtypeStruct(s, BF16) for s in shapes],
         scratch_shapes=[pltpu.VMEM(s, BF16) for s in held]
-        + [pltpu.SemaphoreType.DMA((k,)) for k in (copies, copies, 1 + 2 * chunks + 2 * len(wides), 6)],
+        + [pltpu.SemaphoreType.DMA((k,)) for k in (copies, copies, 1 + 2 * chunks + 2 * len(wides), 4 + 2 * spans)],
         compiler_params=pltpu.CompilerParams(collective_id=2, has_side_effects=True, vmem_limit_bytes=VMEM_LIMIT),
     )(own_rows, *cots, *wides, *narrows)
 
@@ -973,8 +1027,7 @@
 
 def return_kernel(
     sizes, steps, quarters, heads, inner, branch, out_w, y_pre, states, decay, flow, conv, recur, inject, xb, chan, gate,
-    near, far, wide, narrow, branch_o, y_grad, dx, spill, gate_o, small, down, wides, narrows,
-    grad, local, after, enter, carry, line, blocks, inflow, dmix, from_side, to_inner, from_inner, sends, recvs,
+    resid, near, far, wide, narrow, branch_o, y_grad, x_grad, gate_o, small, output, wides, narrows, dx, spill, came_back, grad, local, after, enter, carry, line, blocks, inflow, dmix, from_side, to_inner, from_inner, sends, recvs,
 ):
     spans, seqs = sizes
     tops = [2 * seqs * k for k in range(1, spans // 2)]
@@ -982,7 +1035,12 @@
     links = Links(sizes, sends, recvs)
     side = links.seq % 2
     own, width = branch.shape
-    links.greet([1, *inner, *[m * seqs for m in range(1, spans)]])
+    me, count = links.span * seqs + links.seq, spans * seqs
+
+    def device(index):
+        return (index // seqs, index % seqs)
+
+    links.greet([1, *inner, *[m * seqs for m in range(1, spans)]], [device((me + 2) % count)])
     place = pl.ds(pl.multiple_of(side * own, 16), own)
     whole = links.send(branch, branch_o.at[place], 1)
     tall = wide.shape[1] // 2
@@ -1043,21 +1101,44 @@
         )
 
     by_head(heads, head_w, second)
+    edge = (CONV - 1) * SUBS
+    slot = links.used
+    links.used += 1
+    handed = pltpu.make_async_remote_copy(
+        spill, came_back, links.sends.at[slot], links.recvs.at[slot], device_id=device(jnp.maximum(me - 2, 0)), device_id_type=MESH
+    )
+    pl.when(me >= 2)(handed.start)
+    links.open.append((handed, me >= 2))
+    rows = 2 * own
+    x_grad[: rows - 2 * edge] = dx[: rows - 2 * edge].astype(BF16)
     for i in range(2, n):
         inner_sum(i)
         if i + 1 < n:
             side_sum(i + 1)
+    pl.when(me + 2 < count)(handed.wait_recv)
+
+    @pl.when(me + 2 >= count)
+    def _():
+        came_back[...] = jnp.zeros_like(came_back)
+
+    last = quarter_of((SUBS, came_back.shape[1]), quarters) == quarters - 1
+    total = [dx[rows - 2 * edge : rows - edge]]
+    for k in range(CONV - 1, 0, -1):
+        added = roll(came_back[(k - 1) * SUBS : k * SUBS], quarters - 1)
+        total.append(dx[rows - k * SUBS : rows - (k - 1) * SUBS] + jnp.where(last, added, 0.0))
+    x_grad[rows - 2 * edge :] = jnp.concatenate(total, axis=0).astype(BF16)
     few = 16
+    size = width // spans
     for copy in over_inner:
         copy.wait_recv()
 
-    @pl.loop(0, own // few)
-    def _(k):
-        here = pl.ds(pl.multiple_of(k * few, few), few)
-        total = near[0, here].astype(F32) + from_side[0, here].astype(F32)
-        for j in range(n - 1):
-            total = total + from_inner[j, here].astype(F32)
-        down[here] = total
+    for j in range(spans):
+        columns = slice(j * size, (j + 1) * size)
+        there = pl.ds(pl.multiple_of(links.flipped(links.span, j) * size, 128), size)
+        total = resid[:, there] + near[0, :, columns].astype(F32) + from_side[0, :, columns].astype(F32)
+        for k in range(n - 1):
+            total = total + from_inner[k, :, columns].astype(F32)
+        output[:, there] = total.astype(BF16)
 
     for copy in across:
         copy.wait_recv()
@@ -1065,7 +1146,7 @@
 
 
 def returned(sizes, steps, quarters, heads, inner, branch, out_w, y_pre, states, decay, flow, conv, recur, inject, xb, chan, gate,
-             near, far, wide, narrow):
+             resid, near, far, wide, narrow):
     spans, _ = sizes
     own, width = branch.shape
     rows, half = y_pre.shape
@@ -1079,24 +1160,25 @@
         return jax.ShapeDtypeStruct(shape, BF16)
 
     shapes = [
-        low(rows, width), low(rows, half), high(rows, half), high((CONV - 1) * SUBS, half), high(*gate.shape), high(SUBS, half),
-        high(own, width), low(*wide.shape), low(*narrow.shape),
+        low(rows, width), low(rows, half), low(rows, half), high(*gate.shape), high(SUBS, half), low(own, width),
+        low(*wide.shape), low(*narrow.shape),
     ]
     end = (SUBS, half)
-    copies = 3 * (spans // 2) + 2 * n + 2 * n + spans + 1
+    copies = 3 * (spans // 2) + 2 * n + 2 * n + spans + 2
+    tail = ((CONV - 1) * SUBS, half)
     return pl.pallas_call(
         functools.partial(return_kernel, sizes, steps, quarters, heads, inner),
-        in_specs=[inside] * 14 + [anywhere] * 2,
-        out_specs=[inside] * 7 + [anywhere] * 2,
+        in_specs=[inside] * 15 + [anywhere] * 2,
+        out_specs=[inside] * 6 + [anywhere] * 2,
         out_shape=shapes,
         scratch_shapes=[
-            *[pltpu.VMEM((rows, half), F32)] * 3, pltpu.VMEM((4 * SUBS, half), F32), pltpu.VMEM(end, F32),
+            pltpu.VMEM((rows, half), F32), pltpu.VMEM(tail, F32), pltpu.VMEM(tail, F32), *[pltpu.VMEM((rows, half), F32)] * 3, pltpu.VMEM((4 * SUBS, half), F32), pltpu.VMEM(end, F32),
             pltpu.VMEM((n, *end), F32), pltpu.VMEM((spans, *end), F32), pltpu.VMEM(end, F32), pltpu.VMEM(end, F32),
             pltpu.VMEM((n, own, width), BF16), pltpu.VMEM((n - 1, own, width), BF16), pltpu.VMEM((n - 1, own, width), BF16),
             pltpu.SemaphoreType.DMA((copies,)), pltpu.SemaphoreType.DMA((copies,)),
         ],
         compiler_params=pltpu.CompilerParams(collective_id=4, has_side_effects=True, vmem_limit_bytes=VMEM_LIMIT),
-    )(branch, out_w, y_pre, states, decay, flow, conv, recur, inject, xb, chan, gate, near, far, wide, narrow)
+    )(branch, out_w, y_pre, states, decay, flow, conv, recur, inject, xb, chan, gate, resid, near, far, wide, narrow)
 
 
 def on_device(
@@ -1264,11 +1346,17 @@
             total = block if m == 0 else total + swap(block.astype(BF16), m).astype(F32)
         return by_span(total)
 
+    size = width // spans
+
+    def by_core(v):
+        blocks = [v[:, j * size : (j + 1) * size] for j in range(spans)]
+        return [*blocks[::2], jnp.concatenate(blocks[1::2], axis=1)]
+
     if direct:
-        normal_two_grad, near, far, all_normal, all_grads, all_act, all_hidden = feed_forward(
+        normal_two_grad, near, far, all_act, all_hidden, *features = feed_forward(
             (spans, seqs), [0, *inner], normal_two, cots, wides, narrows
         )
-        normal_two_grad = by_span(normal_two_grad)
+        all_normal, all_grads = features[: 1 + spans // 2], features[1 + spans // 2 :]
     else:
         wide, narrow = jnp.concatenate(wides, axis=1), jnp.concatenate(narrows, axis=1)
         all_normal = jnp.concatenate(token_gather(normal_two), axis=0)
@@ -1285,18 +1373,13 @@
             v = v.reshape(len(inner) + 1, 2, own, width)
             return v[:, 0], v[:, 1]
 
+        all_normal, all_grads = by_core(all_normal), by_core(all_grads)
         normal_two_grad = token_scatter(*sided(nn(all_act, wide, BF16)))
         near, far = sided(nn(all_hidden, narrow, BF16))
-    size = width // spans
-
     def core_sum(left, right):
-        def columns(odd):
-            return jnp.concatenate([right[:, j * size : (j + 1) * size] for j in range(odd, spans, 2)], axis=1)
-
-        recv = swap(tn(left, columns(1), BF16), core)
-        total = tn(left, columns(0)) + recv.astype(F32)
-        away = [total[:, k * size : (k + 1) * size].astype(BF16) for k in range(1, spans // 2)]
-        return total[:, :size], jnp.stack(away)
+        recv = swap(tn(left, right[-1], BF16), core).astype(F32)
+        total = [tn(left, v) + recv[:, k * size : (k + 1) * size] for k, v in enumerate(right[:-1])]
+        return total[0], jnp.stack([v.astype(BF16) for v in total[1:]])
 
     wide_kept, wide_away = core_sum(all_act, all_normal)
     narrow_kept, narrow_away = core_sum(all_hidden, all_grads)
@@ -1304,13 +1387,12 @@
     resid_grad = c + resid_part
     branch_low = resid_grad.astype(BF16)
     if direct:
-        branch_low, y_grad, dx, spill, gate_grad, small_grad, down, wide_came, narrow_came = returned(
+        branch_low, y_grad, x_grad, gate_grad, small_grad, output, wide_came, narrow_came = returned(
             (spans, seqs), steps, quarters, heads, inner, branch_low, out_half, y_pre, states, decay, flow, conv, recur, inject,
-            x_branch, chan, gates, near, far, wide_away, narrow_away,
+            x_branch, chan, gates, resid, near, far, wide_away, narrow_away,
         )
-        down = by_span(down)
     else:
-        down = token_scatter(near, far)
+        output = (resid + token_scatter(near, far)).astype(BF16)
         wide_came = jnp.stack([swap(wide_away[k], m) for k, m in enumerate(xs)])
         narrow_came = jnp.stack([swap(narrow_away[k], m) for k, m in enumerate(xs)])
         branch_low = in_order(branch_low, swap(branch_low, 1), 0)
@@ -1333,21 +1415,18 @@
             + [(gates, True)],
             [full, ((edge * SUBS, half), False), ((half, 2 * head_w), True), ((SUBS, half), False)],
         )
-    output = from_rows((resid + down).astype(BF16))
+        spill = lax.ppermute(
+            spill.reshape(edge, batch, quarters, half)[::-1, :, 0], AXES, [(i, i - 2) for i in range(2, count)]
+        )
+        spill = jnp.pad(
+            spill[:, :, None], ((0, 0), (0, 0), (quarters - 1, 0), (0, 0))
+        ).reshape(edge * SUBS, half)
+        x_grad = jnp.concatenate([dx[: rows - edge * SUBS], dx[rows - edge * SUBS :] + spill], axis=0).astype(BF16)
+    output = from_rows(output)
     wide_owned = wide_kept + jnp.sum(wide_came.astype(F32), axis=0)
     wide_owned = wide_owned.reshape(2, units, size).transpose(2, 0, 1)
     narrow_owned = (narrow_kept + jnp.sum(narrow_came.astype(F32), axis=0)).T
-    spill = lax.ppermute(
-        spill.reshape(edge, batch, quarters, half)[::-1, :, 0], AXES, [(i, i - 2) for i in range(2, count)]
-    )
-    spill = jnp.pad(
-        spill[:, :, None], ((0, 0), (0, 0), (quarters - 1, 0), (0, 0))
-    ).reshape(edge * SUBS, half)
-    x_grad = jnp.concatenate([dx[: rows - edge * SUBS], dx[rows - edge * SUBS :] + spill], axis=0).astype(BF16)
-
-    normal_one_grad = over_sides(nt(y_grad, proj_y) + nt(x_grad, proj_x))
-    input_part, gain_one_grad = norm_back(x, gain_one, normal_one_grad)
-    input_grad = from_rows(resid_grad + input_part)
+    normal_one_part = nt(y_grad, proj_y) + nt(x_grad, proj_x)
 
     def blocks_of(v, masks, wrap):
         size = 2 * share
@@ -1387,24 +1466,32 @@
     def ordered(v, masks, wrap):
         return [jnp.concatenate(blocks_of(v, [m ^ c for m in masks], wrap), axis=0) for c in (0, core)]
 
-    kept_d, given_d = ordered(normal_one.T, order, pairs)
-    kept_m, given_m = ordered(mixed.T, low_order, pairs // 2)
-    by_row = jnp.concatenate([gate_grad, small_grad.T, jnp.zeros((half, head_w - SUBS), F32)], axis=1)
-    kept_g, given_g = ordered(by_row, low_order, pairs // 2)
-    gains = jnp.pad(jnp.stack([gain_one_grad, gain_two_grad], axis=1), ((0, 0), (0, 126)))
-    kept_n, given_n = ordered(gains, order, pairs)
     if direct:
-        proj_owned, out_owned, rest, gains = scatter_grads(
-            (spans, seqs), kept_d, given_d, kept_m, given_m, x_grad, y_grad, branch_low, kept_g, given_g, kept_n, given_n
+        part = normal_one_part.reshape(2, own, width)
+        proj_owned, out_owned, gate_owned, input_grad, sums = scatter_grads(
+            (spans, seqs), share, normal_one.T, mixed.T, x_grad, y_grad, branch_low, gate_grad, small_grad, gain_two_grad[None],
+            mine, gain_one[None], resid_grad, lax.dynamic_index_in_dim(part, side, 0, keepdims=False),
+            lax.dynamic_index_in_dim(part, 1 - side, 0, keepdims=False).astype(BF16),
         )
+        gains = cut(sums[:2, :width], me, share, 1).T
+        small_owned = cut(sums[:, width:], me % (count // 2), share, 1).T
     else:
+        input_part, gain_one_grad = norm_back(x, gain_one, over_sides(normal_one_part))
+        input_grad = resid_grad + input_part
+        kept_d, given_d = ordered(normal_one.T, order, pairs)
+        kept_m, given_m = ordered(mixed.T, low_order, pairs // 2)
+        by_row = jnp.concatenate([gate_grad, small_grad.T, jnp.zeros((half, head_w - SUBS), F32)], axis=1)
+        kept_g, given_g = ordered(by_row, low_order, pairs // 2)
+        gains = jnp.pad(jnp.stack([gain_one_grad, gain_two_grad], axis=1), ((0, 0), (0, 126)))
+        kept_n, given_n = ordered(gains, order, pairs)
         proj_owned = jnp.concatenate(
             [in_order(*to_columns_owner(nn(kept_d, g), nn(given_d, g, BF16)), 1) for g in (x_grad, y_grad)], axis=1
         )
         out_owned = to_rows_owner(nn(kept_m, branch_low), nn(given_m, branch_low, BF16))
         rest = to_rows_owner(kept_g, given_g.astype(BF16))
+        gate_owned, small_owned = rest[:, : 2 * head_w], rest[:, 2 * head_w : 2 * head_w + SUBS]
         gains = sum(to_columns_owner(kept_n, given_n.astype(BF16)))
-    gate_owned, small_owned = rest[:, : 2 * head_w], rest[:, 2 * head_w : 2 * head_w + SUBS]
+    input_grad = from_rows(input_grad)
 
     return (
         output,

time: 876 us -> 814 us (0.929)
  local copies, waits for them, and re-layouts: 61.1 us -> 29.7 us
  other arithmetic: 28.8 us -> 12.6 us
    unnamed x141 -> x74, local copies, waits for them, and re-layouts: 26.7 us -> 10.2 us
    slice x8 -> x2, local copies, waits for them, and re-layouts: 11.7 us -> 1.67 us  [the longest x1 0.89 us: on_device(): gains = cut(sums[:2, :width], me, share, 1).T]
    pallas_call x1, Pallas kernels: 175 us -> 165 us  [scatter_grads(): pl.pallas_call(functools.partial(scatter_kernel, sizes, share), in_specs=...]
    dot_general x8 -> x10, matrix products: 45.8 us -> 50.2 us  [dot(): lax.dot_general(a, b, ((dims[0], dims[1]), ((), ())), preferred_element_t...]
  transfers between devices with their start and end apart: 7 -> 5, of which waited for: 1 -> 0; matrix products, arithmetic and copies ran while one was open for 5% -> 3% of each run, Pallas kernels for 18% -> 20%
where the time goes in v4:
time: 814 us; the launch traced here: 806 us
  Pallas kernels  705 us (87%)
  matrix products  50.2 us (6%)
  local copies, waits for them, and re-layouts  29.7 us (4%)
  other arithmetic  12.6 us (2%)
    pallas_call x1, Pallas kernels, scatter_grads(): pl.pallas_call(functools.partial(scatter_kernel, sizes, share), in_specs=...  165 us
    pallas_call x1, Pallas kernels, feed_forward(): pl.pallas_call(functools.partial(feed_kernel, sizes, masks, own), in_spec...  165 us
    pallas_call x1, Pallas kernels, gather_weights(): pl.pallas_call(functools.partial(gather_kernel, sizes, share, half), in_s...  157 us
    pallas_call x1, Pallas kernels, returned(): pl.pallas_call(functools.partial(return_kernel, sizes, steps, quarters, h...  118 us
    pallas_call x1, Pallas kernels, recurrent(): pl.pallas_call(functools.partial(recur_kernel, sizes, steps, quarters, he...  98.5 us
    dot_general x10, matrix products, dot(): lax.dot_general(a, b, ((dims[0], dims[1]), ((), ())), preferred_element_t...  50.2 us
  transfers between devices with their start and end apart: 5, of which 0 were waited for; matrix products, arithmetic and copies ran while one was open for 3% of the time, Pallas kernels for 20%

profile of v4, /device:TPU:8, one launch (start us, length us, event | category | flops | bytes accessed | tf_op | source)
XLA Modules:
  0.0 805.8 jit_solution(8554640468770768829)
XLA Ops:
  0.7 2.6 copy.53
  3.2 1.5 copy.52
  5.6 1.3 collective-permute-start.1
  7.7 4.4 collective-permute-start
  14.5 157.4 %shard_map.228 = (bf16[2560,1280]{1,0:T(8,128)(2,1)}, bf16[2560,1280]{1,0:T(8,128)(2,1)}, bf16[1280,2560]{1,0:T(8,128)(2,1)}, bf16[1280,512]{1,0:T(8,128)(2,1)},...) custom-call(bf16[80,5120]{1,0:T(8,128)(2,1)} %rec_proj.1, ...), custom_call_target="tpu_custom_call", output_to_operand_aliasing={{5}: (4, {}), {6}: (5, {}), {7}: (6, {})} | custom-call | tf_op jit(solution)/shard_map/pallas_call | solution.py:481
  171.9 0.9 convert_bitcast_fusion
  176.2 1.0 fusion.4
  177.2 1.2 copy-done.3
  178.4 3.1 convolution_convert_fusion.2.xb
  181.4 2.9 fusion.10.y_pre
  184.3 98.5 %shard_map.229 = (f32[256,1280]{1,0:T(8,128)}, f32[256,1280]{1,0:T(8,128)}, f32[256,1280]{1,0:T(8,128)}, f32[256,1280]{1,0:T(8,128)}, f32[256,1280]{1,0:T(8,128)...) custom-call(bf16[288,1280]{1,0:T(8,128)(2,1)} %convolution_convert_f, ...), custom_call_target="tpu_custom_call" | custom-call | tf_op jit(solution)/shard_map/pallas_call | solution.py:1009
  282.9 165.2 %shard_map.230 = (f32[128,2560]{1,0:T(8,128)}, bf16[4,128,2560]{2,1,0:T(8,128)(2,1)}, bf16[4,128,2560]{2,1,0:T(8,128)(2,1)}, bf16[1024,1920]{1,0:T(8,128)(2,1)},...) custom-call(bf16[128,2560]{1,0:T(8,128)(2,1)} %get-tuple-element.88., ...), custom_call_target="tpu_custom_call" | custom-call | tf_op jit(solution)/shard_map/pallas_call | solution.py:839
  448.1 10.6 %convolution_convert_fusion = bf16[1920,1280]{1,0:T(8,128)(2,1)} fusion(bf16[1024,1920]{1,0:T(8,128)(2,1)} %get-tuple-element.111, bf16[1024,1280]{1,0:T(8,128)(2,1)} %get-tuple-element.113), kind=kOutput, calls=%fused_computation | convolution fusion | flops 5035622400 | bytes 11468800 | tf_op jit(solution)/shard_map/dot_general | solution.py:24
  458.8 4.3 convolution_convert_fusion.1
  464.4 1.6 copy.35.turned
  466.1 2.3 copy.34
  469.6 1.7 fusion.16
  471.2 2.2 convert_element_type.63
  473.9 2.8 fusion.9.narrow
  476.8 3.3 convert_element_type.60
  480.7 4.8 fusion.5.wide
  485.5 118.4 %shard_map.231 = (bf16[256,2560]{1,0:T(8,128)(2,1)}, bf16[256,1280]{1,0:T(8,128)(2,1)}, bf16[256,1280]{1,0:T(8,128)(2,1)}, f32[1280,512]{1,0:T(8,128)}, f32[8,12...) custom-call(bf16[128,2560]{1,0:T(8,128)(2,1)} %get-tuple-element.135.branch, ...), custom_call_target="tpu_custom_call" | custom-call | tf_op jit(solution)/shard_map/pallas_call | solution.py:1169
  604.0 5.0 fusion.18
  609.0 4.8 convolution_add_fusion
  614.7 1.1 dynamic-slice_bitcast_fusion.part_own
  615.9 165.4 %shard_map.232 = (f32[80,5120]{1,0:T(8,128)}, f32[80,2560]{1,0:T(8,128)}, f32[80,512]{1,0:T(8,128)}, f32[128,2560]{1,0:T(8,128)}, f32[8,3840]{1,0:T(8,128)}) custom-call(bf16[2560,256]{1,0:T(8,128)(2,1)} %copy.35.turned, bf16[1280,256]{1,0:T(8,128)(2,1)} %bitcast.97, bf16[256,1280]{1,0:T(8,128)(2,1)} %get-tuple-element.119.grad_x, ...), custom_call_target="tpu_custom_call" | custom-call | tf_op jit(solution)/shard_map/pallas_call | solution.py:671
  784.8 1.0 copy.33
  785.9 1.7 reshape.150
  787.6 1.8 copy.36
  790.0 6.4 fusion.7
  797.3 5.5 fusion
  802.9 1.2 copy.54
  (124 shorter events, 18.5 us)
Async XLA Ops:
  4.8 7.3 copy-start.11
  4.8 169.9 %collective-permute-start.2 = (bf16[2,3,2560]{2,1,0:T(4,128)(2,1)S(1)}, bf16[2,3,2560]{2,1,0:T(4,128)(2,1)S(1)}, u32[]{:S(2)}, u32[]{:S(2)}) collective-permute-start(bf16[2,3,2560]{2,1,0:T(4,128)(2,1)S(1)} %slice.95), channel_id=1, source_target_pairs={{1,3},{3,5},{5,7},{7,9},{9,11},{11,13},{13,15},{15,17},{17,19},{19... | collective-permute-start | bytes 92168 | tf_op jit(solution)/shard_map/ppermute | solution.py:1275
  5.6 169.1 %collective-permute-start.1 = (bf16[2,3,2560]{2,1,0:T(4,128)(2,1)S(1)}, bf16[2,3,2560]{2,1,0:T(4,128)(2,1)S(1)}, u32[]{:S(2)}, u32[]{:S(2)}) collective-permute-start(bf16[2,3,2560]{2,1,0:T(4,128)(2,1)S(1)} %slice.95), channel_id=1, source_target_pairs={{1,2},{3,4},{5,6},{7,8},{9,10},{11,12},{13,14},{15,16},{17,18},{19... | collective-permute-start | bytes 92168 | tf_op jit(solution)/shard_map/ppermute | solution.py:1275
  6.9 5.8 copy-start.14
  6.9 5.8 copy-start.15
  6.9 5.8 copy-start.16
  6.9 5.8 copy-start.17
  6.9 5.8 copy-start.18
  7.0 5.8 copy-start.19
  7.6 167.9 %copy-start.1 = (bf16[128,2560]{1,0:T(8,128)(2,1)}, bf16[128,2560]{1,0:T(8,128)(2,1)S(1)}, u32[]{:S(2)}) copy-start(bf16[128,2560]{1,0:T(8,128)(2,1)S(1)} %reshape.142.x_own) | copy-start | bytes 1966084
  7.7 167.8 %collective-permute-start = (bf16[128,2560]{1,0:T(8,128)(2,1)S(1)}, bf16[128,2560]{1,0:T(8,128)(2,1)S(1)}, u32[]{:S(2)}, u32[]{:S(2)}) collective-permute-start(bf16[128,2560]{1,0:T(8,128)(2,1)S(1)} %reshape.142.x_own), channel_id=1, source_target_pairs={{0,1},{1,0},{2,3},{3,2},{4,5},{5,4},{6,7},{7,6},{8,9},{9,8},{10,11... | collective-permute-start | bytes 1966088 | tf_op jit(solution)/shard_map/ppermute | solution.py:20
  175.5 2.9 copy-start.3
  176.2 5.3 slice-start.3
  178.4 3.1 slice-start.4
  448.1 10.7 %copy-start.22 = (bf16[1024,1280]{1,0:T(8,128)(2,1)S(1)}, bf16[1024,1280]{1,0:T(8,128)(2,1)}, u32[]{:S(2)}) copy-start(bf16[1024,1280]{1,0:T(8,128)(2,1)} %get-tuple-element.116) | copy-start | bytes 7864324
  448.1 10.7 %copy-start.24 = (bf16[1024,960]{1,0:T(8,128)(2,1)S(1)}, bf16[1024,960]{1,0:T(8,128)(2,1)}, u32[]{:S(2)}) copy-start(bf16[1024,960]{1,0:T(8,128)(2,1)} %get-tuple-element.114) | copy-start | bytes 5898244
  458.7 18.0 %collective-permute-start.3 = (bf16[1920,1280]{1,0:T(8,128)(2,1)}, bf16[1920,1280]{1,0:T(8,128)(2,1)}, u32[]{:S(2)}, u32[]{:S(2)}) collective-permute-start(bf16[1920,1280]{1,0:T(8,128)(2,1)} %convolution_convert_fusion), channel_id=1, source_target_pairs={{0,8},{1,9},{2,10},{3,11},{4,12},{5,13},{6,14},{7,15},{8,0},{9,1},... | collective-permute-start | bytes 14745608 | tf_op jit(solution)/shard_map/ppermute | solution.py:20
  463.1 8.2 %collective-permute-start.4 = (bf16[960,1280]{1,0:T(8,128)(2,1)}, bf16[960,1280]{1,0:T(8,128)(2,1)}, u32[]{:S(2)}, u32[]{:S(2)}) collective-permute-start(bf16[960,1280]{1,0:T(8,128)(2,1)} %convolution_convert_fusion.1), channel_id=1, source_target_pairs={{0,8},{1,9},{2,10},{3,11},{4,12},{5,13},{6,14},{7,15},{8,0},{9,1},... | collective-permute-start | bytes 7372808 | tf_op jit(solution)/shard_map/ppermute | solution.py:20
  464.4 3.9 copy-start
  473.5 3.3 copy-start.5
  476.8 3.6 copy-start.20
  476.8 4.0 copy-start.27
  480.1 5.4 copy-start.2
  604.0 5.0 copy-start.6
  615.9 168.8 %copy-start.12 = (bf16[128,2560]{1,0:T(8,128)(2,1)S(1)}, bf16[128,2560]{1,0:T(8,128)(2,1)}, u32[]{:S(2)}) copy-start(bf16[128,2560]{1,0:T(8,128)(2,1)} %get-tuple-element.117) | copy-start | bytes 1966084
  784.7 11.7 %slice-start = ((s8[9830400]{0:T(1024)(128)(4,1)}), s8[1441792]{0:T(1024)(128)(4,1)S(1)}, s32[]{:S(2)}) async-start(s8[9830400]{0:T(1024)(128)(4,1)} %bitcast.92), calls=%async_computation | async-start | bytes 2883584
  787.5 8.8 %slice-start.1 = ((s8[9830400]{0:T(1024)(128)(4,1)}), s8[4194304]{0:T(1024)(128)(4,1)S(1)}, s32[]{:S(2)}) async-start(s8[9830400]{0:T(1024)(128)(4,1)} %bitcast.92), calls=%async_computation.1 | async-start | bytes 8388608
  790.0 6.4 slice-start.2
  790.0 6.4 copy-start.21
  790.0 6.6 copy-start.23
  790.0 7.4 copy-start.26
  797.3 5.5 copy-start.8
  (7 other events, 14.6 us)

commit v5 on v4

--- a/solution.py
+++ b/solution.py
@@ -288,6 +288,9 @@
             bit *= 2
         return index
 
+    def flipped_index(self, index, mask):
+        return self.flipped(index, mask)
+
     def peer(self, mask):
         low, high = mask % self.seqs, mask // self.seqs
         return (self.flipped(self.span, high), self.flipped(self.seq, low))
@@ -302,11 +305,12 @@
             pl.semaphore_signal(barrier, inc=1, device_id=device, device_id_type=MESH)
         pl.semaphore_wait(barrier, len(masks) + len(others))
 
-    def plan(self, source, target, mask, only=None):
+    def plan(self, source, target, mask, only=None, device=None):
         slot = self.used
         self.used += 1
+        device = self.peer(mask) if device is None else device
         copy = pltpu.make_async_remote_copy(
-            source, target, self.sends.at[slot], self.recvs.at[slot], device_id=self.peer(mask), device_id_type=MESH
+            source, target, self.sends.at[slot], self.recvs.at[slot], device_id=device, device_id_type=MESH
         )
         self.open.append((copy, only))
         return copy
@@ -337,158 +341,6 @@
     for part in parts.values():
         for _ in part:
             pass
-
-
-def gather_kernel(
-    sizes, share, half, rec_proj, out_proj, gate_weight, small, tokens, wide, narrow,
-    proj_x, proj_y, out_half, gates, every, tokens_o, wide_o, narrow_o, sends, recvs, locals_,
-):
-    links = Links(sizes, sends, recvs)
-    spans, seqs = sizes
-    count = spans * seqs
-    me = links.span * seqs + links.seq
-    side = me % 2
-    upper = me // (count // 2)
-    inner = [2 * k for k in range(1, seqs // 2)]
-    core, top = seqs, count // 2
-    double = 2 * share
-    links.greet([1, *inner, core, top])
-    kept = [0]
-
-    def local(source, target, only=None):
-        copy = pltpu.make_async_copy(source, target, locals_.at[kept[0]])
-        kept[0] += 1
-        if only is None:
-            copy.start()
-        else:
-            pl.when(only)(copy.start)
-        return copy
-
-    def pieces_out(place, piece):
-        over_inner = {m: links.send(piece(place(me)), piece(place(me)), m) for m in inner}
-        over_top = {0: links.send(piece(place(me)), piece(place(me)), top)}
-        over_core = [links.send(piece(place(me)), piece(place(me)), core)]
-        yield
-        for m in inner:
-            over_inner[m].wait_recv()
-            there = piece(place(links.other(m)))
-            over_top[m] = links.send(there, there, top)
-            over_core.append(links.send(there, there, core))
-        yield
-        for m in (0, *inner):
-            over_top[m].wait_recv()
-            there = piece(place(links.other(top + m)))
-            over_core.append(links.send(there, there, core))
-        yield
-        for copy in over_core:
-            copy.wait_recv()
-
-    def columns_part(source, first, target):
-        def piece(start):
-            return target.at[pl.ds(pl.multiple_of(start, 16), double)]
-
-        def columns(which):
-            return source.at[:, pl.ds(pl.multiple_of(first + which * half, 128), half)]
-
-        row = target.at[pl.ds(pl.multiple_of(me * share, 16), share)]
-        mine = local(columns(side), row)
-        theirs = links.send(columns(1 - side), row, 1)
-        yield
-        mine.wait()
-        theirs.wait_recv()
-        yield from pieces_out(lambda d: d // 2 * double, piece)
-
-    def whole_part(source, target):
-        height = source.shape[0]
-
-        def piece(start):
-            return target.at[pl.ds(pl.multiple_of(start, 16), 2 * height)]
-
-        row = target.at[pl.ds(pl.multiple_of(me * height, 16), height)]
-        mine = local(source, row)
-        theirs = links.send(source, row, 1)
-        yield
-        mine.wait()
-        theirs.wait_recv()
-        yield from pieces_out(lambda d: d // 2 * 2 * height, piece)
-
-    def rows_part(source, target):
-        width = source.shape[1]
-        pairs_half = count // 4
-
-        def place(d):
-            return d // 2 % pairs_half * double
-
-        def rows(start, size):
-            return target.at[pl.ds(pl.multiple_of(start, 16), size)]
-
-        def piece(start, which):
-            return target.at[pl.ds(pl.multiple_of(start, 16), double), pl.ds(pl.multiple_of(which * (width // 2), 128), width // 2)]
-
-        holds = side == upper
-        row = rows(place(me) + side * share, share)
-        mine = local(source, row, holds)
-        gift = links.send(source, row, 1, side != upper)
-        yield
-
-        @pl.when(holds)
-        def _():
-            mine.wait()
-            gift.wait_recv()
-
-        across = links.send(rows(place(me), double), rows(place(me), double), top, holds)
-        pl.when(side != upper)(across.wait_recv)
-        over_inner = {m: links.send(piece(place(me), upper), piece(place(me), upper), m) for m in inner}
-        over_core = [links.send(rows(place(me), double), rows(place(me), double), core)]
-        over_top = {}
-        yield
-        for m in inner:
-            over_inner[m].wait_recv()
-            there = piece(place(links.other(m)), upper)
-            over_top[m] = links.send(there, there, top)
-            over_core.append(links.send(there, there, core))
-        yield
-        for m in inner:
-            over_top[m].wait_recv()
-            there = piece(place(links.other(m)), 1 - upper)
-            over_core.append(links.send(there, there, core))
-        yield
-        for copy in over_core:
-            copy.wait_recv()
-
-    parts = {
-        "x": columns_part(rec_proj, 0, proj_x),
-        "s": whole_part(small, every),
-        "g": rows_part(gate_weight, gates),
-        "y": columns_part(rec_proj, 2 * half, proj_y),
-        "o": rows_part(out_proj, out_half),
-    }
-    in_turn(parts, "xsgxsgyoxyxogsygsygoyo")
-    links.close()
-
-
-def gather_weights(sizes, rec_proj, out_proj, gate_weight, small, tokens, wide, narrow):
-    share = rec_proj.shape[0]
-    half = rec_proj.shape[1] // 4
-    count = sizes[0] * sizes[1]
-    held = [
-        (count * share, half), (count * share, half), (count // 2 * share, out_proj.shape[1]),
-        (count // 2 * share, gate_weight.shape[1]), (count * small.shape[0], small.shape[1]),
-        tokens.shape, wide.shape, narrow.shape,
-    ]
-    anywhere = pl.BlockSpec(memory_space=pl.ANY)
-    copies = 5 * 16
-    return pl.pallas_call(
-        functools.partial(gather_kernel, sizes, share, half),
-        in_specs=[anywhere] * 7,
-        out_specs=[anywhere] * 8,
-        out_shape=[jax.ShapeDtypeStruct(s, BF16) for s in held],
-        scratch_shapes=[
-            pltpu.SemaphoreType.DMA((copies,)), pltpu.SemaphoreType.DMA((copies,)), pltpu.SemaphoreType.DMA((8,))
-        ],
-        input_output_aliases={4: 5, 5: 6, 6: 7},
-        compiler_params=pltpu.CompilerParams(collective_id=0, has_side_effects=True, vmem_limit_bytes=VMEM_LIMIT),
-    )(rec_proj, out_proj, gate_weight, small, tokens, wide, narrow)
 
 
 def scatter_kernel(
@@ -692,9 +544,9 @@
     chunks = len(masks)
     spans = sizes[0]
     own_rows, refs = refs[0], refs[1:]
-    cots, refs = refs[: 2 * chunks], refs[2 * chunks :]
+    cots, refs = refs[0], refs[1:]
     wides, refs = refs[:spans], refs[spans:]
-    narrows, refs = refs[:spans], refs[spans:]
+    narrows, refs = refs[:2], refs[2:]
     grad_o, near_o, far_o, act_o, hidden_o, refs = *refs[:5], refs[5:]
     parts_o, refs = refs[: 2 + spans], refs[2 + spans :]
     (rows, cot, wide, narrow, act, hidden, near, down_near, down_far, to_side, from_side, to_inner, from_inner,
@@ -711,13 +563,19 @@
         return copy
 
     first = load(own_rows, rows.at[pl.ds(0, own)], 0)
-    late = [load(cots[b], cot.at[pl.ds(b * own, own)], 1 + b) for b in range(2 * chunks)]
+    late = [
+        load(cots.at[links.flipped(links.seq // 2, masks[b // 2] // 2), b % 2], cot.at[pl.ds(b * own, own)], 1 + b)
+        for b in range(2 * chunks)
+    ]
     for j in range(spans):
         columns = pl.ds(j * size, size)
         late.append(load(wides[j], wide.at[:, columns], 1 + 2 * chunks + j))
-        late.append(load(narrows[j], narrow.at[:, columns], 1 + 2 * chunks + spans + j))
-    links.greet([1, *masks[1:]])
+        if j < 2:
+            late.append(load(narrows[j], narrow.at[:, columns], 1 + 2 * chunks + spans + j))
+    core, tops = sizes[1], range(2, spans, 2)
+    links.greet([1, *masks[1:], core, *[m * core for m in tops]])
     first.wait()
+    across = [links.send(narrows[0], narrow.at[:, pl.ds(m * size, size)], m * core) for m in tops]
 
     def block(b):
         return rows.at[pl.ds(b * own, own)]
@@ -728,35 +586,51 @@
     back_side = [links.plan(to_side.at[i], from_side.at[i], 1) for i in each]
     back_inner = [links.plan(to_inner.at[i - 1], from_inner.at[i - 1], masks[i]) for i in each[1:]]
     over_side[0].start()
-    over_inner[1].start()
+    for i in each[1:]:
+        over_inner[i].start()
     for copy in late:
         copy.wait()
+    beside = [links.plan(narrow.at[:, pl.ds(m * size, size)], narrow.at[:, pl.ds((m + 1) * size, size)], core) for m in tops]
+
+    def narrow_here():
+        for copy, onto in zip(across, beside):
+            copy.wait_recv()
+            onto.start()
+        for copy in beside:
+            copy.wait_recv()
 
     def onward(i):
         over_inner[i].wait_recv()
         over_side[i].start()
-        if i + 1 < chunks:
-            over_inner[i + 1].start()
 
     def give_on(i):
         back_side[i].wait_recv()
         to_inner[i - 1] = (near[i].astype(F32) + from_side[i].astype(F32)).astype(BF16)
         back_inner[i - 1].start()
 
+    last = chunks - 1
+
     def ahead(i):
         over_side[i].wait_recv()
         if i == 0:
-            onward(1)
-        else:
-            back_side[i - 1].start()
+            for k in (2, 1):
+                if k < last:
+                    onward(k)
+            narrow_here()
+
+    def midway(i):
+        if i == min(1, last - 1):
+            for k in range(3, chunks):
+                onward(k)
+        if i == last:
+            give_on(1)
 
     def behind(i):
-        if 0 < i < chunks - 1:
-            onward(i + 1)
-        if i == chunks - 1:
+        if 0 < i < last - 1:
             back_side[i].start()
-        if i > 1:
-            give_on(i - 1)
+        if i == last:
+            for k in (last, last - 1, 0):
+                back_side[k].start()
 
     def compute(i):
         here = pl.ds(pl.multiple_of(i * pair, 16), pair)
@@ -775,6 +649,8 @@
             act[here, start : start + n] = (back * up * slope).astype(BF16)
             act[here, units + start : units + start + n] = (back * value).astype(BF16)
             start += n
+        for k in range(chunks):
+            pl.when(i == k)(functools.partial(midway, k))
         step = 512
 
         @pl.loop(0, width // step)
@@ -806,7 +682,8 @@
     for k, (source, target) in enumerate(pairs):
         out.append(pltpu.make_async_copy(source, target, stores.at[k]))
         out[-1].start()
-    give_on(chunks - 1)
+    for k in range(last, 1, -1):
+        give_on(k)
     back_side[0].wait_recv()
     for k in range(chunks - 1):
         back_inner[k].wait_recv()
@@ -827,7 +704,7 @@
     chunks = len(masks)
     total = 2 * chunks * own
     anywhere = pl.BlockSpec(memory_space=pl.ANY)
-    copies = 4 * chunks
+    copies = 4 * chunks + sizes[0]
     blocks = (chunks, own, width)
     spans = sizes[0]
     features = [(total, width // spans)] * (spans // 2) + [(total, width // 2)]
@@ -838,13 +715,13 @@
     ]
     return pl.pallas_call(
         functools.partial(feed_kernel, sizes, masks, own),
-        in_specs=[anywhere] * (1 + 2 * chunks + 2 * len(wides)),
+        in_specs=[anywhere] * (4 + len(wides)),
         out_specs=[pl.BlockSpec(memory_space=pltpu.VMEM)] + [anywhere] * len(shapes),
         out_shape=[jax.ShapeDtypeStruct((own, width), F32)] + [jax.ShapeDtypeStruct(s, BF16) for s in shapes],
         scratch_shapes=[pltpu.VMEM(s, BF16) for s in held]
-        + [pltpu.SemaphoreType.DMA((k,)) for k in (copies, copies, 1 + 2 * chunks + 2 * len(wides), 4 + 2 * spans)],
+        + [pltpu.SemaphoreType.DMA((k,)) for k in (copies, copies, 3 + 2 * chunks + len(wides), 4 + 2 * spans)],
         compiler_params=pltpu.CompilerParams(collective_id=2, has_side_effects=True, vmem_limit_bytes=VMEM_LIMIT),
-    )(own_rows, *cots, *wides, *narrows)
+    )(own_rows, cots, *wides, *narrows)
 
 
 def expanded(v, quarters):
@@ -895,51 +772,279 @@
         body(lambda ref: ref.at[:, columns], lambda ref: ref.at[pl.ds(start, head_w)])
 
 
-def recur_kernel(
-    sizes, steps, quarters, heads, inner, xb, chan, gate, y_pre, out_w, x_own, gain, cot, wide, narrow, *refs
+def front_kernel(
+    sizes, steps, quarters, heads, head_w, share, x_own, halo, params_in, rec_proj, out_proj, gate_weight, cot, wide, narrow, *refs
 ):
     spans, seqs = sizes
-    core, tops = seqs, [2 * seqs * k for k in range(1, spans // 2)]
+    count = spans * seqs
+    inner = [2 * k for k in range(1, seqs // 2)]
     n = len(inner) + 1
-    outs, refs = refs[: 8 + 2 * (spans - 1) + 2 * n], refs[8 + 2 * (spans - 1) + 2 * n :]
-    conv, recur, inject, decay, states, flow_o, mixed, resid = outs[:8]
-    wides, narrows = outs[8 : 7 + spans], outs[7 + spans : 6 + 2 * spans]
-    cots, normal = outs[6 + 2 * spans : -1], outs[-1]
-    prod, enter, line, blocks, inflow, to_side, from_side, low, sends, recvs = refs
+    core, top = seqs, count // 2
+    (normal, xb, y_pre, conv, recur, inject, decay, states, flow, mixed, resid, normal_two, params, chan), refs = refs[:14], refs[14:]
+    (proj_x, proj_y, out_half, gates), refs = refs[:4], refs[4:]
+    wides, beside_narrow, cots, refs = refs[: spans - 1], refs[spans - 1], refs[spans], refs[spans + 1 :]
+    (lead, held_x, held_y, held_o, held_g, every, prod, enter, line, blocks, inflow, to_side, from_side, low,
+     sends, recvs, locals_) = refs
     links = Links(sizes, sends, recvs)
-    side = links.seq % 2
+    me = links.span * seqs + links.seq
+    side, upper = me % 2, me // (count // 2)
     own, width = x_own.shape
     rows = 2 * own
-    masks = [1, *inner, *[m * seqs for m in range(1, spans)]]
-    links.greet(masks)
-    early = pl.ds(0, wide.shape[0] // 4)
-    later = pl.ds(wide.shape[0] // 4, wide.shape[0] - wide.shape[0] // 4)
-    across_wide = [links.send(wide.at[early], wides[m // seqs - 1].at[early], m) for m in tops]
-    beside = [links.send(wide, wides[0], core), links.send(narrow, narrows[0], core)]
-    over_inner = {m: links.plan(cot, cots[2 * k], m) for k, m in enumerate(inner)}
-    over_side = [links.send(cot, cots[2 * len(inner)], 1)]
-    head_w = gate.shape[1] // 2
-
-    def gates(cols, tall):
+    half = width // 2
+    double = 2 * share
+    links.greet([1, *inner, *[m * seqs for m in range(1, spans)]])
+    kept = [0]
+
+    def local(source, target, only=None):
+        copy = pltpu.make_async_copy(source, target, locals_.at[kept[0]])
+        kept[0] += 1
+        if only is None:
+            copy.start()
+        else:
+            pl.when(only)(copy.start)
+        return copy
+
+    z = links.seq // 2
+    offsets = [o for s in range(1, n) for o in (-s, s)]
+    there = {o: jnp.logical_and(z + o >= 0, z + o < n) for o in offsets}
+    beyond = {-1: (links.span, jnp.maximum(links.seq - 2, 0)), 1: (links.span, jnp.minimum(links.seq + 2, seqs - 1))}
+
+    def along(piece):
+        passing = {}
+        for o in (0, *offsets):
+            for way in (-1, 1):
+                if o * way <= 0 and abs(o) + 1 < n:
+                    both = jnp.logical_and(there[way], there[o]) if o else there[way]
+                    passing[o, way] = links.plan(piece(o), piece(o), None, both, beyond[way])
+        return passing
+
+    def arrival(passing, o):
+        way = 1 if o < 0 else -1
+        return passing[o + way, way]
+
+    def begin(passing):
+        for way in (-1, 1):
+            pl.when(there[way])(passing[0, way].start)
+
+    def take(passing, o):
+        arrival(passing, o).wait_recv()
+        way = 1 if o < 0 else -1
+        if (o, way) in passing:
+            pl.when(there[way])(passing[o, way].start)
+
+    def pieces_out(own_out, piece, part, far):
+        passing = along(piece)
+        over_top = {o: links.plan(piece(o), piece(o), top, there[o]) for o in offsets}
+        over_core = {o: links.plan(part(o), part(o), core, there[o]) for o in offsets}
+        far_core = {o: links.plan(far(o), far(o), core, there[o]) for o in offsets}
+        begin(passing)
+        first_core = links.send(own_out, own_out, core)
+        first_top = first_far = None
+        if far(0) is not None:
+            first_top = links.send(piece(0), piece(0), top)
+        yield
+        for o in offsets:
+
+            @pl.when(there[o])
+            def _():
+                take(passing, o)
+                over_top[o].start()
+                over_core[o].start()
+
+            if o == offsets[len(offsets) // 2 - 1]:
+                yield
+        yield
+        if first_top is not None:
+            first_top.wait_recv()
+            first_far = links.send(far(0), far(0), core)
+        for o in offsets:
+
+            @pl.when(there[o])
+            def _():
+                over_top[o].wait_recv()
+                far_core[o].start()
+
+        yield
+        first_core.wait_recv()
+        if first_far is not None:
+            first_far.wait_recv()
+        for o in offsets:
+
+            @pl.when(there[o])
+            def _():
+                over_core[o].wait_recv()
+                far_core[o].wait_recv()
+
+    def pieces_direct(whole, piece):
+        over_inner = {m: links.send(piece(0), piece(0), m) for m in inner}
+        over_core = [links.send(whole, whole, core)]
+        over_top = {}
+        yield
+        for m in inner:
+            over_inner[m].wait_recv()
+            here = piece(links.flipped(z, m // 2) - z)
+            over_top[m] = links.send(here, here, top)
+            over_core.append(links.send(here, here, core))
+        yield
+        for m in inner:
+            over_top[m].wait_recv()
+            here = piece(links.flipped(z, m // 2) - z, 1 - upper)
+            over_core.append(links.send(here, here, core))
+        yield
+        for copy in over_core:
+            copy.wait_recv()
+
+    def columns_part(source, first, target):
+        def piece(o, over=0):
+            device = (links.other(over) if over else me) + 2 * o
+            start = jnp.clip(device // 2 * double, 0, target.shape[0] - double)
+            return target.at[pl.ds(pl.multiple_of(start, 16), double)]
+
+        def columns(which):
+            return source.at[:, pl.ds(pl.multiple_of(first + which * half, 128), half)]
+
+        row = target.at[pl.ds(pl.multiple_of(me * share, 16), share)]
+        mine = local(columns(side), row)
+        theirs = links.send(columns(1 - side), row, 1)
+        yield
+        mine.wait()
+        theirs.wait_recv()
+        yield from pieces_out(piece(0), piece, piece, lambda o: piece(o, top))
+
+    def rows_part(source, target, direct):
+        cols = source.shape[1]
+        pairs_half = count // 4
+
+        def rows_at(start, size):
+            return target.at[pl.ds(pl.multiple_of(start, 16), size)]
+
+        begin_at = me // 2 % pairs_half * double
+
+        def piece(o, which=None):
+            start = jnp.clip(begin_at + o * double, 0, target.shape[0] - double)
+            which = upper if which is None else which
+            return target.at[pl.ds(pl.multiple_of(start, 16), double), pl.ds(pl.multiple_of(which * (cols // 2), 128), cols // 2)]
+
+        holds = side == upper
+        row = rows_at(begin_at + side * share, share)
+        mine = local(source, row, holds)
+        gift = links.send(source, row, 1, side != upper)
+        yield
+
+        @pl.when(holds)
+        def _():
+            mine.wait()
+            gift.wait_recv()
+
+        whole = rows_at(begin_at, double)
+        across = links.send(whole, whole, top, holds)
+        yield
+        pl.when(side != upper)(across.wait_recv)
+        if direct:
+            yield from pieces_direct(whole, piece)
+        else:
+            yield from pieces_out(whole, piece, piece, lambda o: piece(o, 1 - upper) if o else None)
+
+    def small_part():
+        height = params_in.shape[0]
+
+        def rows_of(device):
+            return every.at[pl.ds(pl.multiple_of(device // 2 * 2 * height, 16), 2 * height)]
+
+        row = pl.ds(pl.multiple_of(me * height, 16), height)
+        every[row] = params_in[...]
+        theirs = links.send(every.at[row], every.at[row], 1)
+        yield
+        theirs.wait_recv()
+        held = [me]
+        for masks in (inner, [top], [core]):
+            copies = [links.send(rows_of(d), rows_of(d), m) for d in held for m in masks]
+            held = held + [links.flipped_index(d, m) for d in held for m in masks]
+            yield
+            for copy in copies:
+                copy.wait_recv()
+        params[...] = jnp.zeros_like(params)
+        lanes = params_in.shape[1]
+        for d in range(count):
+            tile = every[d * height : (d + 1) * height]
+            base, shift = d * share // lanes * lanes, d * share % lanes
+            if shift + share <= lanes:
+                params[:, base : base + lanes] += pltpu.roll(tile, shift, 1) if shift else tile
+            else:
+                turned = pltpu.roll(jnp.concatenate([tile, jnp.zeros_like(tile)], axis=1), shift, 1)
+                params[:, base : base + 2 * lanes] += turned
+        chan[...] = params[:SUBS, pl.ds(pl.multiple_of(side * half, 128), half)]
+
+    parts = {
+        "x": columns_part(rec_proj, 0, proj_x),
+        "v": small_part(),
+        "g": rows_part(gate_weight, gates, False),
+        "y": columns_part(rec_proj, 2 * half, proj_y),
+        "o": rows_part(out_proj, out_half, True),
+    }
+
+    def advance(order):
+        for name in order:
+            next(parts[name], None)
+
+    place = pl.ds(pl.multiple_of(side * own, 16), own)
+    def cot_at(o, far=0):
+        return cots.at[jnp.clip(z + o, 0, n - 1), far]
+
+    cot_inner = [links.plan(cot_at(0), cot_at(0), m) for m in inner]
+    cot_side = []
+    own_cot = local(cot, cot_at(0))
+    advance("xvgoy")
+    tokens = links.send(x_own, lead.at[place], 1)
+    lead[place] = x_own[...]
+    lead[rows:] = halo[...]
+    advance("xvgo")
+    own_cot.wait()
+    own_side = links.send(cot_at(0), cot_at(0, 1), 1)
+    advance("xvxgyov")
+    advance("ggxgvyyxg")
+    loads = [local(proj_x, held_x), local(gates, held_g)]
+    tokens.wait_recv()
+    few = 16
+
+    @pl.loop(0, lead.shape[0] // few)
+    def _(k):
+        here = pl.ds(pl.multiple_of(k * few, few), few)
+        normal[here] = normed(lead[here].astype(F32), params[SUBS : SUBS + 1]).astype(BF16)
+
+    for copy in loads:
+        copy.wait()
+
+    def gate(cols, tall):
+        cols(xb)[...] = jnp.dot(normal[...], cols(held_x)[...], preferred_element_type=F32).astype(BF16)
         forward_kernel(
-            steps, quarters, cols(xb), cols(chan), tall(gate), cols(conv), cols(recur), cols(inject), cols(decay),
+            steps, quarters, cols(xb), cols(chan), tall(held_g), cols(conv), cols(recur), cols(inject), cols(decay),
             cols(states), cols(prod), cols(enter), cols(line.at[0]),
         )
 
-    by_head(heads, head_w, gates)
-    inflow[...] = chunk_inflow(
-        links, line, blocks, quarters, False, lambda: [over_inner[m].start() for m in inner]
-    )
-    across_wide += [links.send(wide.at[later], wides[m // seqs - 1].at[later], m) for m in tops]
-    across_narrow = {m: links.send(narrow, narrows[m // seqs - 1], m) for m in tops}
+    by_head(heads, head_w, gate)
+    inflow[...] = chunk_inflow(links, line, blocks, quarters, False, lambda: [copy.start() for copy in cot_inner])
+    advance("o")
+    tops = [2 * seqs * k for k in range(1, spans // 2)]
+    across = {m: links.send(wide, wides[m // seqs - 1], m) for m in tops}
+    beside = [links.send(wide, wides[0], core), links.send(narrow, beside_narrow, core)]
+    def onward(k):
+        cot_inner[k].wait_recv()
+        here = links.flipped(z, inner[k] // 2) - z
+        cot_side.append(links.send(cot_at(here), cot_at(here, 1), 1))
+
+    advance("yy")
+    loads = [local(proj_y, held_y)]
+    loads[0].wait()
     block = steps * SUBS
 
     def mix(cols, tall):
-        ins, flow, hold, gain_y = cols(inflow), cols(flow_o), cols(states), cols(y_pre)
+        cols(y_pre)[...] = jnp.dot(normal[:rows], cols(held_y)[...], preferred_element_type=F32)
+        ins, flows, hold, gain_y = cols(inflow), cols(flow), cols(states), cols(y_pre)
         for b in (0, 1):
             entered = cols(enter)[b * SUBS : (b + 1) * SUBS] * ins[...] + cols(enter)[(2 + b) * SUBS : (3 + b) * SUBS]
-            flow[b * SUBS : (b + 1) * SUBS] = entered
-            flow[(2 + b) * SUBS : (3 + b) * SUBS] = cols(prod)[(b + 1) * block - SUBS : (b + 1) * block]
+            flows[b * SUBS : (b + 1) * SUBS] = entered
+            flows[(2 + b) * SUBS : (3 + b) * SUBS] = cols(prod)[(b + 1) * block - SUBS : (b + 1) * block]
             here = slice(b * block, (b + 1) * block)
             total = hold[here].reshape(steps, SUBS, head_w) + cols(prod)[here].reshape(steps, SUBS, head_w) * entered[None]
             total = total.reshape(block, head_w)
@@ -947,19 +1052,25 @@
             cols(mixed)[here] = (total * gelu_parts(gain_y[here])[0]).astype(BF16)
 
     by_head(heads, head_w, mix)
+
+    onward(0)
+    advance("oo")
+    load = local(out_half, held_o)
+    load.wait()
     step = 512
 
     @pl.loop(0, width // step)
     def _(k):
         columns = pl.ds(pl.multiple_of(k * step, 128), step)
-        total = jnp.dot(mixed[...], out_w[:, columns], preferred_element_type=F32)
+        total = jnp.dot(mixed[...], held_o[:, columns], preferred_element_type=F32)
         first = side == 0
         resid[:, columns] = x_own[:, columns].astype(F32) + jnp.where(first, total[:own], total[own:])
         to_side[:, columns] = jnp.where(first, total[own:], total[:own]).astype(BF16)
 
     partial = links.send(to_side, from_side, 1)
+    for k in range(1, n - 2):
+        onward(k)
     partial.wait_recv()
-    few = 16
     size = width // spans
 
     @pl.loop(0, own // few)
@@ -967,62 +1078,65 @@
         here = pl.ds(pl.multiple_of(k * few, few), few)
         total = resid[here] + from_side[here].astype(F32)
         resid[here] = total
-        low[here] = normed(total, gain[...]).astype(BF16)
+        low[here] = normed(total, params[SUBS + 1 : SUBS + 2]).astype(BF16)
 
     for j in range(spans):
         start = pl.multiple_of(links.flipped(links.span, j) * size, 128)
-        normal[:, j * size : (j + 1) * size] = low[:, pl.ds(start, size)]
-
-    for k, m in enumerate(inner):
-        over_inner[m].wait_recv()
-        over_side.append(links.send(cots[2 * k], cots[2 * k + 1], 1))
-    for copy in across_wide:
+        normal_two[:, j * size : (j + 1) * size] = low[:, pl.ds(start, size)]
+
+    onward(n - 2)
+    for m in tops:
+        across[m].wait_recv()
+        beside.append(links.send(wides[m // seqs - 1], wides[m // seqs], core))
+    for copy in (*beside, own_side, *cot_side):
         copy.wait_recv()
-    for m in tops:
-        beside.append(links.send(wides[m // seqs - 1], wides[m // seqs], core))
-    for m in tops:
-        across_narrow[m].wait_recv()
-        beside.append(links.send(narrows[m // seqs - 1], narrows[m // seqs], core))
-    for copy in (*beside, *over_side):
-        copy.wait_recv()
+    for part in parts.values():
+        for _ in part:
+            pass
     links.close()
 
 
-def recurrent(sizes, steps, quarters, heads, inner, xb, chan, gate, y_pre, out_w, x_own, gain, cot, wide, narrow):
+def front(sizes, steps, quarters, heads, head_w, x_own, halo, params, rec_proj, out_proj, gate_weight, cot, wide, narrow):
     spans, seqs = sizes
-    half = xb.shape[1]
+    count = spans * seqs
     own, width = x_own.shape
-    rows = 2 * own
-    n = len(inner) + 1
+    half, rows, share = width // 2, 2 * own, rec_proj.shape[0]
+    n = seqs // 2
     inside, anywhere = pl.BlockSpec(memory_space=pltpu.VMEM), pl.BlockSpec(memory_space=pl.ANY)
-    full = jax.ShapeDtypeStruct((rows, half), F32)
-
-    def low(shape):
+
+    def high(*shape):
+        return jax.ShapeDtypeStruct(shape, F32)
+
+    def low(*shape):
         return jax.ShapeDtypeStruct(shape, BF16)
 
-    shapes = [
-        *[full] * 5, jax.ShapeDtypeStruct((4 * SUBS, half), F32), low((rows, half)), jax.ShapeDtypeStruct((own, width), F32),
-        *[low(wide.shape)] * (spans - 1), *[low(narrow.shape)] * (spans - 1), *[low(cot.shape)] * (2 * n - 1), low((own, width)),
+    lead = rows + halo.shape[0]
+    near = [
+        low(lead, width), low(lead, half), *[high(rows, half)] * 6, high(4 * SUBS, half), low(rows, half), high(own, width),
+        low(own, width), high(params.shape[0], width), high(SUBS, half),
     ]
-    copies = 3 * (spans // 2) * 2 + 2 * n + 2 + (n - 1) + spans
+    far = [
+        low(width, half), low(width, half), low(half, width), low(half, gate_weight.shape[1]), *[low(*wide.shape)] * (spans - 1),
+        low(*narrow.shape), low(n, 2, *cot.shape),
+    ]
     end = (SUBS, half)
+    copies = 4 * (3 + 10 * n) + 4 * n + 3 + 6 * n + (n - 1) + 2 * spans + 4
     outs = pl.pallas_call(
-        functools.partial(recur_kernel, sizes, steps, quarters, heads, inner),
-        in_specs=[inside] * 7 + [anywhere] * 3,
-        out_specs=[inside] * 8 + [anywhere] * (len(shapes) - 9) + [inside],
-        out_shape=shapes,
+        functools.partial(front_kernel, sizes, steps, quarters, heads, head_w, share),
+        in_specs=[inside] * 7 + [anywhere] * 2,
+        out_specs=[inside] * len(near) + [anywhere] * len(far),
+        out_shape=[*near, *far],
         scratch_shapes=[
+            pltpu.VMEM((lead, width), BF16), pltpu.VMEM((width, half), BF16), pltpu.VMEM((width, half), BF16),
+            pltpu.VMEM((half, width), BF16), pltpu.VMEM((half, gate_weight.shape[1]), BF16), pltpu.VMEM((count * params.shape[0], params.shape[1]), F32),
             pltpu.VMEM((rows, half), F32), pltpu.VMEM((4 * SUBS, half), F32), pltpu.VMEM((n, *end), F32),
             pltpu.VMEM((spans, *end), F32), pltpu.VMEM(end, F32), *[pltpu.VMEM((own, width), BF16)] * 3,
-            pltpu.SemaphoreType.DMA((copies,)), pltpu.SemaphoreType.DMA((copies,)),
+            pltpu.SemaphoreType.DMA((copies,)), pltpu.SemaphoreType.DMA((copies,)), pltpu.SemaphoreType.DMA((16,)),
         ],
-        compiler_params=pltpu.CompilerParams(collective_id=3, has_side_effects=True, vmem_limit_bytes=VMEM_LIMIT),
-    )(xb, chan, gate, y_pre, out_w, x_own, gain, cot, wide, narrow)
-    wides, narrows = outs[8 : 7 + spans], outs[7 + spans : 6 + 2 * spans]
-    received = outs[6 + 2 * spans : -1]
-    near, far = [cot] + [received[2 * k] for k in range(n - 1)], [received[2 * (n - 1)]] + [received[2 * k + 1] for k in range(n - 1)]
-    cots = [b for pair in zip(near, far) for b in pair]
-    return outs[:8], [wide, *wides], [narrow, *narrows], cots, outs[-1]
+        compiler_params=pltpu.CompilerParams(collective_id=0, has_side_effects=True, vmem_limit_bytes=VMEM_LIMIT),
+    )(x_own, halo, params, rec_proj, out_proj, gate_weight, cot, wide, narrow)
+    wides, narrows, cots = outs[18 : 17 + spans], outs[17 + spans], outs[18 + spans]
+    return outs[:14], outs[14:18], [wide, *wides], [narrow, narrows], cots
 
 
 def return_kernel(
@@ -1208,6 +1322,7 @@
     xs = [2 * seqs * k for k in range(1, spans // 2)]
     top = count // 2
     upper = me // top
+    chunk_masks = [0, *inner[1::-1], *inner[2:]]
 
     def to_rows(v):
         return v.reshape(batch, quarters, steps, width).transpose(2, 0, 1, 3).reshape(own, width)
@@ -1221,7 +1336,7 @@
     def cut(v, index, size, axis):
         return lax.dynamic_slice_in_dim(v, index * size, size, axis)
 
-    direct = share % 16 == 0 and spans == 4
+    direct = share % 16 == 0 and (spans, seqs) == (4, 8)
 
     def gathered_rows(block, buffer, place):
         pieces = {0: block}
@@ -1249,25 +1364,41 @@
         size = width // spans
         return jnp.concatenate([cut(v, span ^ j, size, 1) for j in range(spans)], axis=1)
 
-    small = jnp.stack([norm_one, norm_two, *conv_weight.T, conv_bias, *gate_bias.T, decay_param])
+    def over_sides(partial):
+        partial = partial.reshape(2, own, width)
+        other = lax.dynamic_index_in_dim(partial, 1 - side, 0, keepdims=False).astype(BF16)
+        return lax.dynamic_index_in_dim(partial, side, 0, keepdims=False) + swap(other, 1).astype(F32)
+
+    def exchanged(carry):
+        every = lax.all_gather(carry, AXES, axis=0).reshape(pairs, 2, batch, quarters, half)
+        every = lax.dynamic_index_in_dim(every, side, 1, keepdims=False)
+        return every[:, :, 0], every[:, :, 1]
+
+    def entering(enter, h):
+        enter = enter.reshape(2, 2, SUBS, half)
+        return enter[0] * jnp.repeat(h, quarters, axis=0)[None] + enter[1]
+
+    def by_steps(v):
+        return v.reshape(2, steps, SUBS, half)
+
+    def span_gather(block):
+        pieces = {0: block}
+        for m in xs:
+            pieces[m] = swap(block, m)
+        for n in list(pieces):
+            pieces[n ^ core] = swap(pieces[n], core)
+        return [pieces[m * seqs] for m in range(spans)]
+
+    def token_gather(v):
+        blocks = [v] + [swap(v, m) for m in inner]
+        return [b for block in blocks for b in (block, swap(block, 1))]
+
+    small = jnp.stack([*conv_weight.T, conv_bias, *gate_bias.T, decay_param, norm_one, norm_two]).astype(F32)
+    small = jnp.concatenate([small[:7], jax.nn.softplus(small[7:8]), small[8:]], axis=0)
     wide_own = mlp_wide.transpose(1, 2, 0).reshape(2 * units, width // spans)
     narrow_own = mlp_narrow.T
     grads_own = by_span(to_rows(cotangent))
-    if direct:
-        packed = jnp.pad(small, ((0, 6), (0, -share % 128)))
-        proj_x, proj_y, out_half, gates, small, grads_own, wide_own, narrow_own = gather_weights(
-            (spans, seqs), rec_proj, out_proj, gate_weight, packed, grads_own, wide_own, narrow_own
-        )
-        small = small.reshape(count, 16, -1)[:, :10, :share].transpose(1, 0, 2).reshape(10, width)
-    else:
-        proj_x = columns_half(rec_proj[:, :width])
-        proj_y = columns_half(rec_proj[:, width:])
-        gates = rows_half(gate_weight)
-        out_half = rows_half(out_proj)
-        small = lax.all_gather(small, AXES, axis=1, tiled=True)
-    small = small.astype(F32)
-    gain_one, gain_two = small[0], small[1]
-    chan = cut(jnp.concatenate([small[2:9], jax.nn.softplus(small[9:10])], axis=0), side, half, 1)
+    c = to_rows(cotangent).astype(F32)
 
     mine = to_rows(inputs)
     x = mine.astype(F32)
@@ -1276,48 +1407,30 @@
         tail, AXES, [(i, i + 2) for i in range(1, count - 2, 2)]
     )
     halo = jnp.zeros((edge, batch, quarters, width), BF16).at[:, :, 0].set(halo[:, ::-1].transpose(1, 0, 2))
-    both = in_order(mine, swap(mine, 1), 0)
-    lead = jnp.concatenate([both, halo.reshape(edge * SUBS, width), jnp.zeros((8, width), BF16)], axis=0)
-    normal_one = normed(lead.astype(F32), gain_one).astype(BF16)
-    x_branch = nn(normal_one, proj_x, BF16)
-    normal_one = normal_one[:rows]
-    y_pre = nn(normal_one, proj_y)
-    def over_sides(partial):
-        partial = partial.reshape(2, own, width)
-        other = lax.dynamic_index_in_dim(partial, 1 - side, 0, keepdims=False).astype(BF16)
-        return lax.dynamic_index_in_dim(partial, side, 0, keepdims=False) + swap(other, 1).astype(F32)
-
-    def exchanged(carry):
-        every = lax.all_gather(carry, AXES, axis=0).reshape(pairs, 2, batch, quarters, half)
-        every = lax.dynamic_index_in_dim(every, side, 1, keepdims=False)
-        return every[:, :, 0], every[:, :, 1]
-
-    def entering(enter, h):
-        enter = enter.reshape(2, 2, SUBS, half)
-        return enter[0] * jnp.repeat(h, quarters, axis=0)[None] + enter[1]
-
-    def by_steps(v):
-        return v.reshape(2, steps, SUBS, half)
-
-    def span_gather(block):
-        pieces = {0: block}
-        for m in xs:
-            pieces[m] = swap(block, m)
-        for n in list(pieces):
-            pieces[n ^ core] = swap(pieces[n], core)
-        return [pieces[m * seqs] for m in range(spans)]
-
-    def token_gather(v):
-        blocks = [v] + [swap(v, m) for m in inner]
-        return [b for block in blocks for b in (block, swap(block, 1))]
-
-    c = to_rows(cotangent).astype(F32)
+    halo = jnp.concatenate([halo.reshape(edge * SUBS, width), jnp.zeros((8, width), BF16)], axis=0)
+
     if direct:
-        (conv, recur, inject, decay, states, flow, mixed, resid), wides, narrows, cots, normal_two = recurrent(
-            (spans, seqs), steps, quarters, heads, inner, x_branch, chan, gates, y_pre, out_half, mine, gain_two[None],
-            grads_own, wide_own, narrow_own,
+        packed = jnp.pad(small, ((0, 6), (0, -share % 128)))
+        nearby, (proj_x, proj_y, out_half, gates), wides, narrows, cots = front(
+            (spans, seqs), steps, quarters, heads, head_w, mine, halo, packed, rec_proj, out_proj, gate_weight, grads_own,
+            wide_own, narrow_own,
         )
+        normal_one, x_branch, y_pre, conv, recur, inject, decay, states, flow, mixed, resid, normal_two, params, chan = nearby
+        gain_one, gain_two = params[SUBS], params[SUBS + 1]
+        normal_one = normal_one[:rows]
     else:
+        proj_x = columns_half(rec_proj[:, :width])
+        proj_y = columns_half(rec_proj[:, width:])
+        gates = rows_half(gate_weight)
+        out_half = rows_half(out_proj)
+        small = lax.all_gather(small, AXES, axis=1, tiled=True)
+        gain_one, gain_two = small[SUBS], small[SUBS + 1]
+        chan = cut(small[:SUBS], side, half, 1)
+        lead = jnp.concatenate([in_order(mine, swap(mine, 1), 0), halo], axis=0)
+        normal_one = normed(lead.astype(F32), gain_one).astype(BF16)
+        x_branch = nn(normal_one, proj_x, BF16)
+        normal_one = normal_one[:rows]
+        y_pre = nn(normal_one, proj_y)
         y_branch, gelu_back = jax.vjp(jax.nn.gelu, y_pre)
         kernel = functools.partial(forward_kernel, steps, quarters)
         full = ((rows, half), False)
@@ -1354,7 +1467,7 @@
 
     if direct:
         normal_two_grad, near, far, all_act, all_hidden, *features = feed_forward(
-            (spans, seqs), [0, *inner], normal_two, cots, wides, narrows
+            (spans, seqs), chunk_masks, normal_two, cots, wides, narrows
         )
         all_normal, all_grads = features[: 1 + spans // 2], features[1 + spans // 2 :]
     else:
@@ -1388,7 +1501,7 @@
     branch_low = resid_grad.astype(BF16)
     if direct:
         branch_low, y_grad, x_grad, gate_grad, small_grad, output, wide_came, narrow_came = returned(
-            (spans, seqs), steps, quarters, heads, inner, branch_low, out_half, y_pre, states, decay, flow, conv, recur, inject,
+            (spans, seqs), steps, quarters, heads, chunk_masks[1:], branch_low, out_half, y_pre, states, decay, flow, conv, recur, inject,
             x_branch, chan, gates, resid, near, far, wide_away, narrow_away,
         )
     else:

time: 814 us -> 729 us (0.90)
  Pallas kernels: 705 us -> 634 us
  matrix products: 50.2 us -> 41.5 us
    pallas_call x2 -> x1, Pallas kernels: 256 us -> 217 us  [front(): pl.pallas_call(functools.partial(front_kernel, sizes, steps, quarters, he...]
    pallas_call x1, Pallas kernels: 165 us -> 147 us  [feed_forward(): pl.pallas_call(functools.partial(feed_kernel, sizes, masks, own), in_spec...]
    pallas_call x1, Pallas kernels: 118 us -> 104 us  [returned(): pl.pallas_call(functools.partial(return_kernel, sizes, steps, quarters, h...]
    dot_general x10 -> x8, matrix products: 50.2 us -> 41.5 us  [dot(): lax.dot_general(a, b, ((dims[0], dims[1]), ((), ())), preferred_element_t...]
  transfers between devices with their start and end apart: 5 -> 4, of which waited for: 0 -> 0; matrix products, arithmetic and copies ran while one was open for 3% -> 5% of each run, Pallas kernels for 20% -> 0%
where the time goes in v5:
time: 729 us; the launch traced here: 725 us
  Pallas kernels  634 us (87%)
  matrix products  41.5 us (6%)
  local copies, waits for them, and re-layouts  28.4 us (4%)
  other arithmetic  17.4 us (2%)
    pallas_call x1, Pallas kernels, front(): pl.pallas_call(functools.partial(front_kernel, sizes, steps, quarters, he...  217 us
    pallas_call x1, Pallas kernels, scatter_grads(): pl.pallas_call(functools.partial(scatter_kernel, sizes, share), in_specs=...  165 us
    pallas_call x1, Pallas kernels, feed_forward(): pl.pallas_call(functools.partial(feed_kernel, sizes, masks, own), in_spec...  147 us
    pallas_call x1, Pallas kernels, returned(): pl.pallas_call(functools.partial(return_kernel, sizes, steps, quarters, h...  104 us
    dot_general x8, matrix products, dot(): lax.dot_general(a, b, ((dims[0], dims[1]), ((), ())), preferred_element_t...  41.5 us
  transfers between devices with their start and end apart: 4, of which 0 were waited for; matrix products, arithmetic and copies ran while one was open for 5% of the time, Pallas kernels for 0%

profile of v5, /device:TPU:8, one launch (start us, length us, event | category | flops | bytes accessed | tf_op | source)
XLA Modules:
  0.0 724.9 jit_solution(4956880686286735673)
XLA Ops:
  0.6 0.9 slice.83
  2.2 1.3 collective-permute-start
  3.6 1.4 stack.26
  5.0 1.6 copy.37
  8.9 1.0 reshape.123.x_own
  11.3 217.4 %shard_map.228 = (bf16[288,2560]{1,0:T(8,128)(2,1)}, bf16[288,1280]{1,0:T(8,128)(2,1)}, f32[256,1280]{1,0:T(8,128)}, f32[256,1280]{1,0:T(8,128)}, f32[256,1280]{...) custom-call(bf16[128,2560]{1,0:T(8,128)(2,1)} %reshape.123.x_own, ...), custom_call_target="tpu_custom_call" | custom-call | tf_op jit(solution)/shard_map/pallas_call | solution.py:1124
  228.7 147.2 %shard_map.229 = (f32[128,2560]{1,0:T(8,128)}, bf16[4,128,2560]{2,1,0:T(8,128)(2,1)}, bf16[4,128,2560]{2,1,0:T(8,128)(2,1)}, bf16[1024,1920]{1,0:T(8,128)(2,1)},...) custom-call(bf16[128,2560]{1,0:T(8,128)(2,1)} %get-tuple-element.73., ...), custom_call_target="tpu_custom_call" | custom-call | tf_op jit(solution)/shard_map/pallas_call | solution.py:716
  376.0 10.6 %convolution_convert_fusion = bf16[1920,1280]{1,0:T(8,128)(2,1)} fusion(bf16[1024,1920]{1,0:T(8,128)(2,1)} %get-tuple-element.94, bf16[1024,1280]{1,0:T(8,128)(2,1)} %get-tuple-element.96), kind=kOutput, calls=%fused_computation | convolution fusion | flops 5035622400 | bytes 11468800 | tf_op jit(solution)/shard_map/dot_general | solution.py:24
  386.5 1.1 copy.31
  387.6 4.0 copy.30
  391.9 1.7 fusion.10
  394.6 4.6 convolution_convert_fusion.1
  399.7 3.2 fusion.13
  402.9 5.5 fusion.12
  408.4 1.1 slice_bitcast_fusion.turned
  409.6 1.7 fusion.9
  411.6 0.9 copy-done.20
  412.6 2.9 fusion.6.narrow
  415.4 3.3 convert_element_type.43
  418.7 5.0 fusion.2.wide
  423.8 103.6 %shard_map.230 = (bf16[256,2560]{1,0:T(8,128)(2,1)}, bf16[256,1280]{1,0:T(8,128)(2,1)}, bf16[256,1280]{1,0:T(8,128)(2,1)}, f32[1280,512]{1,0:T(8,128)}, f32[8,12...) custom-call(bf16[128,2560]{1,0:T(8,128)(2,1)} %get-tuple-element.121.branch, ...), custom_call_target="tpu_custom_call" | custom-call | tf_op jit(solution)/shard_map/pallas_call | solution.py:1283
  527.3 5.0 fusion.11
  532.4 4.8 convolution_add_fusion
  537.2 0.9 fusion.7.part_other
  538.1 1.1 dynamic-slice_bitcast_fusion.part_own
  539.2 165.4 %shard_map.231 = (f32[80,5120]{1,0:T(8,128)}, f32[80,2560]{1,0:T(8,128)}, f32[80,512]{1,0:T(8,128)}, f32[128,2560]{1,0:T(8,128)}, f32[8,3840]{1,0:T(8,128)}) custom-call(bf16[2560,256]{1,0:T(8,128)(2,1)} %slice_bitcast_fusion.turned, bf16[1280,256]{1,0:T(8,128)(2,1)} %bitcast.86, bf16[256,1280]{1,0:T(8,128)(2,1)} %get-tuple-element.103.grad_x, ...), custom_call_target="tpu_custom_call" | custom-call | tf_op jit(solution)/shard_map/pallas_call | solution.py:523
  704.7 1.0 slice.92
  708.4 1.0 copy.29
  709.8 1.8 copy.32
  712.2 3.9 fusion.4
  716.2 5.5 fusion
  721.7 1.2 copy.41
  (89 shorter events, 11.8 us)
Async XLA Ops:
  1.6 8.3 %collective-permute-start.1 = (bf16[2,3,2560]{2,1,0:T(4,128)(2,1)S(1)}, bf16[2,3,2560]{2,1,0:T(4,128)(2,1)S(1)}, u32[]{:S(2)}, u32[]{:S(2)}) collective-permute-start(bf16[2,3,2560]{2,1,0:T(4,128)(2,1)S(1)} %slice.83), channel_id=1, source_target_pairs={{1,3},{3,5},{5,7},{7,9},{9,11},{11,13},{13,15},{15,17},{17,19},{19... | collective-permute-start | bytes 92168 | tf_op jit(solution)/shard_map/ppermute | solution.py:1406
  2.2 7.6 %collective-permute-start = (bf16[2,3,2560]{2,1,0:T(4,128)(2,1)S(1)}, bf16[2,3,2560]{2,1,0:T(4,128)(2,1)S(1)}, u32[]{:S(2)}, u32[]{:S(2)}) collective-permute-start(bf16[2,3,2560]{2,1,0:T(4,128)(2,1)S(1)} %slice.83), channel_id=1, source_target_pairs={{1,2},{3,4},{5,6},{7,8},{9,10},{11,12},{13,14},{15,16},{17,18},{19... | collective-permute-start | bytes 92168 | tf_op jit(solution)/shard_map/ppermute | solution.py:1406
  6.6 1.8 copy-start.11
  376.0 10.6 %copy-start.12 = (bf16[256,1280]{1,0:T(8,128)(2,1)S(1)}, bf16[256,1280]{1,0:T(8,128)(2,1)}, u32[]{:S(2)}) copy-start(bf16[256,1280]{1,0:T(8,128)(2,1)} %get-tuple-element.102) | copy-start | bytes 1966084
  386.5 28.9 %collective-permute-start.2 = (bf16[1920,1280]{1,0:T(8,128)(2,1)}, bf16[1920,1280]{1,0:T(8,128)(2,1)}, u32[]{:S(2)}, u32[]{:S(2)}) collective-permute-start(bf16[1920,1280]{1,0:T(8,128)(2,1)} %convolution_convert_fusion), channel_id=1, source_target_pairs={{0,8},{1,9},{2,10},{3,11},{4,12},{5,13},{6,14},{7,15},{8,0},{9,1},... | collective-permute-start | bytes 14745608 | tf_op jit(solution)/shard_map/ppermute | solution.py:20
  386.5 5.1 copy-start.1
  387.6 5.9 copy-start.4
  391.7 2.9 copy-start.17
  394.6 5.2 copy-start.18
  394.6 5.2 copy-start.22
  399.2 12.1 %collective-permute-start.3 = (bf16[960,1280]{1,0:T(8,128)(2,1)S(1)}, bf16[960,1280]{1,0:T(8,128)(2,1)S(1)}, u32[]{:S(2)}, u32[]{:S(2)}) collective-permute-start(bf16[960,1280]{1,0:T(8,128)(2,1)S(1)} %convolution_convert_fusion.1), channel_id=1, source_target_pairs={{0,8},{1,9},{2,10},{3,11},{4,12},{5,13},{6,14},{7,15},{8,0},{9,1},... | collective-permute-start | bytes 7372808 | tf_op jit(solution)/shard_map/ppermute | solution.py:20
  399.7 3.2 copy-start.16
  399.7 3.2 copy-start.21
  402.9 5.5 copy-start.3
  411.3 1.3 copy-start.20
  411.6 3.8 copy-start.2
  415.4 3.3 copy-start.19
  418.7 5.0 copy-start
  527.3 5.0 copy-start.5
  539.2 167.3 %copy-start.15 = (bf16[80]{0:T(256)(128)(2,1)S(1)}, bf16[80]{0:T(256)(128)(2,1)}, u32[]{:S(2)}) copy-start(bf16[80]{0:T(256)(128)(2,1)} %param.22) | copy-start | bytes 484
  539.2 169.0 %copy-start.13 = (bf16[128,2560]{1,0:T(8,128)(2,1)S(1)}, bf16[128,2560]{1,0:T(8,128)(2,1)}, u32[]{:S(2)}) copy-start(bf16[128,2560]{1,0:T(8,128)(2,1)} %get-tuple-element.100) | copy-start | bytes 1966084
  704.7 4.7 copy-start.9
  709.8 2.4 copy-start.6
  709.8 6.3 slice-start
  712.2 3.9 slice-start.1
  712.2 3.9 copy-start.7
  716.2 5.5 copy-start.8
  721.7 1.2 copy-start.14
  721.7 1.8 copy-start.10

commit v6 on v5

--- a/solution.py
+++ b/solution.py
@@ -548,7 +548,7 @@
     wides, refs = refs[:spans], refs[spans:]
     narrows, refs = refs[:2], refs[2:]
     grad_o, near_o, far_o, act_o, hidden_o, refs = *refs[:5], refs[5:]
-    parts_o, refs = refs[: 2 + spans], refs[2 + spans :]
+    (rows_o, cots_o, wide_away, narrow_away, wide_recv, narrow_recv), refs = refs[:6], refs[6:]
     (rows, cot, wide, narrow, act, hidden, near, down_near, down_far, to_side, from_side, to_inner, from_inner,
      sends, recvs, loads, stores) = refs
     units = narrow.shape[0]
@@ -671,19 +671,65 @@
         for k in range(chunks):
             pl.when(i == k)(functools.partial(behind, k))
 
-    pairs = [(act, act_o), (hidden, hidden_o), (down_near, near_o), (down_far, far_o)]
-    for k, source in enumerate((rows, cot)):
-        for j in range(spans):
-            target = parts_o[k * (1 + spans // 2) + (j // 2 if j % 2 == 0 else spans // 2)]
-            if j % 2:
-                target = target.at[:, pl.ds(j // 2 * size, size)]
-            pairs.append((source.at[:, pl.ds(j * size, size)], target))
     out = []
-    for k, (source, target) in enumerate(pairs):
-        out.append(pltpu.make_async_copy(source, target, stores.at[k]))
+
+    def store(source, target):
+        out.append(pltpu.make_async_copy(source, target, stores.at[len(out)]))
         out[-1].start()
-    for k in range(last, 1, -1):
+        return out[-1]
+
+    own_columns, away_columns = pl.ds(0, size), pl.ds(2 * size, size)
+    for source, target in (
+        (act, act_o), (hidden, hidden_o), (down_near, near_o), (down_far, far_o), (rows.at[:, own_columns], rows_o),
+        (cot.at[:, own_columns], cots_o),
+    ):
+        store(source, target)
+    for copy in beside:
+        links.sent(copy)
+
+    def gradient(left, right, start, count, j):
+        return lax.dot_general(
+            left[:, pl.ds(start, count)], right[:, j * size : (j + 1) * size], (((0,), (0,)), ((), ())), preferred_element_type=F32
+        )
+
+    def by_tiles(total, body):
+        whole = total // 384
+
+        @pl.loop(0, whole)
+        def _(k):
+            body(pl.multiple_of(k * 384, 128), 384)
+
+        if total % 384:
+            body(whole * 384, total % 384)
+
+    def give_core(left, right, held, landed):
+        def tile(start, count):
+            for k, j in enumerate(range(1, spans, 2)):
+                held[pl.ds(start, count), k * size : (k + 1) * size] = gradient(left, right, start, count, j).astype(BF16)
+
+        by_tiles(left.shape[1], tile)
+        return links.send(held.at[:, pl.ds(0, 2 * size)], landed, core)
+
+    def give_top(left, right, held, landed, came, target):
+        came.wait_recv()
+        store(landed.at[:, pl.ds(size, size)], held.at[:, away_columns]).wait()
+        out.pop()
+
+        def tile(start, count):
+            here = pl.ds(start, count)
+            total = gradient(left, right, start, count, 2) + held[here, 2 * size : 3 * size].astype(F32)
+            held[here, 3 * size : 4 * size] = total.astype(BF16)
+
+        by_tiles(left.shape[1], tile)
+        store(held.at[:, pl.ds(3 * size, size)], target)
+
+    crossing = give_core(act, rows, wide, wide_recv)
+    give_on(last)
+    crossing_narrow = give_core(hidden, cot, narrow, narrow_recv)
+    for k in range(last - 1, 1, -1):
         give_on(k)
+    give_top(act, rows, wide, wide_recv, crossing, wide_away)
+    give_top(hidden, cot, narrow, narrow_recv, crossing_narrow, narrow_away)
     back_side[0].wait_recv()
     for k in range(chunks - 1):
         back_inner[k].wait_recv()
@@ -704,11 +750,14 @@
     chunks = len(masks)
     total = 2 * chunks * own
     anywhere = pl.BlockSpec(memory_space=pl.ANY)
-    copies = 4 * chunks + sizes[0]
+    copies = 4 * chunks + sizes[0] + 2
     blocks = (chunks, own, width)
     spans = sizes[0]
-    features = [(total, width // spans)] * (spans // 2) + [(total, width // 2)]
-    shapes = [blocks, blocks, (total, 2 * units), (total, units), *features, *features]
+    size = width // spans
+    shapes = [
+        blocks, blocks, (total, 2 * units), (total, units), (total, size), (total, size), (2 * units, size), (units, size),
+        (2 * units, 2 * size), (units, 2 * size),
+    ]
     held = [
         (total, width), (total, width), (2 * units, width), (units, width), (total, 2 * units), (total, units), blocks, blocks,
         blocks, blocks, blocks, (chunks - 1, own, width), (chunks - 1, own, width),
@@ -719,7 +768,7 @@
         out_specs=[pl.BlockSpec(memory_space=pltpu.VMEM)] + [anywhere] * len(shapes),
         out_shape=[jax.ShapeDtypeStruct((own, width), F32)] + [jax.ShapeDtypeStruct(s, BF16) for s in shapes],
         scratch_shapes=[pltpu.VMEM(s, BF16) for s in held]
-        + [pltpu.SemaphoreType.DMA((k,)) for k in (copies, copies, 3 + 2 * chunks + len(wides), 4 + 2 * spans)],
+        + [pltpu.SemaphoreType.DMA((k,)) for k in (copies, copies, 3 + 2 * chunks + len(wides), 8)],
         compiler_params=pltpu.CompilerParams(collective_id=2, has_side_effects=True, vmem_limit_bytes=VMEM_LIMIT),
     )(own_rows, cots, *wides, *narrows)
 
@@ -780,7 +829,9 @@
     inner = [2 * k for k in range(1, seqs // 2)]
     n = len(inner) + 1
     core, top = seqs, count // 2
-    (normal, xb, y_pre, conv, recur, inject, decay, states, flow, mixed, resid, normal_two, params, chan), refs = refs[:14], refs[14:]
+    (normal, xb, y_pre, conv, recur, inject, decay, states, flow, mixed, resid, normal_two, params, chan, turned, mixed_turned), refs = (
+        refs[:16], refs[16:]
+    )
     (proj_x, proj_y, out_half, gates), refs = refs[:4], refs[4:]
     wides, beside_narrow, cots, refs = refs[: spans - 1], refs[spans - 1], refs[spans], refs[spans + 1 :]
     (lead, held_x, held_y, held_o, held_g, every, prod, enter, line, blocks, inflow, to_side, from_side, low,
@@ -1049,7 +1100,9 @@
             total = hold[here].reshape(steps, SUBS, head_w) + cols(prod)[here].reshape(steps, SUBS, head_w) * entered[None]
             total = total.reshape(block, head_w)
             hold[here] = total
-            cols(mixed)[here] = (total * gelu_parts(gain_y[here])[0]).astype(BF16)
+            low_part = total * gelu_parts(gain_y[here])[0]
+            cols(mixed)[here] = low_part.astype(BF16)
+            tall(mixed_turned)[:, here] = low_part.T.astype(BF16)
 
     by_head(heads, head_w, mix)
 
@@ -1070,6 +1123,12 @@
     partial = links.send(to_side, from_side, 1)
     for k in range(1, n - 2):
         onward(k)
+
+    @pl.loop(0, width // head_w)
+    def _(k):
+        columns = pl.ds(pl.multiple_of(k * head_w, 128), head_w)
+        turned[columns] = normal[:rows, columns].astype(F32).T.astype(BF16)
+
     partial.wait_recv()
     size = width // spans
 
@@ -1114,6 +1173,7 @@
     near = [
         low(lead, width), low(lead, half), *[high(rows, half)] * 6, high(4 * SUBS, half), low(rows, half), high(own, width),
         low(own, width), high(params.shape[0], width), high(SUBS, half),
+        low(width, rows), low(half, rows),
     ]
     far = [
         low(width, half), low(width, half), low(half, width), low(half, gate_weight.shape[1]), *[low(*wide.shape)] * (spans - 1),
@@ -1135,8 +1195,8 @@
         ],
         compiler_params=pltpu.CompilerParams(collective_id=0, has_side_effects=True, vmem_limit_bytes=VMEM_LIMIT),
     )(x_own, halo, params, rec_proj, out_proj, gate_weight, cot, wide, narrow)
-    wides, narrows, cots = outs[18 : 17 + spans], outs[17 + spans], outs[18 + spans]
-    return outs[:14], outs[14:18], [wide, *wides], [narrow, narrows], cots
+    wides, narrows, cots = outs[20 : 19 + spans], outs[19 + spans], outs[20 + spans]
+    return outs[:16], outs[16:20], [wide, *wides], [narrow, narrows], cots
 
 
 def return_kernel(
@@ -1415,9 +1475,8 @@
             (spans, seqs), steps, quarters, heads, head_w, mine, halo, packed, rec_proj, out_proj, gate_weight, grads_own,
             wide_own, narrow_own,
         )
-        normal_one, x_branch, y_pre, conv, recur, inject, decay, states, flow, mixed, resid, normal_two, params, chan = nearby
+        normal_one, x_branch, y_pre, conv, recur, inject, decay, states, flow, mixed, resid, normal_two, params, chan, turned, mixed_turned = nearby
         gain_one, gain_two = params[SUBS], params[SUBS + 1]
-        normal_one = normal_one[:rows]
     else:
         proj_x = columns_half(rec_proj[:, :width])
         proj_y = columns_half(rec_proj[:, width:])
@@ -1466,10 +1525,11 @@
         return [*blocks[::2], jnp.concatenate(blocks[1::2], axis=1)]
 
     if direct:
-        normal_two_grad, near, far, all_act, all_hidden, *features = feed_forward(
+        normal_two_grad, near, far, all_act, all_hidden, *features, wide_away, narrow_away, wide_recv, narrow_recv = feed_forward(
             (spans, seqs), chunk_masks, normal_two, cots, wides, narrows
         )
-        all_normal, all_grads = features[: 1 + spans // 2], features[1 + spans // 2 :]
+        all_normal, all_grads = [features[0]], [features[1]]
+        wide_away, narrow_away, wide_recv, narrow_recv = wide_away[None], narrow_away[None], wide_recv[:, :size], narrow_recv[:, :size]
     else:
         wide, narrow = jnp.concatenate(wides, axis=1), jnp.concatenate(narrows, axis=1)
         all_normal = jnp.concatenate(token_gather(normal_two), axis=0)
@@ -1490,12 +1550,19 @@
         normal_two_grad = token_scatter(*sided(nn(all_act, wide, BF16)))
         near, far = sided(nn(all_hidden, narrow, BF16))
     def core_sum(left, right):
-        recv = swap(tn(left, right[-1], BF16), core).astype(F32)
-        total = [tn(left, v) + recv[:, k * size : (k + 1) * size] for k, v in enumerate(right[:-1])]
-        return total[0], jnp.stack([v.astype(BF16) for v in total[1:]])
-
-    wide_kept, wide_away = core_sum(all_act, all_normal)
-    narrow_kept, narrow_away = core_sum(all_hidden, all_grads)
+        recv = swap(tn(left, right[-1], BF16), core)
+        away = [
+            (tn(left, v) + recv[:, (k + 1) * size : (k + 2) * size].astype(F32)).astype(BF16) for k, v in enumerate(right[1:-1])
+        ]
+        return recv[:, :size], jnp.stack(away)
+
+    def own_sum(left, right, recv, came):
+        left, came = lax.optimization_barrier((left, came))
+        return tn(left, right[0]) + recv.astype(F32) + jnp.sum(came.astype(F32), axis=0)
+
+    if not direct:
+        wide_recv, wide_away = core_sum(all_act, all_normal)
+        narrow_recv, narrow_away = core_sum(all_hidden, all_grads)
     resid_part, gain_two_grad = norm_back(resid, gain_two, normal_two_grad)
     resid_grad = c + resid_part
     branch_low = resid_grad.astype(BF16)
@@ -1536,9 +1603,9 @@
         ).reshape(edge * SUBS, half)
         x_grad = jnp.concatenate([dx[: rows - edge * SUBS], dx[rows - edge * SUBS :] + spill], axis=0).astype(BF16)
     output = from_rows(output)
-    wide_owned = wide_kept + jnp.sum(wide_came.astype(F32), axis=0)
+    wide_owned = own_sum(all_act, all_normal, wide_recv, wide_came)
     wide_owned = wide_owned.reshape(2, units, size).transpose(2, 0, 1)
-    narrow_owned = (narrow_kept + jnp.sum(narrow_came.astype(F32), axis=0)).T
+    narrow_owned = own_sum(all_hidden, all_grads, narrow_recv, narrow_came).T
     normal_one_part = nt(y_grad, proj_y) + nt(x_grad, proj_x)
 
     def blocks_of(v, masks, wrap):
@@ -1582,7 +1649,7 @@
     if direct:
         part = normal_one_part.reshape(2, own, width)
         proj_owned, out_owned, gate_owned, input_grad, sums = scatter_grads(
-            (spans, seqs), share, normal_one.T, mixed.T, x_grad, y_grad, branch_low, gate_grad, small_grad, gain_two_grad[None],
+            (spans, seqs), share, turned, mixed_turned, x_grad, y_grad, branch_low, gate_grad, small_grad, gain_two_grad[None],
             mine, gain_one[None], resid_grad, lax.dynamic_index_in_dim(part, side, 0, keepdims=False),
             lax.dynamic_index_in_dim(part, 1 - side, 0, keepdims=False).astype(BF16),
         )

time: 729 us -> 697 us (0.956)
  matrix products: 41.5 us -> 21.9 us
  other arithmetic: 17.4 us -> 7.11 us
  local copies, waits for them, and re-layouts: 28.4 us -> 21.1 us
    dot_general x8 -> x4, matrix products: 41.5 us -> 21.9 us  [dot(): lax.dot_general(a, b, ((dims[0], dims[1]), ((), ())), preferred_element_t...]
  transfers between devices with their start and end apart: 4 -> 2, of which waited for: 0 -> 0; matrix products, arithmetic and copies ran while one was open for 5% -> 1% of each run, Pallas kernels for 0% -> 0%
where the time goes in v6:
time: 697 us; the launch traced here: 688 us
  Pallas kernels  635 us (91%)
  matrix products  21.9 us (3%)
  local copies, waits for them, and re-layouts  21.1 us (3%)
  other arithmetic  7.11 us (1%)
    pallas_call x1, Pallas kernels, front(): pl.pallas_call(functools.partial(front_kernel, sizes, steps, quarters, he...  218 us
    pallas_call x1, Pallas kernels, scatter_grads(): pl.pallas_call(functools.partial(scatter_kernel, sizes, share), in_specs=...  167 us
    pallas_call x1, Pallas kernels, feed_forward(): pl.pallas_call(functools.partial(feed_kernel, sizes, masks, own), in_spec...  147 us
    pallas_call x1, Pallas kernels, returned(): pl.pallas_call(functools.partial(return_kernel, sizes, steps, quarters, h...  102 us
    dot_general x4, matrix products, dot(): lax.dot_general(a, b, ((dims[0], dims[1]), ((), ())), preferred_element_t...  21.9 us
  transfers between devices with their start and end apart: 2, of which 0 were waited for; matrix products, arithmetic and copies ran while one was open for 1% of the time, Pallas kernels for 0%

profile of v6, /device:TPU:8, one launch (start us, length us, event | category | flops | bytes accessed | tf_op | source)
XLA Modules:
  0.0 688.0 jit_solution(1512765213724272860)
XLA Ops:
  0.6 0.9 slice.74
  1.6 0.7 collective-permute-start.1
  2.2 1.3 collective-permute-start
  3.6 1.4 stack.20
  5.0 1.6 copy.35
  6.9 0.9 pad_maximum_fusion.cot
  7.8 0.6 select_maximum_fusion.params_in
  8.9 1.0 reshape.123.x_own
  10.6 0.7 concatenate.11.halo
  11.3 218.0 %shard_map.228 = (bf16[288,2560]{1,0:T(8,128)(2,1)}, bf16[288,1280]{1,0:T(8,128)(2,1)}, f32[256,1280]{1,0:T(8,128)}, f32[256,1280]{1,0:T(8,128)}, f32[256,1280]{...) custom-call(bf16[128,2560]{1,0:T(8,128)(2,1)} %reshape.123.x_own, ...), custom_call_target="tpu_custom_call" | custom-call | tf_op jit(solution)/shard_map/pallas_call | solution.py:1184
  229.4 1.5 multiply_reduce_fusion.2
  230.9 1.6 fusion.4
  232.5 147.3 %shard_map.229 = (f32[128,2560]{1,0:T(8,128)}, bf16[4,128,2560]{2,1,0:T(8,128)(2,1)}, bf16[4,128,2560]{2,1,0:T(8,128)(2,1)}, bf16[1024,1920]{1,0:T(8,128)(2,1)},...) custom-call(bf16[128,2560]{1,0:T(8,128)(2,1)} %get-tuple-element.77., ...), custom_call_target="tpu_custom_call" | custom-call | tf_op jit(solution)/shard_map/pallas_call | solution.py:765
  379.8 1.8 multiply_reduce_fusion
  381.6 0.6 broadcast_in_dim.15.gain
  382.2 1.7 fusion.3
  383.9 102.4 %shard_map.230 = (bf16[256,2560]{1,0:T(8,128)(2,1)}, bf16[256,1280]{1,0:T(8,128)(2,1)}, bf16[256,1280]{1,0:T(8,128)(2,1)}, f32[1280,512]{1,0:T(8,128)}, f32[8,12...) custom-call(bf16[128,2560]{1,0:T(8,128)(2,1)} %get-tuple-element.129.branch, ...), custom_call_target="tpu_custom_call" | custom-call | tf_op jit(solution)/shard_map/pallas_call | solution.py:1343
  486.3 5.0 fusion.5
  491.4 4.8 convolution_add_fusion
  496.2 0.9 fusion.1.part_other
  497.1 1.1 dynamic-slice_bitcast_fusion.part_own
  498.2 167.1 %shard_map.231 = (f32[80,5120]{1,0:T(8,128)}, f32[80,2560]{1,0:T(8,128)}, f32[80,512]{1,0:T(8,128)}, f32[128,2560]{1,0:T(8,128)}, f32[8,3840]{1,0:T(8,128)}) custom-call(bf16[2560,256]{1,0:T(8,128)(2,1)} %get-tuple-element.101.turned, bf16[1280,256]{1,0:T(8,128)(2,1)} %get-tuple-element.102.mixed, bf16[256,1280]{1,0:T(8,128)(2,1)} %get-tuple-element.103.grad_x, ...), custom_call_target="tpu_custom_call" | custom-call | tf_op jit(solution)/shard_map/pallas_call | solution.py:523
  665.3 0.9 slice.80
  666.2 0.8 slice.82
  668.1 0.6 slice.83
  668.9 1.0 copy.29
  670.5 1.8 copy.30
  672.9 8.9 %convert_add_fusion = f32[1920,640]{1,0:T(8,128)} fusion(bf16[1024,1920]{1,0:T(8,128)(2,1)} %get-tuple-element.117, bf16[1024,640]{1,0:T(8,128)(2,1)} %get-tuple-element.118, bf16[1,1920,640]{2,1,0:T(8,128)(2,1)S(1)} %copy-done.11, bf16[1920,1280]{1,0:T(8,128)(2,1)} %get-tuple-element.119), kind=kOutput, calls=%fused_computation | convolution fusion | flops 2521497600 | bytes 15073280 | tf_op jit(solution)/shard_map/dot_general | solution.py:24
  681.9 3.2 fusion
  685.1 1.2 copy.39
  686.2 0.7 copy.40
  686.9 0.9 copy.41
  (53 shorter events, 4.1 us)
Async XLA Ops:
  1.6 8.3 %collective-permute-start.1 = (bf16[2,3,2560]{2,1,0:T(4,128)(2,1)S(1)}, bf16[2,3,2560]{2,1,0:T(4,128)(2,1)S(1)}, u32[]{:S(2)}, u32[]{:S(2)}) collective-permute-start(bf16[2,3,2560]{2,1,0:T(4,128)(2,1)S(1)} %slice.74), channel_id=1, source_target_pairs={{1,3},{3,5},{5,7},{7,9},{9,11},{11,13},{13,15},{15,17},{17,19},{19... | collective-permute-start | bytes 92168 | tf_op jit(solution)/shard_map/ppermute | solution.py:1466
  2.2 7.6 %collective-permute-start = (bf16[2,3,2560]{2,1,0:T(4,128)(2,1)S(1)}, bf16[2,3,2560]{2,1,0:T(4,128)(2,1)S(1)}, u32[]{:S(2)}, u32[]{:S(2)}) collective-permute-start(bf16[2,3,2560]{2,1,0:T(4,128)(2,1)S(1)} %slice.74), channel_id=1, source_target_pairs={{1,2},{3,4},{5,6},{7,8},{9,10},{11,12},{13,14},{15,16},{17,18},{19... | collective-permute-start | bytes 92168 | tf_op jit(solution)/shard_map/ppermute | solution.py:1466
  6.8 1.6 copy-start.6
  232.5 147.3 %copy-start = (f32[128,2560]{1,0:T(8,128)S(1)}, f32[128,2560]{1,0:T(8,128)}, u32[]{:S(2)}) copy-start(f32[128,2560]{1,0:T(8,128)} %get-tuple-element.76.resid) | copy-start | bytes 3932164
  379.8 2.5 copy-start.1
  486.3 5.0 copy-start.2
  498.2 168.8 %copy-start.9 = (bf16[80]{0:T(256)(128)(2,1)S(1)}, bf16[80]{0:T(256)(128)(2,1)}, u32[]{:S(2)}) copy-start(bf16[80]{0:T(256)(128)(2,1)} %param.22) | copy-start | bytes 484
  498.2 170.5 %copy-start.7 = (bf16[128,2560]{1,0:T(8,128)(2,1)S(1)}, bf16[128,2560]{1,0:T(8,128)(2,1)}, u32[]{:S(2)}) copy-start(bf16[128,2560]{1,0:T(8,128)(2,1)} %get-tuple-element.100) | copy-start | bytes 1966084
  668.7 1.4 copy-start.4
  670.5 2.4 copy-start.11
  672.9 8.9 %copy-start.10 = (bf16[960,1280]{1,0:T(8,128)(2,1)S(1)}, bf16[960,1280]{1,0:T(8,128)(2,1)}, u32[]{:S(2)}) copy-start(bf16[960,1280]{1,0:T(8,128)(2,1)} %get-tuple-element.125) | copy-start | bytes 7372804
  672.9 9.0 %copy-start.12 = (bf16[1024,960]{1,0:T(8,128)(2,1)S(1)}, bf16[1024,960]{1,0:T(8,128)(2,1)}, u32[]{:S(2)}) copy-start(bf16[1024,960]{1,0:T(8,128)(2,1)} %get-tuple-element.123) | copy-start | bytes 5898244
  672.9 9.0 %copy-start.13 = (bf16[1024,640]{1,0:T(8,128)(2,1)S(1)}, bf16[1024,640]{1,0:T(8,128)(2,1)}, u32[]{:S(2)}) copy-start(bf16[1024,640]{1,0:T(8,128)(2,1)} %get-tuple-element.124) | copy-start | bytes 3932164
  672.9 8.9 %copy-start.14 = (bf16[1,960,640]{2,1,0:T(8,128)(2,1)S(1)}, bf16[1,960,640]{2,1,0:T(8,128)(2,1)}, u32[]{:S(2)}) copy-start(bf16[1,960,640]{2,1,0:T(8,128)(2,1)} %get-tuple-element.126) | copy-start | bytes 3686404
  681.9 3.2 copy-start.3
  685.1 1.2 copy-start.8
  685.1 1.8 copy-start.5

commit v7 on v6

--- a/solution.py
+++ b/solution.py
@@ -1201,7 +1201,7 @@
 
 def return_kernel(
     sizes, steps, quarters, heads, inner, branch, out_w, y_pre, states, decay, flow, conv, recur, inject, xb, chan, gate,
-    resid, near, far, wide, narrow, branch_o, y_grad, x_grad, gate_o, small, output, wides, narrows, dx, spill, came_back, grad, local, after, enter, carry, line, blocks, inflow, dmix, from_side, to_inner, from_inner, sends, recvs,
+    resid, near, far, wide, narrow, proj_y, branch_o, y_grad, x_grad, gate_o, small, output, part, wides, narrows, held_y, loads, dx, spill, came_back, grad, local, after, enter, carry, line, blocks, inflow, dmix, from_side, to_inner, from_inner, sends, recvs,
 ):
     spans, seqs = sizes
     tops = [2 * seqs * k for k in range(1, spans // 2)]
@@ -1220,6 +1220,8 @@
     tall = wide.shape[1] // 2
     across = [links.send(wide.at[k, pl.ds(0, tall)], wides.at[k, pl.ds(0, tall)], m) for k, m in enumerate(tops)]
     branch_o[place] = branch[...]
+    load = pltpu.make_async_copy(proj_y, held_y, loads.at[0])
+    load.start()
     whole.wait_recv()
     sums = [*range(1, n), 0]
     over_side = {}
@@ -1285,6 +1287,17 @@
     links.open.append((handed, me >= 2))
     rows = 2 * own
     x_grad[: rows - 2 * edge] = dx[: rows - 2 * edge].astype(BF16)
+    load.wait()
+    step = 512
+
+    @pl.loop(0, width // step)
+    def _(k):
+        start = pl.multiple_of(k * step, 128)
+        weights = held_y[pl.ds(start, step)]
+        part[:, pl.ds(start, step)] = lax.dot_general(
+            y_grad[...], weights, (((1,), (1,)), ((), ())), preferred_element_type=F32
+        )
+
     for i in range(2, n):
         inner_sum(i)
         if i + 1 < n:
@@ -1320,7 +1333,7 @@
 
 
 def returned(sizes, steps, quarters, heads, inner, branch, out_w, y_pre, states, decay, flow, conv, recur, inject, xb, chan, gate,
-             resid, near, far, wide, narrow):
+             resid, near, far, wide, narrow, proj_y):
     spans, _ = sizes
     own, width = branch.shape
     rows, half = y_pre.shape
@@ -1335,24 +1348,25 @@
 
     shapes = [
         low(rows, width), low(rows, half), low(rows, half), high(*gate.shape), high(SUBS, half), low(own, width),
-        low(*wide.shape), low(*narrow.shape),
+        high(rows, width), low(*wide.shape), low(*narrow.shape),
     ]
     end = (SUBS, half)
     copies = 3 * (spans // 2) + 2 * n + 2 * n + spans + 2
     tail = ((CONV - 1) * SUBS, half)
     return pl.pallas_call(
         functools.partial(return_kernel, sizes, steps, quarters, heads, inner),
-        in_specs=[inside] * 15 + [anywhere] * 2,
-        out_specs=[inside] * 6 + [anywhere] * 2,
+        in_specs=[inside] * 15 + [anywhere] * 3,
+        out_specs=[inside] * 7 + [anywhere] * 2,
         out_shape=shapes,
         scratch_shapes=[
+            pltpu.VMEM(proj_y.shape, BF16), pltpu.SemaphoreType.DMA((1,)),
             pltpu.VMEM((rows, half), F32), pltpu.VMEM(tail, F32), pltpu.VMEM(tail, F32), *[pltpu.VMEM((rows, half), F32)] * 3, pltpu.VMEM((4 * SUBS, half), F32), pltpu.VMEM(end, F32),
             pltpu.VMEM((n, *end), F32), pltpu.VMEM((spans, *end), F32), pltpu.VMEM(end, F32), pltpu.VMEM(end, F32),
             pltpu.VMEM((n, own, width), BF16), pltpu.VMEM((n - 1, own, width), BF16), pltpu.VMEM((n - 1, own, width), BF16),
             pltpu.SemaphoreType.DMA((copies,)), pltpu.SemaphoreType.DMA((copies,)),
         ],
         compiler_params=pltpu.CompilerParams(collective_id=4, has_side_effects=True, vmem_limit_bytes=VMEM_LIMIT),
-    )(branch, out_w, y_pre, states, decay, flow, conv, recur, inject, xb, chan, gate, resid, near, far, wide, narrow)
+    )(branch, out_w, y_pre, states, decay, flow, conv, recur, inject, xb, chan, gate, resid, near, far, wide, narrow, proj_y)
 
 
 def on_device(
@@ -1567,9 +1581,9 @@
     resid_grad = c + resid_part
     branch_low = resid_grad.astype(BF16)
     if direct:
-        branch_low, y_grad, x_grad, gate_grad, small_grad, output, wide_came, narrow_came = returned(
+        branch_low, y_grad, x_grad, gate_grad, small_grad, output, normal_one_part, wide_came, narrow_came = returned(
             (spans, seqs), steps, quarters, heads, chunk_masks[1:], branch_low, out_half, y_pre, states, decay, flow, conv, recur, inject,
-            x_branch, chan, gates, resid, near, far, wide_away, narrow_away,
+            x_branch, chan, gates, resid, near, far, wide_away, narrow_away, proj_y,
         )
     else:
         output = (resid + token_scatter(near, far)).astype(BF16)
@@ -1606,7 +1620,9 @@
     wide_owned = own_sum(all_act, all_normal, wide_recv, wide_came)
     wide_owned = wide_owned.reshape(2, units, size).transpose(2, 0, 1)
     narrow_owned = own_sum(all_hidden, all_grads, narrow_recv, narrow_came).T
-    normal_one_part = nt(y_grad, proj_y) + nt(x_grad, proj_x)
+    if not direct:
+        normal_one_part = nt(y_grad, proj_y)
+    normal_one_part = normal_one_part + nt(x_grad, proj_x)
 
     def blocks_of(v, masks, wrap):
         size = 2 * share

time: 697 us -> 689 us (0.989)
    dot_general x4 -> x3, matrix products: 21.9 us -> 17.8 us  [dot(): lax.dot_general(a, b, ((dims[0], dims[1]), ((), ())), preferred_element_t...]
where the time goes in v7:
time: 689 us; the launch traced here: 685 us
  Pallas kernels  636 us (92%)
  local copies, waits for them, and re-layouts  21.1 us (3%)
  matrix products  17.8 us (3%)
  other arithmetic  7.11 us (1%)
    pallas_call x1, Pallas kernels, front(): pl.pallas_call(functools.partial(front_kernel, sizes, steps, quarters, he...  218 us
    pallas_call x1, Pallas kernels, scatter_grads(): pl.pallas_call(functools.partial(scatter_kernel, sizes, share), in_specs=...  167 us
    pallas_call x1, Pallas kernels, feed_forward(): pl.pallas_call(functools.partial(feed_kernel, sizes, masks, own), in_spec...  147 us
    pallas_call x1, Pallas kernels, returned(): pl.pallas_call(functools.partial(return_kernel, sizes, steps, quarters, h...  103 us
    dot_general x3, matrix products, dot(): lax.dot_general(a, b, ((dims[0], dims[1]), ((), ())), preferred_element_t...  17.8 us
  transfers between devices with their start and end apart: 2, of which 0 were waited for; matrix products, arithmetic and copies ran while one was open for 1% of the time, Pallas kernels for 0%

profile of v7, /device:TPU:8, one launch (start us, length us, event | category | flops | bytes accessed | tf_op | source)
XLA Modules:
  0.0 684.8 jit_solution(3766658927182094550)
XLA Ops:
  0.6 0.9 slice.74
  1.6 0.7 collective-permute-start.1
  2.2 1.3 collective-permute-start
  3.6 1.4 stack.20
  5.0 1.6 copy.35
  6.9 0.9 pad_maximum_fusion.cot
  7.8 0.6 select_maximum_fusion.params_in
  8.9 1.0 reshape.123.x_own
  10.6 0.7 concatenate.11.halo
  11.3 218.1 %shard_map.228 = (bf16[288,2560]{1,0:T(8,128)(2,1)}, bf16[288,1280]{1,0:T(8,128)(2,1)}, f32[256,1280]{1,0:T(8,128)}, f32[256,1280]{1,0:T(8,128)}, f32[256,1280]{...) custom-call(bf16[128,2560]{1,0:T(8,128)(2,1)} %reshape.123.x_own, ...), custom_call_target="tpu_custom_call" | custom-call | tf_op jit(solution)/shard_map/pallas_call | solution.py:1184
  229.4 1.5 multiply_reduce_fusion.2
  230.9 1.6 fusion.4
  232.5 147.3 %shard_map.229 = (f32[128,2560]{1,0:T(8,128)}, bf16[4,128,2560]{2,1,0:T(8,128)(2,1)}, bf16[4,128,2560]{2,1,0:T(8,128)(2,1)}, bf16[1024,1920]{1,0:T(8,128)(2,1)},...) custom-call(bf16[128,2560]{1,0:T(8,128)(2,1)} %get-tuple-element.78., ...), custom_call_target="tpu_custom_call" | custom-call | tf_op jit(solution)/shard_map/pallas_call | solution.py:765
  379.8 1.8 multiply_reduce_fusion
  381.7 0.6 broadcast_in_dim.15.gain
  382.3 1.7 fusion.3
  384.0 103.2 %shard_map.230 = (bf16[256,2560]{1,0:T(8,128)(2,1)}, bf16[256,1280]{1,0:T(8,128)(2,1)}, bf16[256,1280]{1,0:T(8,128)(2,1)}, f32[1280,512]{1,0:T(8,128)}, f32[8,12...) custom-call(bf16[128,2560]{1,0:T(8,128)(2,1)} %get-tuple-element.131, ...), custom_call_target="tpu_custom_call" | custom-call | tf_op jit(solution)/shard_map/pallas_call | solution.py:1356
  487.2 5.7 convolution_add_fusion
  492.9 0.9 fusion.1.part_other
  493.8 1.1 dynamic-slice_bitcast_fusion.part_own
  495.0 167.1 %shard_map.231 = (f32[80,5120]{1,0:T(8,128)}, f32[80,2560]{1,0:T(8,128)}, f32[80,512]{1,0:T(8,128)}, f32[128,2560]{1,0:T(8,128)}, f32[8,3840]{1,0:T(8,128)}) custom-call(bf16[2560,256]{1,0:T(8,128)(2,1)} %get-tuple-element.103.turned, bf16[1280,256]{1,0:T(8,128)(2,1)} %get-tuple-element.104.mixed, bf16[256,1280]{1,0:T(8,128)(2,1)} %get-tuple-element.105.grad_x, ...), custom_call_target="tpu_custom_call" | custom-call | tf_op jit(solution)/shard_map/pallas_call | solution.py:523
  662.1 0.9 slice.80
  663.0 0.8 slice.82
  664.4 0.6 slice.85
  664.9 0.6 slice.83
  665.7 1.0 copy.29
  667.3 1.8 copy.30
  669.8 8.9 %convert_add_fusion = f32[1920,640]{1,0:T(8,128)} fusion(bf16[1024,1920]{1,0:T(8,128)(2,1)} %get-tuple-element.119, bf16[1024,640]{1,0:T(8,128)(2,1)} %get-tuple-element.120, bf16[1,1920,640]{2,1,0:T(8,128)(2,1)S(1)} %copy-done.10, bf16[1920,1280]{1,0:T(8,128)(2,1)} %get-tuple-element.121), kind=kOutput, calls=%fused_computation | convolution fusion | flops 2521497600 | bytes 15073280 | tf_op jit(solution)/shard_map/dot_general | solution.py:24
  678.7 3.2 fusion
  681.9 1.2 copy.39
  683.1 0.7 copy.40
  683.7 0.9 copy.41
  (50 shorter events, 3.5 us)
Async XLA Ops:
  1.6 8.3 %collective-permute-start.1 = (bf16[2,3,2560]{2,1,0:T(4,128)(2,1)S(1)}, bf16[2,3,2560]{2,1,0:T(4,128)(2,1)S(1)}, u32[]{:S(2)}, u32[]{:S(2)}) collective-permute-start(bf16[2,3,2560]{2,1,0:T(4,128)(2,1)S(1)} %slice.74), channel_id=1, source_target_pairs={{1,3},{3,5},{5,7},{7,9},{9,11},{11,13},{13,15},{15,17},{17,19},{19... | collective-permute-start | bytes 92168 | tf_op jit(solution)/shard_map/ppermute | solution.py:1480
  2.2 7.6 %collective-permute-start = (bf16[2,3,2560]{2,1,0:T(4,128)(2,1)S(1)}, bf16[2,3,2560]{2,1,0:T(4,128)(2,1)S(1)}, u32[]{:S(2)}, u32[]{:S(2)}) collective-permute-start(bf16[2,3,2560]{2,1,0:T(4,128)(2,1)S(1)} %slice.74), channel_id=1, source_target_pairs={{1,2},{3,4},{5,6},{7,8},{9,10},{11,12},{13,14},{15,16},{17,18},{19... | collective-permute-start | bytes 92168 | tf_op jit(solution)/shard_map/ppermute | solution.py:1480
  6.8 1.6 copy-start.5
  232.5 147.3 %copy-start = (f32[128,2560]{1,0:T(8,128)S(1)}, f32[128,2560]{1,0:T(8,128)}, u32[]{:S(2)}) copy-start(f32[128,2560]{1,0:T(8,128)} %get-tuple-element.77.resid) | copy-start | bytes 3932164
  379.8 2.5 copy-start.1
  495.0 168.9 %copy-start.8 = (bf16[80]{0:T(256)(128)(2,1)S(1)}, bf16[80]{0:T(256)(128)(2,1)}, u32[]{:S(2)}) copy-start(bf16[80]{0:T(256)(128)(2,1)} %param.22) | copy-start | bytes 484
  495.0 170.6 %copy-start.6 = (bf16[128,2560]{1,0:T(8,128)(2,1)S(1)}, bf16[128,2560]{1,0:T(8,128)(2,1)}, u32[]{:S(2)}) copy-start(bf16[128,2560]{1,0:T(8,128)(2,1)} %get-tuple-element.102) | copy-start | bytes 1966084
  665.5 1.4 copy-start.3
  667.3 2.4 copy-start.10
  669.7 8.9 %copy-start.9 = (bf16[960,1280]{1,0:T(8,128)(2,1)S(1)}, bf16[960,1280]{1,0:T(8,128)(2,1)}, u32[]{:S(2)}) copy-start(bf16[960,1280]{1,0:T(8,128)(2,1)} %get-tuple-element.127) | copy-start | bytes 7372804
  669.7 8.9 %copy-start.11 = (bf16[1024,960]{1,0:T(8,128)(2,1)S(1)}, bf16[1024,960]{1,0:T(8,128)(2,1)}, u32[]{:S(2)}) copy-start(bf16[1024,960]{1,0:T(8,128)(2,1)} %get-tuple-element.125) | copy-start | bytes 5898244
  669.7 9.0 %copy-start.12 = (bf16[1024,640]{1,0:T(8,128)(2,1)S(1)}, bf16[1024,640]{1,0:T(8,128)(2,1)}, u32[]{:S(2)}) copy-start(bf16[1024,640]{1,0:T(8,128)(2,1)} %get-tuple-element.126) | copy-start | bytes 3932164
  669.7 8.9 %copy-start.13 = (bf16[1,960,640]{2,1,0:T(8,128)(2,1)S(1)}, bf16[1,960,640]{2,1,0:T(8,128)(2,1)}, u32[]{:S(2)}) copy-start(bf16[1,960,640]{2,1,0:T(8,128)(2,1)} %get-tuple-element.128) | copy-start | bytes 3686404
  678.7 3.2 copy-start.2
  681.9 1.2 copy-start.7
  681.9 1.8 copy-start.4

commit v8 on v7

--- a/solution.py
+++ b/solution.py
@@ -1201,7 +1201,8 @@
 
 def return_kernel(
     sizes, steps, quarters, heads, inner, branch, out_w, y_pre, states, decay, flow, conv, recur, inject, xb, chan, gate,
-    resid, near, far, wide, narrow, proj_y, branch_o, y_grad, x_grad, gate_o, small, output, part, wides, narrows, held_y, loads, dx, spill, came_back, grad, local, after, enter, carry, line, blocks, inflow, dmix, from_side, to_inner, from_inner, sends, recvs,
+    resid, near, far, wide, narrow, proj_y, proj_x, branch_o, y_grad, x_grad, gate_o, small, output, part_own, part_other, wides, narrows,
+    part, held_y, loads, dx, spill, came_back, grad, local, after, enter, carry, line, blocks, inflow, dmix, from_side, to_inner, from_inner, sends, recvs,
 ):
     spans, seqs = sizes
     tops = [2 * seqs * k for k in range(1, spans // 2)]
@@ -1298,6 +1299,8 @@
             y_grad[...], weights, (((1,), (1,)), ((), ())), preferred_element_type=F32
         )
 
+    load = pltpu.make_async_copy(proj_x, held_y, loads.at[0])
+    load.start()
     for i in range(2, n):
         inner_sum(i)
         if i + 1 < n:
@@ -1327,13 +1330,26 @@
             total = total + from_inner[k, :, columns].astype(F32)
         output[:, there] = total.astype(BF16)
 
+    load.wait()
+
+    @pl.loop(0, width // step)
+    def _(k):
+        start = pl.multiple_of(k * step, 128)
+        columns = pl.ds(start, step)
+        total = part[:, columns] + lax.dot_general(
+            x_grad[...], held_y[columns], (((1,), (1,)), ((), ())), preferred_element_type=F32
+        )
+        lower = side == 0
+        part_own[:, columns] = jnp.where(lower, total[:own], total[own:])
+        part_other[:, columns] = jnp.where(lower, total[own:], total[:own]).astype(BF16)
+
     for copy in across:
         copy.wait_recv()
     links.close()
 
 
 def returned(sizes, steps, quarters, heads, inner, branch, out_w, y_pre, states, decay, flow, conv, recur, inject, xb, chan, gate,
-             resid, near, far, wide, narrow, proj_y):
+             resid, near, far, wide, narrow, proj_y, proj_x):
     spans, _ = sizes
     own, width = branch.shape
     rows, half = y_pre.shape
@@ -1348,25 +1364,25 @@
 
     shapes = [
         low(rows, width), low(rows, half), low(rows, half), high(*gate.shape), high(SUBS, half), low(own, width),
-        high(rows, width), low(*wide.shape), low(*narrow.shape),
+        high(own, width), low(own, width), low(*wide.shape), low(*narrow.shape),
     ]
     end = (SUBS, half)
     copies = 3 * (spans // 2) + 2 * n + 2 * n + spans + 2
     tail = ((CONV - 1) * SUBS, half)
     return pl.pallas_call(
         functools.partial(return_kernel, sizes, steps, quarters, heads, inner),
-        in_specs=[inside] * 15 + [anywhere] * 3,
-        out_specs=[inside] * 7 + [anywhere] * 2,
+        in_specs=[inside] * 15 + [anywhere] * 4,
+        out_specs=[inside] * 8 + [anywhere] * 2,
         out_shape=shapes,
         scratch_shapes=[
-            pltpu.VMEM(proj_y.shape, BF16), pltpu.SemaphoreType.DMA((1,)),
+            pltpu.VMEM((rows, width), F32), pltpu.VMEM(proj_y.shape, BF16), pltpu.SemaphoreType.DMA((1,)),
             pltpu.VMEM((rows, half), F32), pltpu.VMEM(tail, F32), pltpu.VMEM(tail, F32), *[pltpu.VMEM((rows, half), F32)] * 3, pltpu.VMEM((4 * SUBS, half), F32), pltpu.VMEM(end, F32),
             pltpu.VMEM((n, *end), F32), pltpu.VMEM((spans, *end), F32), pltpu.VMEM(end, F32), pltpu.VMEM(end, F32),
             pltpu.VMEM((n, own, width), BF16), pltpu.VMEM((n - 1, own, width), BF16), pltpu.VMEM((n - 1, own, width), BF16),
             pltpu.SemaphoreType.DMA((copies,)), pltpu.SemaphoreType.DMA((copies,)),
         ],
         compiler_params=pltpu.CompilerParams(collective_id=4, has_side_effects=True, vmem_limit_bytes=VMEM_LIMIT),
-    )(branch, out_w, y_pre, states, decay, flow, conv, recur, inject, xb, chan, gate, resid, near, far, wide, narrow, proj_y)
+    )(branch, out_w, y_pre, states, decay, flow, conv, recur, inject, xb, chan, gate, resid, near, far, wide, narrow, proj_y, proj_x)
 
 
 def on_device(
@@ -1581,9 +1597,9 @@
     resid_grad = c + resid_part
     branch_low = resid_grad.astype(BF16)
     if direct:
-        branch_low, y_grad, x_grad, gate_grad, small_grad, output, normal_one_part, wide_came, narrow_came = returned(
+        branch_low, y_grad, x_grad, gate_grad, small_grad, output, part_own, part_other, wide_came, narrow_came = returned(
             (spans, seqs), steps, quarters, heads, chunk_masks[1:], branch_low, out_half, y_pre, states, decay, flow, conv, recur, inject,
-            x_branch, chan, gates, resid, near, far, wide_away, narrow_away, proj_y,
+            x_branch, chan, gates, resid, near, far, wide_away, narrow_away, proj_y, proj_x,
         )
     else:
         output = (resid + token_scatter(near, far)).astype(BF16)
@@ -1621,8 +1637,7 @@
     wide_owned = wide_owned.reshape(2, units, size).transpose(2, 0, 1)
     narrow_owned = own_sum(all_hidden, all_grads, narrow_recv, narrow_came).T
     if not direct:
-        normal_one_part = nt(y_grad, proj_y)
-    normal_one_part = normal_one_part + nt(x_grad, proj_x)
+        normal_one_part = nt(y_grad, proj_y) + nt(x_grad, proj_x)
 
     def blocks_of(v, masks, wrap):
         size = 2 * share
@@ -1663,11 +1678,9 @@
         return [jnp.concatenate(blocks_of(v, [m ^ c for m in masks], wrap), axis=0) for c in (0, core)]
 
     if direct:
-        part = normal_one_part.reshape(2, own, width)
         proj_owned, out_owned, gate_owned, input_grad, sums = scatter_grads(
             (spans, seqs), share, turned, mixed_turned, x_grad, y_grad, branch_low, gate_grad, small_grad, gain_two_grad[None],
-            mine, gain_one[None], resid_grad, lax.dynamic_index_in_dim(part, side, 0, keepdims=False),
-            lax.dynamic_index_in_dim(part, 1 - side, 0, keepdims=False).astype(BF16),
+            mine, gain_one[None], resid_grad, part_own, part_other,
         )
         gains = cut(sums[:2, :width], me, share, 1).T
         small_owned = cut(sums[:, width:], me % (count // 2), share, 1).T

time: 689 us -> 683 us (level)
    dot_general x3 -> x2, matrix products: 17.8 us -> 12.1 us  [dot(): lax.dot_general(a, b, ((dims[0], dims[1]), ((), ())), preferred_element_t...]
where the time goes in v8:
time: 683 us; the launch traced here: 678 us
  Pallas kernels  637 us (93%)
  local copies, waits for them, and re-layouts  19.1 us (3%)
  matrix products  12.1 us (2%)
  other arithmetic  7.11 us (1%)
    pallas_call x1, Pallas kernels, front(): pl.pallas_call(functools.partial(front_kernel, sizes, steps, quarters, he...  218 us
    pallas_call x1, Pallas kernels, scatter_grads(): pl.pallas_call(functools.partial(scatter_kernel, sizes, share), in_specs=...  166 us
    pallas_call x1, Pallas kernels, feed_forward(): pl.pallas_call(functools.partial(feed_kernel, sizes, masks, own), in_spec...  147 us
    pallas_call x1, Pallas kernels, returned(): pl.pallas_call(functools.partial(return_kernel, sizes, steps, quarters, h...  105 us
  transfers between devices with their start and end apart: 2, of which 0 were waited for; matrix products, arithmetic and copies ran while one was open for 1% of the time, Pallas kernels for 0%

profile of v8, /device:TPU:8, one launch (start us, length us, event | category | flops | bytes accessed | tf_op | source)
XLA Modules:
  0.0 677.9 jit_solution(13273118153097028273)
XLA Ops:
  0.6 0.9 slice.74
  1.6 0.7 collective-permute-start.1
  2.2 1.3 collective-permute-start
  3.6 1.4 stack.20
  5.0 1.6 copy.35
  6.9 0.9 pad_maximum_fusion.cot
  7.8 0.6 select_maximum_fusion.params_in
  8.9 1.0 reshape.119.x_own
  9.9 0.6 rev.3
  10.6 0.7 concatenate.11.halo
  11.3 218.1 %shard_map.228 = (bf16[288,2560]{1,0:T(8,128)(2,1)}, bf16[288,1280]{1,0:T(8,128)(2,1)}, f32[256,1280]{1,0:T(8,128)}, f32[256,1280]{1,0:T(8,128)}, f32[256,1280]{...) custom-call(bf16[128,2560]{1,0:T(8,128)(2,1)} %reshape.119.x_own, ...), custom_call_target="tpu_custom_call" | custom-call | tf_op jit(solution)/shard_map/pallas_call | solution.py:1184
  229.4 1.5 multiply_reduce_fusion.2
  230.9 1.6 fusion.3
  232.5 147.3 %shard_map.229 = (f32[128,2560]{1,0:T(8,128)}, bf16[4,128,2560]{2,1,0:T(8,128)(2,1)}, bf16[4,128,2560]{2,1,0:T(8,128)(2,1)}, bf16[1024,1920]{1,0:T(8,128)(2,1)},...) custom-call(bf16[128,2560]{1,0:T(8,128)(2,1)} %get-tuple-element.79., ...), custom_call_target="tpu_custom_call" | custom-call | tf_op jit(solution)/shard_map/pallas_call | solution.py:765
  379.8 1.8 multiply_reduce_fusion
  381.7 0.6 broadcast_in_dim.15.gain
  382.3 1.7 fusion.2
  384.0 105.0 %shard_map.230 = (bf16[256,2560]{1,0:T(8,128)(2,1)}, bf16[256,1280]{1,0:T(8,128)(2,1)}, bf16[256,1280]{1,0:T(8,128)(2,1)}, f32[1280,512]{1,0:T(8,128)}, f32[8,12...) custom-call(bf16[128,2560]{1,0:T(8,128)(2,1)} %get-tuple-element.133, ...), custom_call_target="tpu_custom_call" | custom-call | tf_op jit(solution)/shard_map/pallas_call | solution.py:1372
  489.0 166.2 %shard_map.231 = (f32[80,5120]{1,0:T(8,128)}, f32[80,2560]{1,0:T(8,128)}, f32[80,512]{1,0:T(8,128)}, f32[128,2560]{1,0:T(8,128)}, f32[8,3840]{1,0:T(8,128)}) custom-call(bf16[2560,256]{1,0:T(8,128)(2,1)} %get-tuple-element.105.turned, bf16[1280,256]{1,0:T(8,128)(2,1)} %get-tuple-element.106.mixed, bf16[256,1280]{1,0:T(8,128)(2,1)} %get-tuple-element.107.grad_x, ...), custom_call_target="tpu_custom_call" | custom-call | tf_op jit(solution)/shard_map/pallas_call | solution.py:523
  655.2 0.9 slice.80
  656.1 0.8 slice.82
  656.9 0.5 divide_multiply_fusion
  657.5 0.6 slice.85
  658.0 0.6 slice.83
  658.8 1.0 copy.29
  660.4 1.8 copy.30
  662.3 0.5 slice_bitcast_fusion
  662.8 8.9 %convert_add_fusion = f32[1920,640]{1,0:T(8,128)} fusion(bf16[1024,1920]{1,0:T(8,128)(2,1)} %get-tuple-element.121, bf16[1024,640]{1,0:T(8,128)(2,1)} %get-tuple-element.122, bf16[1,1920,640]{2,1,0:T(8,128)(2,1)S(1)} %copy-done.10, bf16[1920,1280]{1,0:T(8,128)(2,1)} %get-tuple-element.123), kind=kOutput, calls=%fused_computation | convolution fusion | flops 2521497600 | bytes 15073280 | tf_op jit(solution)/shard_map/dot_general | solution.py:24
  671.8 3.2 fusion
  675.0 1.2 copy.39
  676.1 0.7 copy.40
  676.8 0.9 copy.41
  (47 shorter events, 1.9 us)
Async XLA Ops:
  1.6 8.3 %collective-permute-start.1 = (bf16[2,3,2560]{2,1,0:T(4,128)(2,1)S(1)}, bf16[2,3,2560]{2,1,0:T(4,128)(2,1)S(1)}, u32[]{:S(2)}, u32[]{:S(2)}) collective-permute-start(bf16[2,3,2560]{2,1,0:T(4,128)(2,1)S(1)} %slice.74), channel_id=1, source_target_pairs={{1,3},{3,5},{5,7},{7,9},{9,11},{11,13},{13,15},{15,17},{17,19},{19... | collective-permute-start | bytes 92168 | tf_op jit(solution)/shard_map/ppermute | solution.py:1496
  2.2 7.6 %collective-permute-start = (bf16[2,3,2560]{2,1,0:T(4,128)(2,1)S(1)}, bf16[2,3,2560]{2,1,0:T(4,128)(2,1)S(1)}, u32[]{:S(2)}, u32[]{:S(2)}) collective-permute-start(bf16[2,3,2560]{2,1,0:T(4,128)(2,1)S(1)} %slice.74), channel_id=1, source_target_pairs={{1,2},{3,4},{5,6},{7,8},{9,10},{11,12},{13,14},{15,16},{17,18},{19... | collective-permute-start | bytes 92168 | tf_op jit(solution)/shard_map/ppermute | solution.py:1496
  6.8 1.6 copy-start.5
  232.5 147.3 %copy-start = (f32[128,2560]{1,0:T(8,128)S(1)}, f32[128,2560]{1,0:T(8,128)}, u32[]{:S(2)}) copy-start(f32[128,2560]{1,0:T(8,128)} %get-tuple-element.78.resid) | copy-start | bytes 3932164
  379.8 2.5 copy-start.1
  489.0 167.9 %copy-start.8 = (bf16[80]{0:T(256)(128)(2,1)S(1)}, bf16[80]{0:T(256)(128)(2,1)}, u32[]{:S(2)}) copy-start(bf16[80]{0:T(256)(128)(2,1)} %param.22) | copy-start | bytes 484
  489.0 169.6 %copy-start.6 = (bf16[128,2560]{1,0:T(8,128)(2,1)S(1)}, bf16[128,2560]{1,0:T(8,128)(2,1)}, u32[]{:S(2)}) copy-start(bf16[128,2560]{1,0:T(8,128)(2,1)} %get-tuple-element.104) | copy-start | bytes 1966084
  658.6 1.4 copy-start.3
  660.4 2.4 copy-start.10
  662.8 8.9 %copy-start.9 = (bf16[960,1280]{1,0:T(8,128)(2,1)S(1)}, bf16[960,1280]{1,0:T(8,128)(2,1)}, u32[]{:S(2)}) copy-start(bf16[960,1280]{1,0:T(8,128)(2,1)} %get-tuple-element.129) | copy-start | bytes 7372804
  662.8 8.9 %copy-start.11 = (bf16[1024,960]{1,0:T(8,128)(2,1)S(1)}, bf16[1024,960]{1,0:T(8,128)(2,1)}, u32[]{:S(2)}) copy-start(bf16[1024,960]{1,0:T(8,128)(2,1)} %get-tuple-element.127) | copy-start | bytes 5898244
  662.8 9.0 %copy-start.12 = (bf16[1024,640]{1,0:T(8,128)(2,1)S(1)}, bf16[1024,640]{1,0:T(8,128)(2,1)}, u32[]{:S(2)}) copy-start(bf16[1024,640]{1,0:T(8,128)(2,1)} %get-tuple-element.128) | copy-start | bytes 3932164
  662.8 8.9 %copy-start.13 = (bf16[1,960,640]{2,1,0:T(8,128)(2,1)S(1)}, bf16[1,960,640]{2,1,0:T(8,128)(2,1)}, u32[]{:S(2)}) copy-start(bf16[1,960,640]{2,1,0:T(8,128)(2,1)} %get-tuple-element.130) | copy-start | bytes 3686404
  671.8 3.2 copy-start.2
  675.0 1.2 copy-start.7
  675.0 1.8 copy-start.4
